TPU v7x, 32 devices: a whole 2x2x4 slice. The times are simulated.
32 devices in a mesh: lon: 8 (over z, core), lat: 4 (over y, x).
Axes of the slice: x: 2, y: 2, z: 4, core: 2. Of those that a mesh axis runs over, the one named last changes fastest.
Arguments:
- perturbations: float32 [12, 3, 64, 1024], P(None, None, 'lat', 'lon'), as said below
- base_wind: float32 [2, 64, 1024], P(None, 'lat', 'lon'), may hold values from -4 to 4
- base_height: float32 [64, 1024], P('lat', 'lon'), may hold values from 0.5 to 1.5
Outputs:
- fields: float32 [12, 3, 64, 1024], P(None, None, 'lat', 'lon')
- factor: float32 [12, 12], replicated
Inputs may be any that keep to these rules, and one draw needn't show every extreme that they name: `perturbations`: finite real values.
All inputs are finite; a program needn't handle non-finite values.
Results may differ from a plain program's by a relative error of at most 0.00012.
Values sent between devices are 32-bit elements; how exact they have to be, the bound alone decides.
No kernel may reach another device: no remote copies, remote signals or barrier semaphores. Data moves between devices by JAX's collectives and lax.ppermute only.
A program may use at most 64 MiB of HBM per device.

v0:
```python
import math

import jax
import jax.numpy as jnp
from jax import lax
from jax.sharding import PartitionSpec as P

STEPS = 8


advect_rate = 0.1
turn_rate = 0.5
gravity_rate = 0.2
diffuse_rate = 0.12


def with_halo(block, sides, width, periodic):
    for axis, dim in sides:
        count = lax.axis_size(axis)
        forward = [(i, i + 1) for i in range(count - 1)]
        if periodic:
            forward.append((count - 1, 0))
        backward = [(target, source) for source, target in forward]
        low = lax.ppermute(
            lax.slice_in_dim(block, block.shape[dim] - width, None, axis=dim), axis, forward
        )
        high = lax.ppermute(lax.slice_in_dim(block, 0, width, axis=dim), axis, backward)
        block = jnp.concatenate([low, block, high], axis=dim)
    return block


def centre(array):
    return array[..., 1:-1, 1:-1]


def diff_lon(array):
    return 0.5 * (array[..., 1:-1, 2:] - array[..., 1:-1, :-2])


def diff_lat(array):
    return 0.5 * (array[..., 2:, 1:-1] - array[..., :-2, 1:-1])


def laplacian(array):
    return (
        array[..., 2:, 1:-1]
        + array[..., :-2, 1:-1]
        + array[..., 1:-1, 2:]
        + array[..., 1:-1, :-2]
        - 4.0 * centre(array)
    )


def advance(field, base, turning):
    wind_x = field[..., 0, :, :]
    wind_y = field[..., 1, :, :]
    height = field[..., 2, :, :]
    base_x = base[0]
    base_y = base[1]
    base_depth = base[2]
    mean_x = centre(base_x)
    mean_y = centre(base_y)
    inner_x = centre(wind_x)
    inner_y = centre(wind_y)
    new_x = (
        inner_x
        - advect_rate
        * (
            mean_x * diff_lon(wind_x)
            + inner_x * diff_lon(base_x)
            + mean_y * diff_lat(wind_x)
            + inner_y * diff_lat(base_x)
        )
        + turn_rate * turning * inner_y
        - gravity_rate * diff_lon(height)
        + diffuse_rate * laplacian(wind_x)
    )
    new_y = (
        inner_y
        - advect_rate
        * (
            mean_x * diff_lon(wind_y)
            + inner_x * diff_lon(base_y)
            + mean_y * diff_lat(wind_y)
            + inner_y * diff_lat(base_y)
        )
        - turn_rate * turning * inner_x
        - gravity_rate * diff_lat(height)
        + diffuse_rate * laplacian(wind_y)
    )
    new_height = (
        centre(height)
        - advect_rate
        * (
            diff_lon(base_depth * wind_x + height * base_x)
            + diff_lat(base_depth * wind_y + height * base_y)
        )
        + diffuse_rate * laplacian(height)
    )
    return jnp.stack([new_x, new_y, new_height], axis=-3)


def coriolis(start, rows, total):
    glob = (start + jnp.arange(rows, dtype=jnp.int32)).astype(jnp.float32)
    return jnp.sin(math.pi * ((glob + 0.5) / total - 0.5))[:, None]


def inside_grid(start, rows, total):
    glob = start + jnp.arange(rows, dtype=jnp.int32)
    return ((glob >= 0) & (glob < total)).astype(jnp.float32)[:, None]


def extend(block, width):
    wide = with_halo(block, (("lon", 3),), width, True)
    return with_halo(wide, (("lat", 2),), width, False)


def per_device(perturbations, base_wind, base_height):
    rows = perturbations.shape[2]
    cols = perturbations.shape[3]
    total_rows = rows * lax.axis_size("lat")
    total_cols = cols * lax.axis_size("lon")
    row_start = lax.axis_index("lat") * rows
    depth = 4
    stacked = jnp.concatenate([base_wind, base_height[None]], axis=0)[None]
    base_ext = extend(stacked, depth)[0]
    field = perturbations
    for group_index in range(STEPS // depth):
        current = extend(field, depth)
        for inner_index in range(depth):
            margin = depth - 1 - inner_index
            turning = coriolis(row_start - margin, rows + 2 * margin, total_rows)
            base_margin = margin + 1
            current = advance(
                current,
                base_ext[
                    :,
                    depth - base_margin : depth + rows + base_margin,
                    depth - base_margin : depth + cols + base_margin,
                ],
                turning,
            )
            if margin > 0:
                current = current * inside_grid(row_start - margin, rows + 2 * margin, total_rows)
        field = current
    flattened = field.reshape(field.shape[0], -1)
    cell_count = float(3 * total_rows * total_cols)
    local_gram = jnp.dot(flattened, flattened.T, precision=lax.Precision.HIGHEST) / cell_count
    gram = lax.psum(local_gram, ("lon", "lat"))
    upper_factor = jnp.linalg.cholesky(gram).T
    lower_factor = upper_factor.T
    fields = jax.scipy.linalg.solve_triangular(lower_factor, flattened, lower=True)
    return (fields.reshape(perturbations.shape), upper_factor)


def solution(mesh):
    return jax.shard_map(
        per_device,
        mesh=mesh,
        in_specs=(P(None, None, "lat", "lon"), P(None, "lat", "lon"), P("lat", "lon")),
        out_specs=(P(None, None, "lat", "lon"), P()),
        check_vma=False,
    )
```

profile of v0, /device:TPU:0, one launch (start us, length us, event | category | flops | bytes accessed | tf_op | source)
XLA Modules:
  0.0 118.7 jit_solution(2515264463206278063)
XLA Ops:
  0.6 0.7 maximum_bitcast_fusion
  1.9 4.1 %collective-permute-start.5 = (f32[1,3,16,4]{3,2,1,0:T(8,128)S(1)}, f32[1,3,16,4]{3,2,1,0:T(8,128)S(1)}, u32[]{:S(2)}, u32[]{:S(2)}) collective-permute-start(f32[1,3,16,4]{3,2,1,0:T(8,128)S(1)} %get-tuple-element.93), channel_id=1, source_target_pairs={{4,0},{8,4},{12,8},{16,12},{20,16},{24,20},{28,24},{0,28},{5,1},{9... | collective-permute-start | bytes 2312 | tf_op jit(solution)/shard_map/ppermute | solution.py:27
  6.0 1.1 copy.13
  7.3 3.5 %collective-permute-start.1 = (f32[12,3,16,4]{3,0,2,1:T(8,128)S(1)}, f32[12,3,16,4]{3,0,2,1:T(8,128)S(1)}, u32[]{:S(2)}, u32[]{:S(2)}) collective-permute-start(f32[12,3,16,4]{3,0,2,1:T(8,128)S(1)} %get-tuple-element.53), channel_id=1, source_target_pairs={{4,0},{8,4},{12,8},{16,12},{20,16},{24,20},{28,24},{0,28},{5,1},{9... | collective-permute-start | bytes 27656 | tf_op jit(solution)/shard_map/ppermute | solution.py:27
  11.1 3.8 %collective-permute-start.6 = (f32[1,3,4,136]{3,2,1,0:T(4,128)S(1)}, f32[1,3,4,136]{3,2,1,0:T(4,128)S(1)}, u32[]{:S(2)}, u32[]{:S(2)}) collective-permute-start(f32[1,3,4,136]{3,2,1,0:T(4,128)S(1)} %get-tuple-element.66), channel_id=1, source_target_pairs={{0,1},{1,2},{2,3},{4,5},{5,6},{6,7},{8,9},{9,10},{10,11},{12,13},{... | collective-permute-start | bytes 19592 | tf_op jit(solution)/shard_map/ppermute | solution.py:24
  15.0 1.3 %collective-permute-start.7 = (f32[1,3,4,136]{3,2,1,0:T(4,128)S(1)}, f32[1,3,4,136]{3,2,1,0:T(4,128)S(1)}, u32[]{:S(2)}, u32[]{:S(2)}) collective-permute-start(f32[1,3,4,136]{3,2,1,0:T(4,128)S(1)} %get-tuple-element.67), channel_id=1, source_target_pairs={{1,0},{2,1},{3,2},{5,4},{6,5},{7,6},{9,8},{10,9},{11,10},{13,12},{... | collective-permute-start | bytes 19592 | tf_op jit(solution)/shard_map/ppermute | solution.py:27
  16.4 4.2 %collective-permute-done.7 = f32[1,3,4,136]{3,2,1,0:T(4,128)S(1)} collective-permute-done((f32[1,3,4,136]{3,2,1,0:T(4,128)S(1)}, f32[1,3,4,136]{3,2,1,0:T(4,128)S(1)}, u32[]{:S(2)}, u32[]{:S(2)}) %collective-permute-start.7) | collective-permute-done | bytes 6560 | tf_op jit(solution)/shard_map/ppermute | solution.py:27
  21.7 4.3 %collective-permute-start.2 = (f32[12,3,4,136]{3,0,2,1:T(8,128)S(1)}, f32[12,3,4,136]{3,0,2,1:T(8,128)S(1)}, u32[]{:S(2)}, u32[]{:S(2)}) collective-permute-start(f32[12,3,4,136]{3,0,2,1:T(8,128)S(1)} %get-tuple-element.18), channel_id=1, source_target_pairs={{0,1},{1,2},{2,3},{4,5},{5,6},{6,7},{8,9},{9,10},{10,11},{12,13},{... | collective-permute-start | bytes 235016 | tf_op jit(solution)/shard_map/ppermute | solution.py:24
  26.0 1.3 %collective-permute-start.3 = (f32[12,3,4,136]{3,0,2,1:T(8,128)S(1)}, f32[12,3,4,136]{3,0,2,1:T(8,128)S(1)}, u32[]{:S(2)}, u32[]{:S(2)}) collective-permute-start(f32[12,3,4,136]{3,0,2,1:T(8,128)S(1)} %get-tuple-element.19), channel_id=1, source_target_pairs={{1,0},{2,1},{3,2},{5,4},{6,5},{7,6},{9,8},{10,9},{11,10},{13,12},{... | collective-permute-start | bytes 235016 | tf_op jit(solution)/shard_map/ppermute | solution.py:27
  27.4 1.8 %collective-permute-done.2 = f32[12,3,4,136]{3,0,2,1:T(8,128)S(1)} collective-permute-done((f32[12,3,4,136]{3,0,2,1:T(8,128)S(1)}, f32[12,3,4,136]{3,0,2,1:T(8,128)S(1)}, u32[]{:S(2)}, u32[]{:S(2)}) %collective-permute-start.2) | collective-permute-done | bytes 78368 | tf_op jit(solution)/shard_map/ppermute | solution.py:24
  29.2 4.4 %collective-permute-done.3 = f32[12,3,4,136]{3,0,2,1:T(8,128)S(1)} collective-permute-done((f32[12,3,4,136]{3,0,2,1:T(8,128)S(1)}, f32[12,3,4,136]{3,0,2,1:T(8,128)S(1)}, u32[]{:S(2)}, u32[]{:S(2)}) %collective-permute-start.3) | collective-permute-done | bytes 78368 | tf_op jit(solution)/shard_map/ppermute | solution.py:27
  34.9 0.7 add_bitcast_fusion.2
  35.7 0.7 fusion.12
  42.5 3.5 %collective-permute-start.9 = (f32[12,3,16,4]{3,0,2,1:T(8,128)S(1)}, f32[12,3,16,4]{3,0,2,1:T(8,128)S(1)}, u32[]{:S(2)}, u32[]{:S(2)}) collective-permute-start(f32[12,3,16,4]{3,0,2,1:T(8,128)S(1)} %get-tuple-element.51), channel_id=1, source_target_pairs={{4,0},{8,4},{12,8},{16,12},{20,16},{24,20},{28,24},{0,28},{5,1},{9... | collective-permute-start | bytes 27656 | tf_op jit(solution)/shard_map/ppermute | solution.py:27
  46.0 9.6 %collective-permute-done.8 = f32[12,3,16,4]{3,0,2,1:T(8,128)S(1)} collective-permute-done((f32[12,3,16,4]{3,0,2,1:T(8,128)S(1)}, f32[12,3,16,4]{3,0,2,1:T(8,128)S(1)}, u32[]{:S(2)}, u32[]{:S(2)}) %collective-permute-start.8) | collective-permute-done | bytes 9248 | tf_op jit(solution)/shard_map/ppermute | solution.py:24
  55.8 3.3 %collective-permute-start.10 = (f32[12,3,4,136]{3,0,2,1:T(8,128)S(1)}, f32[12,3,4,136]{3,0,2,1:T(8,128)S(1)}, u32[]{:S(2)}, u32[]{:S(2)}) collective-permute-start(f32[12,3,4,136]{3,0,2,1:T(8,128)S(1)} %get-tuple-element.13), channel_id=1, source_target_pairs={{0,1},{1,2},{2,3},{4,5},{5,6},{6,7},{8,9},{9,10},{10,11},{12,13},{... | collective-permute-start | bytes 235016 | tf_op jit(solution)/shard_map/ppermute | solution.py:24
  59.1 1.5 %collective-permute-start.11 = (f32[12,3,4,136]{3,0,2,1:T(8,128)S(1)}, f32[12,3,4,136]{3,0,2,1:T(8,128)S(1)}, u32[]{:S(2)}, u32[]{:S(2)}) collective-permute-start(f32[12,3,4,136]{3,0,2,1:T(8,128)S(1)} %get-tuple-element.14), channel_id=1, source_target_pairs={{1,0},{2,1},{3,2},{5,4},{6,5},{7,6},{9,8},{10,9},{11,10},{13,12},{... | collective-permute-start | bytes 235016 | tf_op jit(solution)/shard_map/ppermute | solution.py:27
  60.6 1.7 %collective-permute-done.10 = f32[12,3,4,136]{3,0,2,1:T(8,128)S(1)} collective-permute-done((f32[12,3,4,136]{3,0,2,1:T(8,128)S(1)}, f32[12,3,4,136]{3,0,2,1:T(8,128)S(1)}, u32[]{:S(2)}, u32[]{:S(2)}) %collective-permute-start.10) | collective-permute-done | bytes 78368 | tf_op jit(solution)/shard_map/ppermute | solution.py:24
  62.3 4.4 %collective-permute-done.11 = f32[12,3,4,136]{3,0,2,1:T(8,128)S(1)} collective-permute-done((f32[12,3,4,136]{3,0,2,1:T(8,128)S(1)}, f32[12,3,4,136]{3,0,2,1:T(8,128)S(1)}, u32[]{:S(2)}, u32[]{:S(2)}) %collective-permute-start.11) | collective-permute-done | bytes 78368 | tf_op jit(solution)/shard_map/ppermute | solution.py:27
  67.8 0.7 add_bitcast_fusion
  76.0 37.1 %psum.7 = f32[12,12]{0,1:T(8,128)S(1)} all-reduce(f32[12,12]{0,1:T(8,128)S(1)} %fusion), channel_id=1, replica_groups=mesh['lon'=8,'lat'=4] {'lon','lat'}, use_global_device_ids=true, to_apply=%region_0.0 | all-reduce | flops 144 | bytes 1152 | tf_op jit(solution)/shard_map/psum | solution.py:149
  113.2 1.1 cholesky.16
  115.6 0.9 custom-call.7
  117.2 0.8 copy.21
  (88 shorter events, 20.9 us)
Async XLA Ops:
  1.4 9.6 %collective-permute-start.4 = (f32[1,3,16,4]{3,2,1,0:T(8,128)S(1)}, f32[1,3,16,4]{3,2,1,0:T(8,128)S(1)}, u32[]{:S(2)}, u32[]{:S(2)}) collective-permute-start(f32[1,3,16,4]{3,2,1,0:T(8,128)S(1)} %get-tuple-element.92), channel_id=1, source_target_pairs={{0,4},{4,8},{8,12},{12,16},{16,20},{20,24},{24,28},{28,0},{1,5},{5... | collective-permute-start | bytes 2312 | tf_op jit(solution)/shard_map/ppermute | solution.py:24
  1.9 9.1 %collective-permute-start.5 = (f32[1,3,16,4]{3,2,1,0:T(8,128)S(1)}, f32[1,3,16,4]{3,2,1,0:T(8,128)S(1)}, u32[]{:S(2)}, u32[]{:S(2)}) collective-permute-start(f32[1,3,16,4]{3,2,1,0:T(8,128)S(1)} %get-tuple-element.93), channel_id=1, source_target_pairs={{4,0},{8,4},{12,8},{16,12},{20,16},{24,20},{28,24},{0,28},{5,1},{9... | collective-permute-start | bytes 2312 | tf_op jit(solution)/shard_map/ppermute | solution.py:27
  7.2 14.2 %collective-permute-start = (f32[12,3,16,4]{3,0,2,1:T(8,128)S(1)}, f32[12,3,16,4]{3,0,2,1:T(8,128)S(1)}, u32[]{:S(2)}, u32[]{:S(2)}) collective-permute-start(f32[12,3,16,4]{3,0,2,1:T(8,128)S(1)} %get-tuple-element.52), channel_id=1, source_target_pairs={{0,4},{4,8},{8,12},{12,16},{16,20},{20,24},{24,28},{28,0},{1,5},{5... | collective-permute-start | bytes 27656 | tf_op jit(solution)/shard_map/ppermute | solution.py:24
  7.3 14.2 %collective-permute-start.1 = (f32[12,3,16,4]{3,0,2,1:T(8,128)S(1)}, f32[12,3,16,4]{3,0,2,1:T(8,128)S(1)}, u32[]{:S(2)}, u32[]{:S(2)}) collective-permute-start(f32[12,3,16,4]{3,0,2,1:T(8,128)S(1)} %get-tuple-element.53), channel_id=1, source_target_pairs={{4,0},{8,4},{12,8},{16,12},{20,16},{24,20},{28,24},{0,28},{5,1},{9... | collective-permute-start | bytes 27656 | tf_op jit(solution)/shard_map/ppermute | solution.py:27
  11.1 5.2 %collective-permute-start.6 = (f32[1,3,4,136]{3,2,1,0:T(4,128)S(1)}, f32[1,3,4,136]{3,2,1,0:T(4,128)S(1)}, u32[]{:S(2)}, u32[]{:S(2)}) collective-permute-start(f32[1,3,4,136]{3,2,1,0:T(4,128)S(1)} %get-tuple-element.66), channel_id=1, source_target_pairs={{0,1},{1,2},{2,3},{4,5},{5,6},{6,7},{8,9},{9,10},{10,11},{12,13},{... | collective-permute-start | bytes 19592 | tf_op jit(solution)/shard_map/ppermute | solution.py:24
  15.0 5.6 %collective-permute-start.7 = (f32[1,3,4,136]{3,2,1,0:T(4,128)S(1)}, f32[1,3,4,136]{3,2,1,0:T(4,128)S(1)}, u32[]{:S(2)}, u32[]{:S(2)}) collective-permute-start(f32[1,3,4,136]{3,2,1,0:T(4,128)S(1)} %get-tuple-element.67), channel_id=1, source_target_pairs={{1,0},{2,1},{3,2},{5,4},{6,5},{7,6},{9,8},{10,9},{11,10},{13,12},{... | collective-permute-start | bytes 19592 | tf_op jit(solution)/shard_map/ppermute | solution.py:27
  21.7 7.5 %collective-permute-start.2 = (f32[12,3,4,136]{3,0,2,1:T(8,128)S(1)}, f32[12,3,4,136]{3,0,2,1:T(8,128)S(1)}, u32[]{:S(2)}, u32[]{:S(2)}) collective-permute-start(f32[12,3,4,136]{3,0,2,1:T(8,128)S(1)} %get-tuple-element.18), channel_id=1, source_target_pairs={{0,1},{1,2},{2,3},{4,5},{5,6},{6,7},{8,9},{9,10},{10,11},{12,13},{... | collective-permute-start | bytes 235016 | tf_op jit(solution)/shard_map/ppermute | solution.py:24
  26.0 7.6 %collective-permute-start.3 = (f32[12,3,4,136]{3,0,2,1:T(8,128)S(1)}, f32[12,3,4,136]{3,0,2,1:T(8,128)S(1)}, u32[]{:S(2)}, u32[]{:S(2)}) collective-permute-start(f32[12,3,4,136]{3,0,2,1:T(8,128)S(1)} %get-tuple-element.19), channel_id=1, source_target_pairs={{1,0},{2,1},{3,2},{5,4},{6,5},{7,6},{9,8},{10,9},{11,10},{13,12},{... | collective-permute-start | bytes 235016 | tf_op jit(solution)/shard_map/ppermute | solution.py:27
  42.4 13.2 %collective-permute-start.8 = (f32[12,3,16,4]{3,0,2,1:T(8,128)S(1)}, f32[12,3,16,4]{3,0,2,1:T(8,128)S(1)}, u32[]{:S(2)}, u32[]{:S(2)}) collective-permute-start(f32[12,3,16,4]{3,0,2,1:T(8,128)S(1)} %get-tuple-element.50), channel_id=1, source_target_pairs={{0,4},{4,8},{8,12},{12,16},{16,20},{20,24},{24,28},{28,0},{1,5},{5... | collective-permute-start | bytes 27656 | tf_op jit(solution)/shard_map/ppermute | solution.py:24
  42.5 13.1 %collective-permute-start.9 = (f32[12,3,16,4]{3,0,2,1:T(8,128)S(1)}, f32[12,3,16,4]{3,0,2,1:T(8,128)S(1)}, u32[]{:S(2)}, u32[]{:S(2)}) collective-permute-start(f32[12,3,16,4]{3,0,2,1:T(8,128)S(1)} %get-tuple-element.51), channel_id=1, source_target_pairs={{4,0},{8,4},{12,8},{16,12},{20,16},{24,20},{28,24},{0,28},{5,1},{9... | collective-permute-start | bytes 27656 | tf_op jit(solution)/shard_map/ppermute | solution.py:27
  55.8 6.5 %collective-permute-start.10 = (f32[12,3,4,136]{3,0,2,1:T(8,128)S(1)}, f32[12,3,4,136]{3,0,2,1:T(8,128)S(1)}, u32[]{:S(2)}, u32[]{:S(2)}) collective-permute-start(f32[12,3,4,136]{3,0,2,1:T(8,128)S(1)} %get-tuple-element.13), channel_id=1, source_target_pairs={{0,1},{1,2},{2,3},{4,5},{5,6},{6,7},{8,9},{9,10},{10,11},{12,13},{... | collective-permute-start | bytes 235016 | tf_op jit(solution)/shard_map/ppermute | solution.py:24
  59.1 7.6 %collective-permute-start.11 = (f32[12,3,4,136]{3,0,2,1:T(8,128)S(1)}, f32[12,3,4,136]{3,0,2,1:T(8,128)S(1)}, u32[]{:S(2)}, u32[]{:S(2)}) collective-permute-start(f32[12,3,4,136]{3,0,2,1:T(8,128)S(1)} %get-tuple-element.14), channel_id=1, source_target_pairs={{1,0},{2,1},{3,2},{5,4},{6,5},{7,6},{9,8},{10,9},{11,10},{13,12},{... | collective-permute-start | bytes 235016 | tf_op jit(solution)/shard_map/ppermute | solution.py:27
where the time goes:
time: 120 us; the launch traced here: 119 us
  blocking collectives  37.1 us (31%)
  starting transfers between devices  27.2 us (23%)
  waiting for transfers between devices  26.1 us (22%)
  other arithmetic  22 us (18%)
  local copies, waits for them, and re-layouts  4 us (3%)
    psum x1, blocking collectives, per_device(): gram = lax.psum(local_gram, ('lon', 'lat'))  37.1 us
    ppermute x6, starting transfers between devices, with_halo(): lax.ppermute(lax.slice_in_dim(block, 0, width, axis=dim), axis, backward)  15.2 us
    another operation x26, other arithmetic, advance(): return jnp.stack([new_x, new_y, new_height], axis=-3)  13.7 us
    ppermute x6, waiting for transfers between devices, with_halo(): lax.ppermute(lax.slice_in_dim(block, block.shape[dim] - width, None, axis...  13.1 us
    ppermute x6, waiting for transfers between devices, with_halo(): lax.ppermute(lax.slice_in_dim(block, 0, width, axis=dim), axis, backward)  13 us
    ppermute x6, starting transfers between devices, with_halo(): lax.ppermute(lax.slice_in_dim(block, block.shape[dim] - width, None, axis...  12 us
    unnamed x3, local copies, waits for them, and re-layouts  2.55 us
  transfers between devices with their start and end apart: 12, of which 6 were waited for; matrix products, arithmetic and copies ran while one was open for 2% of the time, Pallas kernels for 0%

commit v1 on v0

v1 whole, which is shorter than its diff:
```python
import functools
import math

import jax
import jax.numpy as jnp
from jax import lax
from jax.experimental import pallas as pl
from jax.experimental.pallas import tpu as pltpu
from jax.sharding import PartitionSpec as P

STEPS = 8
HALO = STEPS
LANES = 128
PLANE = 40
STRIP = 3 * HALO
SLOTS = LANES // STRIP
NCOEF = 18

advect_rate = 0.1
turn_rate = 0.5
gravity_rate = 0.2
diffuse_rate = 0.12

VMEM = pl.BlockSpec(memory_space=pltpu.VMEM)
PARAMS = pltpu.CompilerParams(vmem_limit_bytes=32 * 1024 * 1024)


def shift_e(x):
    return pltpu.roll(x, x.shape[-1] - 1, axis=x.ndim - 1)


def shift_w(x):
    return pltpu.roll(x, 1, axis=x.ndim - 1)


def rotate(x, amount):
    amount = amount % LANES
    return x if amount == 0 else pltpu.roll(x, amount, axis=x.ndim - 1)


def lane_ids(rows):
    return lax.broadcasted_iota(jnp.int32, (rows, LANES), 1)


def dynamic_zero():
    return jnp.minimum(lax.axis_index("lat"), 0)


def store_coefs(base, offset, rows_ref, coef, coef_offset):
    half_a = 0.5 * advect_rate
    for t in range(4):
        m = rows_ref[0, 8 * t : 8 * t + 8, :]
        turn = rows_ref[1, 8 * t : 8 * t + 8, :]

        def three(v):
            start = offset + v * PLANE + 8 * t
            return [base[pl.ds(start + d, 8), :] for d in range(3)]

        us, u, un = three(0)
        vs, v, vn = three(1)
        hs, h, hn = three(2)
        ue, uw, ve, vw, he, hw = shift_e(u), shift_w(u), shift_e(v), shift_w(v), shift_e(h), shift_w(h)
        centre = (1.0 - 4.0 * diffuse_rate) * m
        dif = diffuse_rate * m
        am = half_a * m
        values = [
            dif - am * u,
            dif + am * u,
            dif - am * v,
            dif + am * v,
            centre - am * (ue - uw),
            turn - am * (un - us),
            centre - am * (vn - vs),
            -turn - am * (ve - vw),
            (0.5 * gravity_rate) * m,
            dif - am * ue,
            dif + am * uw,
            dif - am * vn,
            dif + am * vs,
            -am * he,
            am * hw,
            -am * hn,
            am * hs,
            centre,
        ]
        for i, value in enumerate(values):
            coef[pl.ds(coef_offset + i * PLANE + 8 * t, 8), :] = value


def tiles_of(step):
    return -(-(32 - 2 * step) // 8)


def advance(src, dst, step, groups):
    for t in range(tiles_of(step)):
        for coef, coef_offset, triples in groups:
            (ae, aw, an, as_, cu, du, cv, dv, k1, he, hw, hn, hs, ue, uw, vn, vs, c0) = [
                coef[pl.ds(coef_offset + i * PLANE + 8 * t + step - 1, 8), :] for i in range(NCOEF)
            ]
            for offset in triples:

                def three(v):
                    start = offset + v * PLANE + 8 * t
                    return [src[pl.ds(start + d, 8), :] for d in range(3)]

                u_s, u, u_n = three(0)
                v_s, v, v_n = three(1)
                h_s, h, h_n = three(2)
                u_e, u_w = shift_e(u), shift_w(u)
                v_e, v_w = shift_e(v), shift_w(v)
                h_e, h_w = shift_e(h), shift_w(h)
                new_u = (
                    (ae * u_e + aw * u_w) + (an * u_n + as_ * u_s) + (cu * u + du * v) + k1 * (h_w - h_e)
                )
                new_v = (
                    (ae * v_e + aw * v_w) + (an * v_n + as_ * v_s) + (cv * v + dv * u) + k1 * (h_s - h_n)
                )
                new_h = (
                    (he * h_e + hw * h_w)
                    + (hn * h_n + hs * h_s)
                    + (ue * u_e + uw * u_w)
                    + (vn * v_n + vs * v_s)
                    + c0 * h
                )
                dst[pl.ds(offset + 8 * t, 8), :] = new_u
                dst[pl.ds(offset + PLANE + 8 * t, 8), :] = new_v
                dst[pl.ds(offset + 2 * PLANE + 8 * t, 8), :] = new_h


def parity(axis):
    return lax.rem(lax.axis_index(axis), 2) == 0


def pack_kernel(members, pert, wind, height, recv_a, recv_b, msg_a, msg_b):
    lat_even = parity("lat")
    lon_even = parity("lon")
    lanes8 = lane_ids(8)
    for v in range(3):
        for piece in range(4):
            pack_e = None
            for m in range(members + 1):
                if piece in (1, 2):
                    rows = slice(8 * piece - 8, 8 * piece)
                    if m < members:
                        x = pert[m, v, rows, :]
                    elif v < 2:
                        x = wind[v, rows, :]
                    else:
                        x = height[rows, :]
                else:
                    north = lat_even if piece == 0 else jnp.logical_not(lat_even)
                    x = jnp.where(north, recv_b[m, v], recv_a[m, v])
                to_w = rotate(x, HALO * m)
                to_e = rotate(x, HALO * m + HALO)
                if m == 0:
                    pack_w, pack_e = to_w, to_e
                else:
                    here = lanes8 >= HALO * m
                    pack_w = jnp.where(here, to_w, pack_w)
                    pack_e = jnp.where(here, to_e, pack_e)
            rows = slice(8 * piece, 8 * piece + 8)
            msg_a[v, rows, :] = jnp.where(lon_even, pack_e, pack_w)
            msg_b[v, rows, :] = jnp.where(lon_even, pack_w, pack_e)


def strip_places(members):
    full = members // SLOTS
    left = members - full * SLOTS
    places = {}
    sets = []
    for side in (0, 1):
        for g in range(full):
            for s in range(SLOTS):
                places[(g * SLOTS + s, side)] = (len(sets), s)
            sets.append(side)
    for r in range(left):
        places[(full * SLOTS + r, 0)] = (len(sets), r)
        places[(full * SLOTS + r, 1)] = (len(sets), left + r)
    sets.append(2)
    return places, sets, left


def centre_kernel(
    members, pert, wind, height, recv_a, recv_b, rows_ref, centre, strips, base_strips, first, second, base, coef
):
    zero = dynamic_zero()
    lat_even = parity("lat")
    off_a = pl.multiple_of(jnp.where(lat_even, 24, 0), 8)
    off_b = pl.multiple_of(jnp.where(lat_even, 0, 24), 8)
    for m in range(members + 1):
        for v in range(3):
            if m < members:
                plane, own = first, pert[m, v]
                start = (3 * m + v) * PLANE
            else:
                plane, own = base, (wind[v] if v < 2 else height[...])
                start = v * PLANE
            plane[start + 8 : start + 24, :] = own
            plane[pl.ds(start + off_a, 8), :] = recv_a[m, v]
            plane[pl.ds(start + off_b, 8), :] = recv_b[m, v]
    store_coefs(base, zero, rows_ref, coef, zero)

    places, sets, left = strip_places(members)
    lanes8 = lane_ids(8)
    for v in range(3):
        for t in range(4):
            rows = slice(8 * t, 8 * t + 8)
            groups = [None] * len(sets)
            for m in range(members):
                start = (3 * m + v) * PLANE + 8 * t
                x = first[start : start + 8, :]
                for side in (0, 1):
                    g, s = places[(m, side)]
                    moved = rotate(x, STRIP * s + (HALO if side == 0 else 2 * HALO))
                    if groups[g] is None:
                        groups[g] = moved
                    else:
                        here = (lanes8 >= STRIP * s) & (lanes8 < STRIP * s + STRIP)
                        groups[g] = jnp.where(here, moved, groups[g])
            for g in range(len(sets)):
                strips[v, g, rows, :] = groups[g]
            start = v * PLANE + 8 * t
            x = base[start : start + 8, :]
            for side in (0, 1):
                acc = None
                for s in range(SLOTS):
                    moved = rotate(x, STRIP * s + (HALO if side == 0 else 2 * HALO))
                    acc = moved if s == 0 else jnp.where(lanes8 >= STRIP * s, moved, acc)
                base_strips[v, side, rows, :] = acc

    per_iter = 3

    def some_members(i, carry):
        offsets = [(i * per_iter + j) * (3 * PLANE) for j in range(per_iter)]
        refs = [first, second]
        for step in range(1, STEPS + 1):
            advance(refs[(step - 1) % 2], refs[step % 2], step, [(coef, zero, offsets)])
        for j in range(per_iter):
            for v in range(3):
                centre[i * per_iter + j, v] = refs[STEPS % 2][pl.ds(offsets[j] + v * PLANE, 16), :]
        return carry

    lax.fori_loop(0, members // per_iter, some_members, 0)


def strips_kernel(
    members, centre, strips, base_strips, got_a, got_b, rows_ref, fields, send, first, second, base, coef, pairs
):
    zero = dynamic_zero()
    lon_even = parity("lon")
    places, sets, left = strip_places(members)
    lanes8 = lane_ids(8)
    in_strip = lax.rem(lanes8, STRIP)
    for v in range(3):
        for t in range(4):
            rows = slice(8 * t, 8 * t + 8)
            a, b = got_a[v, rows, :], got_b[v, rows, :]
            halos = [jnp.where(lon_even, b, a), jnp.where(lon_even, a, b)]
            groups = [strips[v, g, rows, :] for g in range(len(sets))]
            for m in range(members):
                for side in (0, 1):
                    g, s = places[(m, side)]
                    low = STRIP * s + (0 if side == 0 else 2 * HALO)
                    moved = rotate(halos[side], low - HALO * m)
                    groups[g] = jnp.where((lanes8 >= low) & (lanes8 < low + HALO), moved, groups[g])
            for g in range(len(sets)):
                start = (3 * g + v) * PLANE + 8 * t
                first[start : start + 8, :] = groups[g]
            basis = []
            for side in (0, 1):
                acc = None
                for s in range(SLOTS):
                    moved = rotate(halos[side], STRIP * s + (0 if side == 0 else 2 * HALO) - HALO * members)
                    acc = moved if s == 0 else jnp.where(lanes8 >= STRIP * s, moved, acc)
                here = (in_strip < HALO) if side == 0 else (in_strip >= 2 * HALO)
                basis.append(jnp.where(here, acc, base_strips[v, side, rows, :]))
            basis.append(jnp.where(lanes8 < STRIP * left, basis[0], basis[1]))
            for kind in range(3):
                start = (3 * kind + v) * PLANE + 8 * t
                base[start : start + 8, :] = basis[kind]
    for kind in range(3):
        store_coefs(base, zero + kind * 3 * PLANE, rows_ref, coef, zero + kind * NCOEF * PLANE)
    refs = [first, second]
    work = [
        (coef, zero + kind * NCOEF * PLANE, [zero + g * 3 * PLANE for g in range(len(sets)) if sets[g] == kind])
        for kind in range(3)
    ]
    for step in range(1, STEPS + 1):
        advance(refs[(step - 1) % 2], refs[step % 2], step, work)
    done = refs[STEPS % 2]
    lanes16 = lane_ids(16)
    for m in range(members):
        for v in range(3):
            x = centre[m, v]
            for side in (0, 1):
                g, s = places[(m, side)]
                start = (3 * g + v) * PLANE
                moved = rotate(done[start : start + 16, :], (0 if side == 0 else LANES - HALO) - STRIP * s - HALO)
                here = (lanes16 < HALO) if side == 0 else (lanes16 >= LANES - HALO)
                x = jnp.where(here, moved, x)
            fields[m, v] = x
    pairs[...] = jnp.zeros_like(pairs)
    index = 0
    for i in range(members):
        for j in range(i, members):
            total = None
            for v in range(3):
                prod = fields[i, v] * fields[j, v]
                part = prod[:8] + prod[8:]
                total = part if total is None else total + part
            pairs[8 * index : 8 * index + 8, :] = total
            index += 1
    partial = pairs[pl.ds(0, LANES, stride=8), :]
    for s in range(1, 8):
        partial = partial + pairs[pl.ds(s, LANES, stride=8), :]
    row = jnp.sum(partial.T, axis=0, keepdims=True)
    send[...] = jnp.broadcast_to(row, send.shape)


def final_kernel(members, count, fields, got, out, factor):
    total = got[0:8, :]
    for r in range(8, got.shape[0], 8):
        total = total + got[r : r + 8, :]
    packed = jnp.sum(total, axis=0, keepdims=True) / count
    packed = jnp.broadcast_to(packed, (8, LANES))
    rows = []
    at = 0
    for i in range(members):
        rows.append(rotate(packed, i - at))
        at += members - i
    x = [[fields[m, v] for v in range(3)] for m in range(members)]
    lanes8 = lane_ids(8)
    for k in range(members):
        spread = [
            jnp.broadcast_to(rows[k][:, i : i + 1], (8, LANES)) if i >= k else None for i in range(members)
        ]
        inverse = 1.0 / spread[k]
        scale = lax.rsqrt(spread[k])
        scale16 = jnp.concatenate([scale, scale], axis=0)
        for v in range(3):
            out[k, v] = x[k][v] * scale16
        kept = (lanes8 >= k) & (lanes8 < members)
        factor[k : k + 1, :] = jnp.where(kept, rows[k] * scale, 0.0)[0:1, :members]
        for i in range(k + 1, members):
            times = spread[i] * inverse
            rows[i] = rows[i] - times * rows[k]
            times16 = jnp.concatenate([times, times], axis=0)
            for v in range(3):
                x[i][v] = x[i][v] - times16 * x[k][v]


def swap(block, axis, count, even_up, periodic):
    pairs = []
    for i in range(count):
        other = i + 1 if (i % 2 == 0) == even_up else i - 1
        if periodic:
            other %= count
        if 0 <= other < count:
            pairs.append((i, other))
    return lax.ppermute(block, axis, pairs)


def per_device(perturbations, base_wind, base_height):
    members, _, rows, cols = perturbations.shape
    n_lat, n_lon = lax.axis_size("lat"), lax.axis_size("lon")
    devices = n_lat * n_lon
    total_rows = rows * n_lat
    total_cols = cols * n_lon
    f32 = jnp.float32

    glob = lax.axis_index("lat") * rows - HALO + 1 + jnp.arange(PLANE, dtype=jnp.int32)
    inside = ((glob >= 0) & (glob < total_rows)).astype(f32)
    turning = turn_rate * inside * jnp.sin(math.pi * ((glob.astype(f32) + 0.5) / total_rows - 0.5))
    row_facts = jnp.broadcast_to(jnp.stack([inside, turning])[:, :, None], (2, PLANE, LANES))

    base = jnp.concatenate([base_wind, base_height[None]], axis=0)
    everything = jnp.concatenate([perturbations, base[None]], axis=0)
    top, bottom = everything[:, :, :HALO], everything[:, :, rows - HALO :]
    lat_even = lax.axis_index("lat") % 2 == 0
    recv_b = swap(jnp.where(lat_even, top, bottom), "lat", n_lat, False, False)
    recv_a = swap(jnp.where(lat_even, bottom, top), "lat", n_lat, True, False)

    message = jax.ShapeDtypeStruct((3, 32, LANES), f32)
    msg_a, msg_b = pl.pallas_call(
        functools.partial(pack_kernel, members),
        out_shape=[message, message],
        in_specs=[VMEM] * 5,
        out_specs=[VMEM] * 2,
        compiler_params=PARAMS,
        name="pack",
    )(perturbations, base_wind, base_height, recv_a, recv_b)
    got_b = swap(msg_b, "lon", n_lon, False, True)
    got_a = swap(msg_a, "lon", n_lon, True, True)

    _, sets, _ = strip_places(members)
    groups = len(sets)
    centre, strips, base_strips = pl.pallas_call(
        functools.partial(centre_kernel, members),
        out_shape=[
            jax.ShapeDtypeStruct(perturbations.shape, f32),
            jax.ShapeDtypeStruct((3, groups, 32, LANES), f32),
            jax.ShapeDtypeStruct((3, 2, 32, LANES), f32),
        ],
        in_specs=[VMEM] * 6,
        out_specs=[VMEM] * 3,
        scratch_shapes=[
            pltpu.VMEM((members * 3 * PLANE, LANES), f32),
            pltpu.VMEM((members * 3 * PLANE, LANES), f32),
            pltpu.VMEM((3 * PLANE, LANES), f32),
            pltpu.VMEM((NCOEF * PLANE, LANES), f32),
        ],
        compiler_params=PARAMS,
        cost_estimate=pl.CostEstimate(flops=20_000_000, bytes_accessed=2_000_000, transcendentals=0),
        name="centre",
    )(perturbations, base_wind, base_height, recv_a, recv_b, row_facts)

    fields, send = pl.pallas_call(
        functools.partial(strips_kernel, members),
        out_shape=[
            jax.ShapeDtypeStruct(perturbations.shape, f32),
            jax.ShapeDtypeStruct((devices, LANES), f32),
        ],
        in_specs=[VMEM] * 6,
        out_specs=[VMEM] * 2,
        scratch_shapes=[
            pltpu.VMEM((groups * 3 * PLANE, LANES), f32),
            pltpu.VMEM((groups * 3 * PLANE, LANES), f32),
            pltpu.VMEM((3 * 3 * PLANE, LANES), f32),
            pltpu.VMEM((3 * NCOEF * PLANE, LANES), f32),
            pltpu.VMEM((8 * LANES, LANES), f32),
        ],
        compiler_params=PARAMS,
        name="edges",
    )(centre, strips, base_strips, got_a, got_b, row_facts)

    got = lax.all_to_all(send, ("lon", "lat"), 0, 0, tiled=True)

    return pl.pallas_call(
        functools.partial(final_kernel, members, float(3 * total_rows * total_cols)),
        out_shape=[
            jax.ShapeDtypeStruct(perturbations.shape, f32),
            jax.ShapeDtypeStruct((members, members), f32),
        ],
        in_specs=[VMEM] * 2,
        out_specs=[VMEM] * 2,
        compiler_params=PARAMS,
        name="finish",
    )(fields, got)


def solution(mesh):
    return jax.shard_map(
        per_device,
        mesh=mesh,
        in_specs=(P(None, None, "lat", "lon"), P(None, "lat", "lon"), P("lat", "lon")),
        out_specs=(P(None, None, "lat", "lon"), P()),
        check_vma=False,
    )
```

time: 120 us -> 37.8 us (0.32)
  blocking collectives: 37.1 us -> 8.87 us
  other arithmetic: 22 us -> 1.19 us
  waiting for transfers between devices: 26.1 us -> 7.1 us
  starting transfers between devices: 27.2 us -> 10.2 us
  Pallas kernels: 0 us -> 8.63 us
  local copies, waits for them, and re-layouts: 4 us -> 0.77 us
    psum x1 -> x0, blocking collectives: 37.1 us -> none  [per_device(): gram = lax.psum(local_gram, ('lon', 'lat'))]
    ppermute x12 -> x4, waiting for transfers between devices: 26.1 us -> 7.1 us  [swap(): return lax.ppermute(block, axis, pairs)]
    ppermute x12 -> x4, starting transfers between devices: 27.2 us -> 10.2 us  [swap(): return lax.ppermute(block, axis, pairs)]
    another operation x30 -> x1, other arithmetic: 16.4 us -> 0.01 us  [per_device(): jnp.stack([inside, turning])[:, :, None]]
    all_to_all x0 -> x1, blocking collectives: none -> 8.87 us  [per_device(): got = lax.all_to_all(send, ('lon', 'lat'), 0, 0, tiled=True)]
    pallas_call x0 -> x4, Pallas kernels: none -> 8.63 us  [the longest x1 4.56 us: per_device(): pl.pallas_call(functools.partial(centre_kernel, members), out_shape=[jax....]
    unnamed x3 -> x6, local copies, waits for them, and re-layouts: 2.55 us -> 0.7 us
    mul x14 -> x1, other arithmetic: 1.47 us -> 0.05 us  [per_device(): turn_rate * inside]
  transfers between devices with their start and end apart: 12 -> 4, of which waited for: 6 -> 1; matrix products, arithmetic and copies ran while one was open for 2% -> 0% of each run, Pallas kernels for 0% -> 12%
where the time goes in v1:
time: 37.8 us; the launch traced here: 37.5 us
  starting transfers between devices  10.2 us (27%)
  blocking collectives  8.87 us (23%)
  Pallas kernels  8.63 us (23%)
  waiting for transfers between devices  7.1 us (19%)
  other arithmetic  1.19 us (3%)
  local copies, waits for them, and re-layouts  0.77 us (2%)
  between operations  0.73 us (2%)
    ppermute x4, starting transfers between devices, swap(): return lax.ppermute(block, axis, pairs)  10.2 us
    all_to_all x1, blocking collectives, per_device(): got = lax.all_to_all(send, ('lon', 'lat'), 0, 0, tiled=True)  8.87 us
    ppermute x4, waiting for transfers between devices, swap(): return lax.ppermute(block, axis, pairs)  7.1 us
    pallas_call x1, Pallas kernels, per_device(): pl.pallas_call(functools.partial(centre_kernel, members), out_shape=[jax....  4.56 us
    pallas_call x1, Pallas kernels, per_device(): pl.pallas_call(functools.partial(strips_kernel, members), out_shape=[jax....  1.99 us
    pallas_call x1, Pallas kernels, per_device(): pl.pallas_call(functools.partial(final_kernel, members, float(3 * total_r...  1.68 us
    select_n x1, other arithmetic, per_device(): recv_b = swap(jnp.where(lat_even, top, bottom), 'lat', n_lat, False, False)  1.13 us
  transfers between devices with their start and end apart: 4, of which 1 were waited for; matrix products, arithmetic and copies ran while one was open for 0% of the time, Pallas kernels for 12%

profile of v1, /device:TPU:0, one launch (start us, length us, event | category | flops | bytes accessed | tf_op | source)
XLA Modules:
  0.0 37.5 jit_solution(1870219270193628432)
XLA Ops:
  0.6 0.0 copy-start.1
  0.6 0.0 copy-start.2
  0.7 0.7 %copy-done.1 = f32[2,16,128]{2,1,0:T(8,128)S(1)} copy-done((f32[2,16,128]{2,1,0:T(8,128)S(1)}, f32[2,16,128]{2,1,0:T(8,128)}, u32[]{:S(2)}) %copy-start.1) | copy-done | bytes 16408
  1.3 0.0 copy-done.2
  1.4 0.0 copy-start
  1.4 1.1 %broadcast_select_fusion = (f32[13,3,8,128]{3,2,1,0:T(8,128)S(1)}, f32[13,3,8,128]{3,2,1,0:T(8,128)S(1)}) fusion(pred[]{:T(512)S(6)} %eq.5, f32[1,3,16,128]{3,2,1,0:T(8,128)S(1)} %maximum_bitcast_fusion, f32[12,3,16,128]{3,2,1,0:T(8,128)} %pert.3), kind=kLoop, calls=%fused_computation.4 | loop fusion | flops 199680 | bytes 638977 | tf_op jit(solution)/shard_map/jit(_where)/select_n | solution.py:380
  2.5 0.7 %collective-permute-start.1 = (f32[13,3,8,128]{3,2,1,0:T(8,128)S(1)}, f32[13,3,8,128]{3,2,1,0:T(8,128)S(1)}, u32[]{:S(2)}, u32[]{:S(2)}) collective-permute-start(f32[13,3,8,128]{3,2,1,0:T(8,128)S(1)} %get-tuple-element.16), channel_id=1, source_target_pairs={{1,2},{2,1},{5,6},{6,5},{9,10},{10,9},{13,14},{14,13},{17,18},{18,... | collective-permute-start | bytes 479240 | tf_op jit(solution)/shard_map/ppermute | solution.py:360
  3.2 5.7 %collective-permute-start = (f32[13,3,8,128]{3,2,1,0:T(8,128)S(1)}, f32[13,3,8,128]{3,2,1,0:T(8,128)S(1)}, u32[]{:S(2)}, u32[]{:S(2)}) collective-permute-start(f32[13,3,8,128]{3,2,1,0:T(8,128)S(1)} %get-tuple-element.17), channel_id=1, source_target_pairs={{0,1},{1,0},{2,3},{3,2},{4,5},{5,4},{6,7},{7,6},{8,9},{9,8},{10,11... | collective-permute-start | bytes 479240 | tf_op jit(solution)/shard_map/ppermute | solution.py:360
  9.0 0.0 collective-permute-done.1.recv_b
  9.0 7.1 %collective-permute-done.recv_a = f32[13,3,8,128]{3,2,1,0:T(8,128)S(1)} collective-permute-done((f32[13,3,8,128]{3,2,1,0:T(8,128)S(1)}, f32[13,3,8,128]{3,2,1,0:T(8,128)S(1)}, u32[]{:S(2)}, u32[]{:S(2)}) %collective-permute-start) | collective-permute-done | bytes 159776 | tf_op jit(solution)/shard_map/ppermute | solution.py:360
  16.1 0.0 copy-done
  16.1 0.4 %pack.1 = (f32[3,32,128]{2,1,0:T(8,128)S(1)}, f32[3,32,128]{2,1,0:T(8,128)S(1)}) custom-call(f32[12,3,16,128]{3,2,1,0:T(8,128)S(1)} %copy-done, f32[2,16,128]{2,1,0:T(8,128)S(1)} %copy-done.1, f32[16,128]{1,0:T(8,128)S(1)} %copy-done.2, f32[13,3,8,128]{3,2,1,0:T(8,128)S(1)} %collective-permute-done.recv_a, f32[13,3,8,128]{3,2,1,0:T(8,128)S(1)} %collective-permute-done.1.recv_b), custom_call_target="tpu_custom_call" | custom-call | tf_op jit(solution)/shard_map/pack/pallas_call | solution.py:384
  16.5 0.1 collective-permute-start.2
  16.5 3.7 %collective-permute-start.3 = (f32[3,32,128]{2,1,0:T(8,128)S(1)}, f32[3,32,128]{2,1,0:T(8,128)S(1)}, u32[]{:S(2)}, u32[]{:S(2)}) collective-permute-start(f32[3,32,128]{2,1,0:T(8,128)S(1)} %get-tuple-element.13), channel_id=1, source_target_pairs={{0,28},{4,8},{8,4},{12,16},{16,12},{20,24},{24,20},{28,0},{1,29},{... | collective-permute-start | bytes 147464 | tf_op jit(solution)/shard_map/ppermute | solution.py:360
  20.2 0.1 broadcast_in_dim.14.rows_ref
  20.3 4.6 %centre.1 = (f32[12,3,16,128]{3,2,1,0:T(8,128)S(1)}, f32[3,5,32,128]{3,2,1,0:T(8,128)S(1)}, f32[3,2,32,128]{3,2,1,0:T(8,128)S(1)}) custom-call(f32[12,3,16,128]{3,2,1,0:T(8,128)S(1)} %copy-done, f32[2,16,128]{2,1,0:T(8,128)S(1)} %copy-done.1, f32[16,128]{1,0:T(8,128)S(1)} %copy-done.2, f32[13,3,8,128]{3,2,1,0:T(8,128)S(1)} %collective-permute-done.recv_a, ...), custom_call_target="tpu_custom_call" | custom-call | flops 20000000 | bytes 2000000 | tf_op jit(solution)/shard_map/centre/pallas_call | solution.py:397
  24.9 0.0 collective-permute-done.2.got_a
  24.9 0.0 collective-permute-done.3.got_b
  24.9 2.0 %edges.1 = (f32[12,3,16,128]{3,2,1,0:T(8,128)S(1)}, f32[32,128]{1,0:T(8,128)S(1)}) custom-call(f32[12,3,16,128]{3,2,1,0:T(8,128)S(1)} %get-tuple-element.9.centre, f32[3,5,32,128]{3,2,1,0:T(8,128)S(1)} %get-tuple-element.10.strips, f32[3,2,32,128]{3,2,1,0:T(8,128)S(1)} %get-tuple-element.11.base_strips, f32[3,32,128]{2,1,0:T(8,128)S(1)} %collective-permute-done.2.got_a, ...), custom_call_target="tpu_custom_call" | custom-call | tf_op jit(solution)/shard_map/edges/pallas_call | solution.py:417
  26.9 8.9 %all_to_all.11 = f32[32,1,128]{2,1,0:T(1,128)S(1)} all-to-all(f32[32,1,128]{2,1,0:T(1,128)S(1)} %bitcast.9), channel_id=1, replica_groups=mesh['lon'=8,'lat'=4] {'lon','lat'}, dimensions={0} | all-to-all | bytes 32768 | tf_op jit(solution)/shard_map/all_to_all | solution.py:436
  35.8 1.7 %finish.1 = (f32[12,3,16,128]{3,2,1,0:T(8,128)}, f32[12,12]{1,0:T(8,128)}) custom-call(f32[12,3,16,128]{3,2,1,0:T(8,128)S(1)} %get-tuple-element.14.fields, f32[32,128]{1,0:T(8,128)S(1)} %bitcast.8), custom_call_target="tpu_custom_call" | custom-call | tf_op jit(solution)/shard_map/finish/pallas_call | solution.py:438
  (4 shorter events, 0.1 us)
Async XLA Ops:
  0.6 0.7 %copy-start.1 = (f32[2,16,128]{2,1,0:T(8,128)S(1)}, f32[2,16,128]{2,1,0:T(8,128)}, u32[]{:S(2)}) copy-start(f32[2,16,128]{2,1,0:T(8,128)} %wind.3) | copy-start | bytes 49156
  0.6 0.7 %copy-start.2 = (f32[16,128]{1,0:T(8,128)S(1)}, f32[16,128]{1,0:T(8,128)}, u32[]{:S(2)}) copy-start(f32[16,128]{1,0:T(8,128)} %height.3) | copy-start | bytes 24580
  1.4 14.7 %copy-start = (f32[12,3,16,128]{3,2,1,0:T(8,128)S(1)}, f32[12,3,16,128]{3,2,1,0:T(8,128)}, u32[]{:S(2)}) copy-start(f32[12,3,16,128]{3,2,1,0:T(8,128)} %pert.3) | copy-start | bytes 884740
  2.5 6.5 %collective-permute-start.1 = (f32[13,3,8,128]{3,2,1,0:T(8,128)S(1)}, f32[13,3,8,128]{3,2,1,0:T(8,128)S(1)}, u32[]{:S(2)}, u32[]{:S(2)}) collective-permute-start(f32[13,3,8,128]{3,2,1,0:T(8,128)S(1)} %get-tuple-element.16), channel_id=1, source_target_pairs={{1,2},{2,1},{5,6},{6,5},{9,10},{10,9},{13,14},{14,13},{17,18},{18,... | collective-permute-start | bytes 479240 | tf_op jit(solution)/shard_map/ppermute | solution.py:360
  3.2 12.9 %collective-permute-start = (f32[13,3,8,128]{3,2,1,0:T(8,128)S(1)}, f32[13,3,8,128]{3,2,1,0:T(8,128)S(1)}, u32[]{:S(2)}, u32[]{:S(2)}) collective-permute-start(f32[13,3,8,128]{3,2,1,0:T(8,128)S(1)} %get-tuple-element.17), channel_id=1, source_target_pairs={{0,1},{1,0},{2,3},{3,2},{4,5},{5,4},{6,7},{7,6},{8,9},{9,8},{10,11... | collective-permute-start | bytes 479240 | tf_op jit(solution)/shard_map/ppermute | solution.py:360
  16.5 8.4 %collective-permute-start.2 = (f32[3,32,128]{2,1,0:T(8,128)S(1)}, f32[3,32,128]{2,1,0:T(8,128)S(1)}, u32[]{:S(2)}, u32[]{:S(2)}) collective-permute-start(f32[3,32,128]{2,1,0:T(8,128)S(1)} %get-tuple-element.12), channel_id=1, source_target_pairs={{0,4},{4,0},{8,12},{12,8},{16,20},{20,16},{24,28},{28,24},{1,5},{5... | collective-permute-start | bytes 147464 | tf_op jit(solution)/shard_map/ppermute | solution.py:360
  16.5 8.4 %collective-permute-start.3 = (f32[3,32,128]{2,1,0:T(8,128)S(1)}, f32[3,32,128]{2,1,0:T(8,128)S(1)}, u32[]{:S(2)}, u32[]{:S(2)}) collective-permute-start(f32[3,32,128]{2,1,0:T(8,128)S(1)} %get-tuple-element.13), channel_id=1, source_target_pairs={{0,28},{4,8},{8,4},{12,16},{16,12},{20,24},{24,20},{28,0},{1,29},{... | collective-permute-start | bytes 147464 | tf_op jit(solution)/shard_map/ppermute | solution.py:360

commit v2 on v0

v2 whole, which is shorter than its diff:
```python
import functools
import math

import jax
import jax.numpy as jnp
from jax import lax
from jax.experimental import pallas as pl
from jax.experimental.pallas import tpu as pltpu
from jax.sharding import PartitionSpec as P

STEPS = 8
HALO = STEPS
TILE = 8
LANES = 128
FACTS = 40
STRIP = 3 * HALO
SLOTS = LANES // STRIP
MIX = 2 * STRIP + HALO
KINDS = 3
NCOEF = 18

advect_rate = 0.1
turn_rate = 0.5
gravity_rate = 0.2
diffuse_rate = 0.12

f32 = jnp.float32
VMEM = pl.BlockSpec(memory_space=pltpu.VMEM)
HBM = pl.BlockSpec(memory_space=pltpu.HBM)
PARAMS = pltpu.CompilerParams(vmem_limit_bytes=40 * 1024 * 1024)


def rotate(x, amount):
    amount = amount % LANES
    return x if amount == 0 else pltpu.roll(x, amount, axis=x.ndim - 1)


def lane_ids(rows=TILE):
    return lax.broadcasted_iota(jnp.int32, (rows, LANES), 1)


def dynamic_zero():
    return jnp.minimum(lax.axis_index("lat"), 0)


def is_even(axis):
    return lax.rem(lax.axis_index(axis), 2) == 0


def store_coefs(base, at, stride, facts, facts_at, coef, coef_at, tiles):
    half = 0.5 * advect_rate
    for t in tiles:
        m = facts[0, pl.ds(facts_at + TILE * t, TILE), :]
        turn = facts[1, pl.ds(facts_at + TILE * t, TILE), :]

        def three(v):
            return [base[pl.ds(at + v * stride + TILE * t + d, TILE), :] for d in range(3)]

        us, u, un = three(0)
        vs, v, vn = three(1)
        hs, h, hn = three(2)
        ue, ve, he = rotate(u, -1), rotate(v, -1), rotate(h, -1)
        uw, vw, hw = rotate(u, 1), rotate(v, 1), rotate(h, 1)
        centre = (1.0 - 4.0 * diffuse_rate) * m
        dif = diffuse_rate * m
        am = half * m
        values = [
            dif - am * u,
            dif + am * u,
            dif - am * v,
            dif + am * v,
            centre - am * (ue - uw),
            turn - am * (un - us),
            centre - am * (vn - vs),
            -turn - am * (ve - vw),
            (0.5 * gravity_rate) * m,
            dif - am * ue,
            dif + am * uw,
            dif - am * vn,
            dif + am * vs,
            -am * he,
            am * hw,
            -am * hn,
            am * hs,
            centre,
        ]
        for i, value in enumerate(values):
            coef[pl.ds(coef_at + i * FACTS + TILE * t, TILE), :] = value


def load_coefs(coef, at):
    return [coef[pl.ds(at + i * FACTS, TILE), :] for i in range(NCOEF)]


def step_tile(src, at, stride, coefs):
    (ae, aw, an, as_, cu, du, cv, dv, k1, he, hw, hn, hs, ue, uw, vn, vs, c0) = coefs

    def three(v):
        return [src[pl.ds(at + v * stride + d, TILE), :] for d in range(3)]

    u_s, u, u_n = three(0)
    v_s, v, v_n = three(1)
    h_s, h, h_n = three(2)
    u_e, v_e, h_e = rotate(u, -1), rotate(v, -1), rotate(h, -1)
    u_w, v_w, h_w = rotate(u, 1), rotate(v, 1), rotate(h, 1)
    new_u = (ae * u_e + aw * u_w) + (an * u_n + as_ * u_s) + (cu * u + du * v) + k1 * (h_w - h_e)
    new_v = (ae * v_e + aw * v_w) + (an * v_n + as_ * v_s) + (cv * v + dv * u) + k1 * (h_s - h_n)
    new_h = (he * h_e + hw * h_w) + (hn * h_n + hs * h_s) + (ue * u_e + uw * u_w) + (vn * v_n + vs * v_s) + c0 * h
    return new_u, new_v, new_h


PYRAMID = 24
FRONT = 8


def pyramid(refs, zero, work, hist):
    def keep(step, source, plane):
        start = zero + FRONT + plane * PYRAMID
        hist[0, step, plane] = source[pl.ds(start, TILE), :]
        hist[1, step, plane] = source[pl.ds(start + TILE - 2 * step, TILE), :]

    for step in range(1, STEPS):
        src, dst = refs[(step - 1) % 2], refs[step % 2]
        for t in range(-(-(16 - 2 * step) // TILE)):
            for coef, coef_at, triples in work:
                coefs = load_coefs(coef, coef_at + TILE * t + step - 1)
                for triple in triples:
                    at = FRONT + 3 * triple * PYRAMID + TILE * t
                    new = step_tile(src, zero + at, PYRAMID, coefs)
                    for v in range(3):
                        dst[pl.ds(zero + at + v * PYRAMID, TILE), :] = new[v]
        for _, _, triples in work:
            for triple in triples:
                for v in range(3):
                    keep(step, dst, 3 * triple + v)


def first_level(hist, plane, low, high):
    hist[0, 0, plane] = low
    hist[1, 0, plane] = high


def slot_range(s, shift):
    lanes = (lane_ids() + shift) % LANES
    return (lanes >= STRIP * s) & (lanes < STRIP * s + STRIP)


def in_strip():
    return lane_ids() % STRIP


def own_strips(rows_of, members):
    vectors = []
    for q in range(-(-members // SLOTS)):
        west = east = None
        for s in range(min(SLOTS, members - SLOTS * q)):
            moved = rotate(rows_of(SLOTS * q + s), STRIP * s + HALO)
            west = moved if s == 0 else jnp.where(slot_range(s, 0), moved, west)
            east = moved if s == 0 else jnp.where(slot_range(s, HALO), moved, east)
        vectors.append((west, east))
    return vectors


def base_own_strips(rows):
    west = east = None
    for s in range(SLOTS):
        moved = rotate(rows, STRIP * s + HALO)
        west = moved if s == 0 else jnp.where(slot_range(s, 0), moved, west)
        east = moved if s == 0 else jnp.where(slot_range(s, HALO), moved, east)
    return west, east


def mix(west, east):
    return jnp.where(lane_ids() < 2 * STRIP, west, rotate(east, MIX))


def fill_strips(vectors, west_halo, east_halo):
    place = in_strip()
    wests, easts = [], []
    for q, (west, east) in enumerate(vectors):
        wests.append(jnp.where(place < HALO, rotate(west_halo, -HALO * q), west))
        here = (place >= HALO) & (place < 2 * HALO)
        easts.append(jnp.where(here, rotate(east_halo, -HALO * q), east))
    return wests[:-1] + easts[:-1] + [mix(wests[-1], easts[-1])]


def base_strips(rows, west_halo, east_halo, members):
    q, first = members // SLOTS, members % SLOTS
    place = in_strip()
    west, east = base_own_strips(rows)

    def everywhere(halo, edge):
        near = rotate(halo, -HALO * q)
        return jnp.where(lane_ids() < STRIP * first + edge, rotate(near, -STRIP * first), near)

    west = jnp.where(place < HALO, everywhere(west_halo, 0), west)
    here = (place >= HALO) & (place < 2 * HALO)
    east = jnp.where(here, everywhere(east_halo, HALO), east)
    return west, east, mix(west, east)


def strip_kinds(members):
    full = members // SLOTS
    return [0] * full + [1] * full + [2]


def load_kernel(members, pert, wind, height, own, msg_a, msg_b, sems):
    chunk = members // 4
    copies = [
        pltpu.make_async_copy(wind, own.at[members, pl.ds(0, 2)], sems.at[0]),
        pltpu.make_async_copy(height, own.at[members, 2], sems.at[1]),
    ]
    for i in range(4):
        part = pl.ds(i * chunk, chunk)
        copies.append(pltpu.make_async_copy(pert.at[part], own.at[part], sems.at[2 + i]))
    for copy in copies:
        copy.start()
    for copy in copies:
        copy.wait()
    lon_even = is_even("lon")
    lanes = lane_ids()
    for v in range(3):
        for t in range(2):
            rows = slice(TILE * t, TILE * t + TILE)
            to_e = to_w = None
            for q in range(3):
                for s in range(SLOTS):
                    low = STRIP * s + HALO * q
                    moved = rotate(own[min(SLOTS * q + s, members), v, rows, :], low + HALO)
                    if to_e is None:
                        to_e = to_w = moved
                    else:
                        to_e = jnp.where((lanes >= low) & (lanes < low + HALO), moved, to_e)
                        to_w = jnp.where((lanes >= low + HALO) & (lanes < low + 2 * HALO), moved, to_w)
            msg_a[v, rows, :] = jnp.where(lon_even, to_e, to_w)
            msg_b[v, rows, :] = jnp.where(lon_even, to_w, to_e)


def centre_kernel(members, total_rows, own, facts, hist, first, second, base, coef):
    zero = dynamic_zero()
    start = lax.axis_index("lat") * 16 - HALO + 1
    for t in range(FACTS // TILE):
        glob = start + TILE * t + lax.broadcasted_iota(jnp.int32, (TILE, LANES), 0)
        inside = ((glob >= 0) & (glob < total_rows)).astype(f32)
        rows = slice(TILE * t, TILE * t + TILE)
        facts[0, rows, :] = inside
        facts[1, rows, :] = turn_rate * inside * jnp.sin(math.pi * ((glob.astype(f32) + 0.5) / total_rows - 0.5))
    for m in range(members + 1):
        for v in range(3):
            low, high = own[m, v, 0:TILE, :], own[m, v, TILE:16, :]
            plane = 3 * m + v
            if m < members:
                ref, at = first, FRONT + plane * PYRAMID
                first_level(hist, plane, low, high)
            else:
                ref, at = base, FRONT + v * PYRAMID
            ref[at : at + TILE, :] = low
            ref[at + TILE : at + 16, :] = high
    store_coefs(base, zero + FRONT, PYRAMID, facts, HALO, coef, zero, range(2))
    pyramid([first, second], zero, [(coef, zero, list(range(members)))], hist)


def meet_kernel(members, own, got_a, got_b, send_a, send_b, west, east):
    lat_even, lon_even = is_even("lat"), is_even("lon")
    low = pl.multiple_of(jnp.where(lat_even, TILE, 0), TILE)
    for send, at in ((send_a, low), (send_b, TILE - low)):
        at = pl.multiple_of(at, TILE)
        for m in range(members + 1):
            for v in range(3):
                send[3 * m + v] = own[m, v, pl.ds(at, TILE), :]
        for v in range(3):
            a, b = got_a[v, pl.ds(at, TILE), :], got_b[v, pl.ds(at, TILE), :]
            send[3 * members + 3 + v] = jnp.where(lon_even, b, a)
            send[3 * members + 6 + v] = jnp.where(lon_even, a, b)
    for v in range(3):
        for t in range(2):
            rows = slice(TILE * t, TILE * t + TILE)
            west[v, rows, :] = jnp.where(lon_even, got_b[v, rows, :], got_a[v, rows, :])
            east[v, rows, :] = jnp.where(lon_even, got_a[v, rows, :], got_b[v, rows, :])


def edges_kernel(members, own, west, east, facts, hist, strip_base, first, second, base, coef):
    zero = dynamic_zero()
    kinds = strip_kinds(members)
    for v in range(3):
        for t in range(2):
            rows = slice(TILE * t, TILE * t + TILE)
            halos = west[v, rows, :], east[v, rows, :]
            strips = fill_strips(own_strips(lambda m: own[m, v, rows, :], members), *halos)
            for g, strip in enumerate(strips):
                at = FRONT + (3 * g + v) * PYRAMID + TILE * t
                first[at : at + TILE, :] = strip
                hist[t, 0, 3 * g + v] = strip
            for kind, strip in enumerate(base_strips(own[members, v, rows, :], *halos, members)):
                at = FRONT + (3 * kind + v) * PYRAMID + TILE * t
                base[at : at + TILE, :] = strip
                strip_base[kind, v, rows, :] = strip
    work = []
    for kind in range(KINDS):
        coef_at = zero + kind * NCOEF * FACTS
        store_coefs(base, zero + FRONT + 3 * kind * PYRAMID, PYRAMID, facts, HALO, coef, coef_at, range(2))
        work.append((coef, coef_at, [g for g in range(len(kinds)) if kinds[g] == kind]))
    pyramid([first, second], zero, work, hist)


WEDGE = 16
BASE = 40


def side_kernel(
    members, is_a, own, halo, facts, hist_c, hist_e, strip_base, partial_in, fields, result, *scratch
):
    base, base_e, coef, coef_e, pairs = scratch[:5]
    count = (len(scratch) - 5) // 2
    first, second = scratch[5 : 5 + count], scratch[5 + count :]
    north = jnp.logical_not(is_even("lat")) if is_a else is_even("lat")
    side = jnp.where(north, 0, 1)
    wedge_at = jnp.where(north, 0, TILE)
    hist_at = jnp.where(north, TILE, 0)
    read_at = jnp.where(north, 0, TILE - 2)
    own_at = jnp.where(north, 2 * TILE, 1)
    halo_at = jnp.where(north, TILE, 2 * TILE + 1)
    facts_at = jnp.where(north, 0, 2 * TILE - 1)
    zero = dynamic_zero()
    kinds = strip_kinds(members)
    groups = len(kinds)
    triples_c = list(range(members))
    planes_c = 3 * members

    for m in range(members):
        for v in range(3):
            first[m][pl.ds(wedge_at + v * WEDGE, TILE), :] = halo[3 * m + v]
    for v in range(3):
        west, east = halo[planes_c + 3 + v], halo[planes_c + 6 + v]
        strips = fill_strips(own_strips(lambda m: halo[3 * m + v], members), west, east)
        for g, strip in enumerate(strips):
            first[members + g][pl.ds(wedge_at + v * WEDGE, TILE), :] = strip
        for t in range(2):
            base[pl.ds(own_at + v * BASE + TILE * t, TILE), :] = own[members, v, TILE * t : TILE * t + TILE, :]
        base[pl.ds(halo_at + v * BASE, TILE), :] = halo[planes_c + v]
        for kind, strip in enumerate(base_strips(halo[planes_c + v], west, east, members)):
            plane = 3 * kind + v
            for t in range(2):
                base_e[pl.ds(own_at + plane * BASE + TILE * t, TILE), :] = strip_base[
                    kind, v, TILE * t : TILE * t + TILE, :
                ]
            base_e[pl.ds(halo_at + plane * BASE, TILE), :] = strip
    store_coefs(base, zero + TILE, BASE, facts, facts_at, coef, zero, range(2))
    work = [(coef, zero, triples_c)]
    for kind in range(KINDS):
        coef_at = zero + kind * NCOEF * FACTS
        store_coefs(base_e, zero + TILE + 3 * kind * BASE, BASE, facts, facts_at, coef_e, coef_at, range(2))
        work.append((coef_e, coef_at, [members + g for g in range(groups) if kinds[g] == kind]))

    refs = [first, second]

    def lean(step):
        for triple, ref in enumerate(refs[step % 2]):
            for v in range(3):
                if triple < members:
                    rows = hist_c[side, step, 3 * triple + v]
                else:
                    rows = hist_e[side, step, 3 * (triple - members) + v]
                ref[pl.ds(hist_at + v * WEDGE, TILE), :] = rows

    lean(0)
    for step in range(1, STEPS + 1):
        src, dst = refs[(step - 1) % 2], refs[step % 2]
        row = jnp.where(north, step - 1, STEPS - step)
        for ref, coef_at, triples in work:
            coefs = load_coefs(ref, coef_at + row)
            for triple in triples:
                new = step_tile(src[triple], read_at, WEDGE, coefs)
                for v in range(3):
                    dst[triple][pl.ds(wedge_at + v * WEDGE, TILE), :] = new[v]
        if step < STEPS:
            lean(step)

    done = refs[STEPS % 2]
    place = in_strip()
    lanes = lane_ids()
    edge = (lanes < HALO) | (lanes >= LANES - HALO)
    full = members // SLOTS
    for v in range(3):

        def strip(g):
            return done[members + g][pl.ds(wedge_at + v * WEDGE, TILE), :]

        for q in range(full + 1):
            west, east = (strip(q), strip(full + q)) if q < full else (strip(2 * full), rotate(strip(2 * full), -MIX))
            both = jnp.where((place >= HALO) & (place < 2 * HALO), west, east)
            for s in range(min(SLOTS, members - SLOTS * q)):
                m = SLOTS * q + s
                inner = done[m][pl.ds(wedge_at + v * WEDGE, TILE), :]
                fields[m, v] = jnp.where(edge, rotate(both, -STRIP * s - HALO), inner)
    for i in range(members):
        for j in range(i, members):
            at = TILE * pair_place(i, j, members)
            pairs[at : at + TILE, :] = (
                fields[i, 0] * fields[j, 0] + fields[i, 1] * fields[j, 1] + fields[i, 2] * fields[j, 2]
            )
    half = members // 2
    sums = []
    for a in range(members + 1):
        for b in range(half, TILE):
            at = TILE * (TILE * a + b)
            pairs[at : at + TILE, :] = jnp.zeros((TILE, LANES), f32)
        total = pairs[pl.ds(TILE * TILE * a, TILE, stride=TILE), :]
        for s in range(1, TILE):
            total = total + pairs[pl.ds(TILE * TILE * a + s, TILE, stride=TILE), :]
        sums.append(total)
    if is_a:
        for a in range(members + 1):
            result[TILE * a : TILE * a + TILE, :] = sums[a]
    else:
        packed = jnp.zeros((TILE, LANES), f32)
        for a in range(members + 1):
            total = jnp.sum(sums[a] + partial_in[TILE * a : TILE * a + TILE, :], axis=1, keepdims=True)
            packed = jnp.where(lanes == a, total, packed)
        packed = pltpu.roll(packed, 0, axis=1, stride=SPREAD, stride_axis=0)
        result[...] = jnp.broadcast_to(jnp.sum(packed, axis=0, keepdims=True), result.shape)


SPREAD = LANES // TILE


def pair_place(i, j, members):
    b = min(i, members - 1 - i)
    a = j - b if i == b else j + 1
    return TILE * a + b


def first_side_kernel(members, own, halo, facts, hist_c, hist_e, strip_base, fields, result, *scratch):
    side_kernel(members, True, own, halo, facts, hist_c, hist_e, strip_base, None, fields, result, *scratch)


def finish_kernel(members, count, fields_a, fields_b, got, out, factor_out, done, factor, sems):
    total = got[0:TILE, :]
    for r in range(TILE, got.shape[0], TILE):
        total = total + got[r : r + TILE, :]
    packed = jnp.sum(total, axis=0, keepdims=True) / count
    packed = jnp.broadcast_to(packed, (TILE, LANES))
    rows = []
    for i in range(members):
        b = min(i, members - 1 - i)
        rows.append(rotate(packed, b - SPREAD * b if i == b else -1 - SPREAD * b))
    a_at = pl.multiple_of(jnp.where(is_even("lat"), TILE, 0), TILE)
    places = [a_at, pl.multiple_of(TILE - a_at, TILE)]
    x = [[[ref[m, v] for v in range(3)] for ref in (fields_a, fields_b)] for m in range(members)]
    lanes = lane_ids()
    copies = []
    for k in range(members):
        spread = [
            jnp.broadcast_to(rows[k][:, i : i + 1], (TILE, LANES)) if i >= k else None for i in range(members)
        ]
        inverse = 1.0 / spread[k]
        scale = lax.rsqrt(spread[k])
        for half in range(2):
            for v in range(3):
                done[k, v, pl.ds(places[half], TILE), :] = x[k][half][v] * scale
        copy = pltpu.make_async_copy(done.at[k], out.at[k], sems.at[k])
        copy.start()
        copies.append(copy)
        kept = (lanes >= k) & (lanes < members)
        factor[k : k + 1, :] = jnp.where(kept, rows[k] * scale, 0.0)[0:1, :members]
        for i in range(k + 1, members):
            times = spread[i] * inverse
            rows[i] = rows[i] - times * rows[k]
            for half in range(2):
                for v in range(3):
                    x[i][half][v] = x[i][half][v] - times * x[k][half][v]
    copy = pltpu.make_async_copy(factor, factor_out, sems.at[members])
    copy.start()
    for copy in copies + [copy]:
        copy.wait()


def swap(block, axis, count, even_up, periodic):
    pairs = []
    for i in range(count):
        other = i + 1 if (i % 2 == 0) == even_up else i - 1
        if periodic:
            other %= count
        if 0 <= other < count:
            pairs.append((i, other))
    return lax.ppermute(block, axis, pairs)


def shape(*dims):
    return jax.ShapeDtypeStruct(dims, f32)


def cost(flops):
    return pl.CostEstimate(flops=flops, bytes_accessed=1_000_000, transcendentals=0)


def per_device(perturbations, base_wind, base_height):
    members, _, rows, cols = perturbations.shape
    n_lat, n_lon = lax.axis_size("lat"), lax.axis_size("lon")
    total_rows, total_cols = rows * n_lat, cols * n_lon
    groups = len(strip_kinds(members))
    planes_c, planes_e = 3 * members, 3 * groups

    own, msg_a, msg_b = pl.pallas_call(
        functools.partial(load_kernel, members),
        out_shape=[shape(members + 1, 3, rows, LANES), shape(3, rows, LANES), shape(3, rows, LANES)],
        in_specs=[HBM] * 3,
        out_specs=[VMEM] * 3,
        scratch_shapes=[pltpu.SemaphoreType.DMA((6,))],
        compiler_params=PARAMS,
        name="load",
    )(*(pltpu.with_memory_space_constraint(x, pltpu.HBM) for x in (perturbations, base_wind, base_height)))
    got_b = swap(msg_b, "lon", n_lon, False, True)
    got_a = swap(msg_a, "lon", n_lon, True, True)

    facts, hist_c = pl.pallas_call(
        functools.partial(centre_kernel, members, total_rows),
        out_shape=[shape(2, FACTS, LANES), shape(2, STEPS, planes_c, TILE, LANES)],
        in_specs=[VMEM],
        out_specs=[VMEM] * 2,
        scratch_shapes=[
            pltpu.VMEM((FRONT + planes_c * PYRAMID, LANES), f32),
            pltpu.VMEM((FRONT + planes_c * PYRAMID, LANES), f32),
            pltpu.VMEM((FRONT + 3 * PYRAMID, LANES), f32),
            pltpu.VMEM((NCOEF * FACTS, LANES), f32),
        ],
        compiler_params=PARAMS,
        cost_estimate=cost(3_000_000),
        name="centre",
    )(own)

    send = shape(3 * members + 9, TILE, LANES)
    send_a, send_b, west, east = pl.pallas_call(
        functools.partial(meet_kernel, members),
        out_shape=[send, send, shape(3, rows, LANES), shape(3, rows, LANES)],
        in_specs=[VMEM] * 3,
        out_specs=[VMEM] * 4,
        compiler_params=PARAMS,
        name="meet",
    )(own, got_a, got_b)
    halo_a = swap(send_a, "lat", n_lat, True, False)
    halo_b = swap(send_b, "lat", n_lat, False, False)

    hist_e, strip_base = pl.pallas_call(
        functools.partial(edges_kernel, members),
        out_shape=[shape(2, STEPS, planes_e, TILE, LANES), shape(KINDS, 3, rows, LANES)],
        in_specs=[VMEM] * 4,
        out_specs=[VMEM] * 2,
        scratch_shapes=[
            pltpu.VMEM((FRONT + planes_e * PYRAMID, LANES), f32),
            pltpu.VMEM((FRONT + planes_e * PYRAMID, LANES), f32),
            pltpu.VMEM((FRONT + 3 * KINDS * PYRAMID, LANES), f32),
            pltpu.VMEM((KINDS * NCOEF * FACTS, LANES), f32),
        ],
        compiler_params=PARAMS,
        cost_estimate=cost(2_000_000),
        name="edges",
    )(own, west, east, facts)

    wedges = [
        pltpu.VMEM((3 * BASE, LANES), f32),
        pltpu.VMEM((3 * KINDS * BASE, LANES), f32),
        pltpu.VMEM((NCOEF * FACTS, LANES), f32),
        pltpu.VMEM((KINDS * NCOEF * FACTS, LANES), f32),
        pltpu.VMEM((TILE * LANES, LANES), f32),
    ] + [pltpu.VMEM((3 * WEDGE, LANES), f32)] * (2 * (members + groups))
    half = shape(members, 3, TILE, LANES)
    fields_a, partial = pl.pallas_call(
        functools.partial(first_side_kernel, members),
        out_shape=[half, shape((members + 1) * TILE, LANES)],
        in_specs=[VMEM] * 6,
        out_specs=[VMEM] * 2,
        scratch_shapes=wedges,
        compiler_params=PARAMS,
        cost_estimate=cost(4_000_000),
        name="side_a",
    )(own, halo_a, facts, hist_c, hist_e, strip_base)
    fields_b, send_gram = pl.pallas_call(
        functools.partial(side_kernel, members, False),
        out_shape=[half, shape(n_lat * n_lon, LANES)],
        in_specs=[VMEM] * 7,
        out_specs=[VMEM] * 2,
        scratch_shapes=wedges,
        compiler_params=PARAMS,
        cost_estimate=cost(4_000_000),
        name="side_b",
    )(own, halo_b, facts, hist_c, hist_e, strip_base, partial)

    got = lax.all_to_all(send_gram, ("lon", "lat"), 0, 0, tiled=True)

    return pl.pallas_call(
        functools.partial(finish_kernel, members, float(3 * total_rows * total_cols)),
        out_shape=[shape(*perturbations.shape), shape(members, members)],
        in_specs=[VMEM] * 3,
        out_specs=[HBM, HBM],
        scratch_shapes=[
            pltpu.VMEM(perturbations.shape, f32),
            pltpu.VMEM((members, members), f32),
            pltpu.SemaphoreType.DMA((members + 1,)),
        ],
        compiler_params=PARAMS,
        name="finish",
    )(fields_a, fields_b, got)


def solution(mesh):
    return jax.shard_map(
        per_device,
        mesh=mesh,
        in_specs=(P(None, None, "lat", "lon"), P(None, "lat", "lon"), P("lat", "lon")),
        out_specs=(P(None, None, "lat", "lon"), P()),
        check_vma=False,
    )
```

time: 120 us -> 34.2 us (0.29)
  waiting for transfers between devices: 26.1 us -> 2.78 us
  blocking collectives: 37.1 us -> 14.4 us
  other arithmetic: 22 us -> 0 us
  starting transfers between devices: 27.2 us -> 7.45 us
  Pallas kernels: 0 us -> 8.63 us
  local copies, waits for them, and re-layouts: 4 us -> 0 us
    psum x1 -> x0, blocking collectives: 37.1 us -> none  [per_device(): gram = lax.psum(local_gram, ('lon', 'lat'))]
    ppermute x12 -> x4, waiting for transfers between devices: 26.1 us -> 2.78 us  [swap(): return lax.ppermute(block, axis, pairs)]
    ppermute x12 -> x4, starting transfers between devices: 27.2 us -> 7.45 us  [swap(): return lax.ppermute(block, axis, pairs)]
    another operation x30 -> x0, other arithmetic: 16.4 us -> none  [the longest x26 13.7 us: advance(): return jnp.stack([new_x, new_y, new_height], axis=-3)]
    all_to_all x0 -> x1, blocking collectives: none -> 14.4 us  [per_device(): got = lax.all_to_all(send_gram, ('lon', 'lat'), 0, 0, tiled=True)]
    pallas_call x0 -> x7, Pallas kernels: none -> 8.63 us  [the longest x1 1.7 us: per_device(): pl.pallas_call(functools.partial(side_kernel, members, False), out_shape=...]
    unnamed x3 -> x0, local copies, waits for them, and re-layouts: 2.55 us -> none
    mul x14 -> x0, other arithmetic: 1.47 us -> none  [the longest x6 0.84 us: per_device(): current * inside_grid(row_start - margin, rows + 2 * margin, total_rows)]
  transfers between devices with their start and end apart: 12 -> 4, of which waited for: 6 -> 2; matrix products, arithmetic and copies ran while one was open for 2% -> 0% of each run, Pallas kernels for 0% -> 12%
where the time goes in v2:
time: 34.2 us; the launch traced here: 33.9 us
  blocking collectives  14.4 us (42%)
  Pallas kernels  8.63 us (25%)
  starting transfers between devices  7.45 us (22%)
  waiting for transfers between devices  2.78 us (8%)
  between operations  0.68 us (2%)
    all_to_all x1, blocking collectives, per_device(): got = lax.all_to_all(send_gram, ('lon', 'lat'), 0, 0, tiled=True)  14.4 us
    ppermute x4, starting transfers between devices, swap(): return lax.ppermute(block, axis, pairs)  7.45 us
    ppermute x4, waiting for transfers between devices, swap(): return lax.ppermute(block, axis, pairs)  2.78 us
    pallas_call x1, Pallas kernels, per_device(): pl.pallas_call(functools.partial(side_kernel, members, False), out_shape=...  1.7 us
    pallas_call x1, Pallas kernels, per_device(): pl.pallas_call(functools.partial(finish_kernel, members, float(3 * total_...  1.69 us
    pallas_call x1, Pallas kernels, per_device(): pl.pallas_call(functools.partial(first_side_kernel, members), out_shape=[...  1.55 us
    pallas_call x1, Pallas kernels, per_device(): pl.pallas_call(functools.partial(edges_kernel, members), out_shape=[shape...  1.27 us
    pallas_call x1, Pallas kernels, per_device(): pl.pallas_call(functools.partial(load_kernel, members), out_shape=[shape(...  1.24 us
  transfers between devices with their start and end apart: 4, of which 2 were waited for; matrix products, arithmetic and copies ran while one was open for 0% of the time, Pallas kernels for 12%

profile of v2, /device:TPU:0, one launch (start us, length us, event | category | flops | bytes accessed | tf_op | source)
XLA Modules:
  0.0 33.9 jit_solution(6573946714417640588)
XLA Ops:
  0.6 1.2 %load.1 = (f32[13,3,16,128]{3,2,1,0:T(8,128)S(1)}, f32[3,16,128]{2,1,0:T(8,128)S(1)}, f32[3,16,128]{2,1,0:T(8,128)S(1)}) custom-call(f32[12,3,16,128]{3,2,1,0:T(8,128)} %pert.1, f32[2,16,128]{2,1,0:T(8,128)} %wind.1, f32[16,128]{1,0:T(8,128)} %height.1), custom_call_target="tpu_custom_call" | custom-call | tf_op jit(solution)/shard_map/load/pallas_call | solution.py:504
  1.9 0.5 %collective-permute-start = (f32[3,16,128]{2,1,0:T(8,128)S(1)}, f32[3,16,128]{2,1,0:T(8,128)S(1)}, u32[]{:S(2)}, u32[]{:S(2)}) collective-permute-start(f32[3,16,128]{2,1,0:T(8,128)S(1)} %get-tuple-element.18), channel_id=1, source_target_pairs={{0,4},{4,0},{8,12},{12,8},{16,20},{20,16},{24,28},{28,24},{1,5},{5... | collective-permute-start | bytes 73736 | tf_op jit(solution)/shard_map/ppermute | solution.py:486
  2.4 4.7 %collective-permute-start.1 = (f32[3,16,128]{2,1,0:T(8,128)S(1)}, f32[3,16,128]{2,1,0:T(8,128)S(1)}, u32[]{:S(2)}, u32[]{:S(2)}) collective-permute-start(f32[3,16,128]{2,1,0:T(8,128)S(1)} %get-tuple-element.19), channel_id=1, source_target_pairs={{0,28},{4,8},{8,4},{12,16},{16,12},{20,24},{24,20},{28,0},{1,29},{... | collective-permute-start | bytes 73736 | tf_op jit(solution)/shard_map/ppermute | solution.py:486
  7.1 0.0 collective-permute-done.got_a
  7.1 1.5 %collective-permute-done.1.got_b = f32[3,16,128]{2,1,0:T(8,128)S(1)} collective-permute-done((f32[3,16,128]{2,1,0:T(8,128)S(1)}, f32[3,16,128]{2,1,0:T(8,128)S(1)}, u32[]{:S(2)}, u32[]{:S(2)}) %collective-permute-start.1) | collective-permute-done | bytes 24608 | tf_op jit(solution)/shard_map/ppermute | solution.py:486
  8.7 1.6 %collective-permute-start.2 = (f32[45,8,128]{2,1,0:T(8,128)S(1)}, f32[45,8,128]{2,1,0:T(8,128)S(1)}, u32[]{:S(2)}, u32[]{:S(2)}) collective-permute-start(f32[45,8,128]{2,1,0:T(8,128)S(1)} %get-tuple-element.20), channel_id=1, source_target_pairs={{0,1},{1,0},{2,3},{3,2},{4,5},{5,4},{6,7},{7,6},{8,9},{9,8},{10,11... | collective-permute-start | bytes 552968 | tf_op jit(solution)/shard_map/ppermute | solution.py:486
  10.2 0.7 %collective-permute-start.3 = (f32[45,8,128]{2,1,0:T(8,128)S(1)}, f32[45,8,128]{2,1,0:T(8,128)S(1)}, u32[]{:S(2)}, u32[]{:S(2)}) collective-permute-start(f32[45,8,128]{2,1,0:T(8,128)S(1)} %get-tuple-element.28), channel_id=1, source_target_pairs={{1,2},{2,1},{5,6},{6,5},{9,10},{10,9},{13,14},{14,13},{17,18},{18,... | collective-permute-start | bytes 552968 | tf_op jit(solution)/shard_map/ppermute | solution.py:486
  10.9 1.1 %centre.1 = (f32[2,40,128]{2,1,0:T(8,128)S(1)}, f32[2,8,36,8,128]{4,3,2,1,0:T(8,128)S(1)}) custom-call(f32[13,3,16,128]{3,2,1,0:T(8,128)S(1)} %get-tuple-element.17.own), custom_call_target="tpu_custom_call" | custom-call | flops 3000000 | bytes 1000000 | tf_op jit(solution)/shard_map/centre/pallas_call | solution.py:516
  12.0 1.3 %edges.1 = (f32[2,8,15,8,128]{4,3,2,1,0:T(8,128)S(1)}, f32[3,3,16,128]{3,2,1,0:T(8,128)S(1)}) custom-call(f32[13,3,16,128]{3,2,1,0:T(8,128)S(1)} %get-tuple-element.17.own, f32[3,16,128]{2,1,0:T(8,128)S(1)} %get-tuple-element.23.west, f32[3,16,128]{2,1,0:T(8,128)S(1)} %get-tuple-element.24.east, f32[2,40,128]{2,1,0:T(8,128)S(1)} %get-tuple-element.21.facts), custom_call_target="tpu_custom_call" | custom-call | flops 2000000 | bytes 1000000 | tf_op jit(solution)/shard_map/edges/pallas_call | solution.py:544
  13.3 1.3 %collective-permute-done.2.halo = f32[45,8,128]{2,1,0:T(8,128)S(1)} collective-permute-done((f32[45,8,128]{2,1,0:T(8,128)S(1)}, f32[45,8,128]{2,1,0:T(8,128)S(1)}, u32[]{:S(2)}, u32[]{:S(2)}) %collective-permute-start.2) | collective-permute-done | bytes 184352 | tf_op jit(solution)/shard_map/ppermute | solution.py:486
  14.6 1.6 %side_a.1 = (f32[12,3,8,128]{3,2,1,0:T(8,128)S(1)}, f32[104,128]{1,0:T(8,128)S(1)}) custom-call(f32[13,3,16,128]{3,2,1,0:T(8,128)S(1)} %get-tuple-element.17.own, f32[45,8,128]{2,1,0:T(8,128)S(1)} %collective-permute-done.2.halo, f32[2,40,128]{2,1,0:T(8,128)S(1)} %get-tuple-element.21.facts, f32[2,8,36,8,128]{4,3,2,1,0:T(8,128)S(1)} %get-tuple-element.22.hist_c, ...), custom_call_target="tpu_custom_call" | custom-call | flops 4000000 | bytes 1000000 | tf_op jit(solution)/shard_map/side_a/pallas_call | solution.py:568
  16.1 0.0 collective-permute-done.3.halo
  16.1 1.7 %side_b.1 = (f32[12,3,8,128]{3,2,1,0:T(8,128)S(1)}, f32[32,128]{1,0:T(8,128)S(1)}) custom-call(f32[13,3,16,128]{3,2,1,0:T(8,128)S(1)} %get-tuple-element.17.own, f32[45,8,128]{2,1,0:T(8,128)S(1)} %collective-permute-done.3.halo, f32[2,40,128]{2,1,0:T(8,128)S(1)} %get-tuple-element.21.facts, f32[2,8,36,8,128]{4,3,2,1,0:T(8,128)S(1)} %get-tuple-element.22.hist_c, ...), custom_call_target="tpu_custom_call" | custom-call | flops 4000000 | bytes 1000000 | tf_op jit(solution)/shard_map/side_b/pallas_call | solution.py:578
  17.8 14.4 %all_to_all.11 = f32[32,1,128]{2,1,0:T(1,128)S(1)} all-to-all(f32[32,1,128]{2,1,0:T(1,128)S(1)} %bitcast.5), channel_id=1, replica_groups=mesh['lon'=8,'lat'=4] {'lon','lat'}, dimensions={0} | all-to-all | bytes 32768 | tf_op jit(solution)/shard_map/all_to_all | solution.py:589
  32.2 1.7 %finish.1 = (f32[12,3,16,128]{3,2,1,0:T(8,128)}, f32[12,12]{1,0:T(8,128)}) custom-call(f32[12,3,8,128]{3,2,1,0:T(8,128)S(1)} %get-tuple-element.27.fields_a, f32[12,3,8,128]{3,2,1,0:T(8,128)S(1)} %get-tuple-element.30.fields_b, f32[32,128]{1,0:T(8,128)S(1)} %bitcast.4), custom_call_target="tpu_custom_call" | custom-call | tf_op jit(solution)/shard_map/finish/pallas_call | solution.py:591
  (1 shorter events, 0.0 us)
Async XLA Ops:
  1.9 5.2 %collective-permute-start = (f32[3,16,128]{2,1,0:T(8,128)S(1)}, f32[3,16,128]{2,1,0:T(8,128)S(1)}, u32[]{:S(2)}, u32[]{:S(2)}) collective-permute-start(f32[3,16,128]{2,1,0:T(8,128)S(1)} %get-tuple-element.18), channel_id=1, source_target_pairs={{0,4},{4,0},{8,12},{12,8},{16,20},{20,16},{24,28},{28,24},{1,5},{5... | collective-permute-start | bytes 73736 | tf_op jit(solution)/shard_map/ppermute | solution.py:486
  2.4 6.2 %collective-permute-start.1 = (f32[3,16,128]{2,1,0:T(8,128)S(1)}, f32[3,16,128]{2,1,0:T(8,128)S(1)}, u32[]{:S(2)}, u32[]{:S(2)}) collective-permute-start(f32[3,16,128]{2,1,0:T(8,128)S(1)} %get-tuple-element.19), channel_id=1, source_target_pairs={{0,28},{4,8},{8,4},{12,16},{16,12},{20,24},{24,20},{28,0},{1,29},{... | collective-permute-start | bytes 73736 | tf_op jit(solution)/shard_map/ppermute | solution.py:486
  8.7 5.9 %collective-permute-start.2 = (f32[45,8,128]{2,1,0:T(8,128)S(1)}, f32[45,8,128]{2,1,0:T(8,128)S(1)}, u32[]{:S(2)}, u32[]{:S(2)}) collective-permute-start(f32[45,8,128]{2,1,0:T(8,128)S(1)} %get-tuple-element.20), channel_id=1, source_target_pairs={{0,1},{1,0},{2,3},{3,2},{4,5},{5,4},{6,7},{7,6},{8,9},{9,8},{10,11... | collective-permute-start | bytes 552968 | tf_op jit(solution)/shard_map/ppermute | solution.py:486
  10.2 5.9 %collective-permute-start.3 = (f32[45,8,128]{2,1,0:T(8,128)S(1)}, f32[45,8,128]{2,1,0:T(8,128)S(1)}, u32[]{:S(2)}, u32[]{:S(2)}) collective-permute-start(f32[45,8,128]{2,1,0:T(8,128)S(1)} %get-tuple-element.28), channel_id=1, source_target_pairs={{1,2},{2,1},{5,6},{6,5},{9,10},{10,9},{13,14},{14,13},{17,18},{18,... | collective-permute-start | bytes 552968 | tf_op jit(solution)/shard_map/ppermute | solution.py:486

commit v3 on v2

--- a/solution.py
+++ b/solution.py
@@ -236,7 +236,8 @@
             msg_b[v, rows, :] = jnp.where(lon_even, to_w, to_e)
 
 
-def centre_kernel(members, total_rows, own, facts, hist, first, second, base, coef):
+def centre_kernel(members, total_rows, own, msg, facts, hist, msg_late, first, second, base, coef):
+    msg_late[...] = msg[...]
     zero = dynamic_zero()
     start = lax.axis_index("lat") * 16 - HALO + 1
     for t in range(FACTS // TILE):
@@ -440,35 +441,37 @@
         total = total + got[r : r + TILE, :]
     packed = jnp.sum(total, axis=0, keepdims=True) / count
     packed = jnp.broadcast_to(packed, (TILE, LANES))
-    rows = []
+    gram = {}
     for i in range(members):
-        b = min(i, members - 1 - i)
-        rows.append(rotate(packed, b - SPREAD * b if i == b else -1 - SPREAD * b))
+        for j in range(i, members):
+            place = pair_place(i, j, members)
+            lane = SPREAD * (place % TILE) + place // TILE
+            gram[i, j] = jnp.broadcast_to(packed[:, lane : lane + 1], (TILE, LANES))
     a_at = pl.multiple_of(jnp.where(is_even("lat"), TILE, 0), TILE)
     places = [a_at, pl.multiple_of(TILE - a_at, TILE)]
     x = [[[ref[m, v] for v in range(3)] for ref in (fields_a, fields_b)] for m in range(members)]
     lanes = lane_ids()
     copies = []
     for k in range(members):
-        spread = [
-            jnp.broadcast_to(rows[k][:, i : i + 1], (TILE, LANES)) if i >= k else None for i in range(members)
-        ]
-        inverse = 1.0 / spread[k]
-        scale = lax.rsqrt(spread[k])
+        scale = lax.rsqrt(gram[k, k])
         for half in range(2):
             for v in range(3):
-                done[k, v, pl.ds(places[half], TILE), :] = x[k][half][v] * scale
+                x[k][half][v] = x[k][half][v] * scale
+                done[k, v, pl.ds(places[half], TILE), :] = x[k][half][v]
         copy = pltpu.make_async_copy(done.at[k], out.at[k], sems.at[k])
         copy.start()
         copies.append(copy)
-        kept = (lanes >= k) & (lanes < members)
-        factor[k : k + 1, :] = jnp.where(kept, rows[k] * scale, 0.0)[0:1, :members]
+        row = jnp.zeros((TILE, LANES), f32)
+        for i in range(k, members):
+            gram[k, i] = gram[k, i] * scale
+            row = jnp.where(lanes == i, gram[k, i], row)
+        factor[k : k + 1, :] = row[0:1, :members]
         for i in range(k + 1, members):
-            times = spread[i] * inverse
-            rows[i] = rows[i] - times * rows[k]
+            for j in range(i, members):
+                gram[i, j] = gram[i, j] - gram[k, i] * gram[k, j]
             for half in range(2):
                 for v in range(3):
-                    x[i][half][v] = x[i][half][v] - times * x[k][half][v]
+                    x[i][half][v] = x[i][half][v] - gram[k, i] * x[k][half][v]
     copy = pltpu.make_async_copy(factor, factor_out, sems.at[members])
     copy.start()
     for copy in copies + [copy]:
@@ -511,13 +514,12 @@
         name="load",
     )(*(pltpu.with_memory_space_constraint(x, pltpu.HBM) for x in (perturbations, base_wind, base_height)))
     got_b = swap(msg_b, "lon", n_lon, False, True)
-    got_a = swap(msg_a, "lon", n_lon, True, True)
-
-    facts, hist_c = pl.pallas_call(
+
+    facts, hist_c, msg_a = pl.pallas_call(
         functools.partial(centre_kernel, members, total_rows),
-        out_shape=[shape(2, FACTS, LANES), shape(2, STEPS, planes_c, TILE, LANES)],
-        in_specs=[VMEM],
-        out_specs=[VMEM] * 2,
+        out_shape=[shape(2, FACTS, LANES), shape(2, STEPS, planes_c, TILE, LANES), shape(3, rows, LANES)],
+        in_specs=[VMEM] * 2,
+        out_specs=[VMEM] * 3,
         scratch_shapes=[
             pltpu.VMEM((FRONT + planes_c * PYRAMID, LANES), f32),
             pltpu.VMEM((FRONT + planes_c * PYRAMID, LANES), f32),
@@ -527,7 +529,8 @@
         compiler_params=PARAMS,
         cost_estimate=cost(3_000_000),
         name="centre",
-    )(own)
+    )(own, msg_a)
+    got_a = swap(msg_a, "lon", n_lon, True, True)
 
     send = shape(3 * members + 9, TILE, LANES)
     send_a, send_b, west, east = pl.pallas_call(

time: 34.2 us -> 33.5 us (0.980)
  waiting for transfers between devices: 2.78 us -> 4.46 us
  blocking collectives: 14.4 us -> 13.3 us
  Pallas kernels: 8.63 us -> 7.99 us
  starting transfers between devices: 7.45 us -> 6.84 us
    ppermute x4, waiting for transfers between devices: 2.78 us -> 4.46 us  [swap(): return lax.ppermute(block, axis, pairs)]
    all_to_all x1, blocking collectives: 14.4 us -> 13.3 us  [per_device(): got = lax.all_to_all(send_gram, ('lon', 'lat'), 0, 0, tiled=True)]
    pallas_call x1, Pallas kernels: 1.69 us -> 1.05 us  [per_device(): pl.pallas_call(functools.partial(finish_kernel, members, float(3 * total_...]
    ppermute x4, starting transfers between devices: 7.45 us -> 6.84 us  [swap(): return lax.ppermute(block, axis, pairs)]
  transfers between devices with their start and end apart: 4 -> 4, of which waited for: 2 -> 3; matrix products, arithmetic and copies ran while one was open for 0% -> 0% of each run, Pallas kernels for 12% -> 12%
where the time goes in v3:
time: 33.5 us; the launch traced here: 33.2 us
  blocking collectives  13.3 us (40%)
  Pallas kernels  7.99 us (24%)
  starting transfers between devices  6.84 us (20%)
  waiting for transfers between devices  4.46 us (13%)
  between operations  0.68 us (2%)
    all_to_all x1, blocking collectives, per_device(): got = lax.all_to_all(send_gram, ('lon', 'lat'), 0, 0, tiled=True)  13.3 us
    ppermute x4, starting transfers between devices, swap(): return lax.ppermute(block, axis, pairs)  6.84 us
    ppermute x4, waiting for transfers between devices, swap(): return lax.ppermute(block, axis, pairs)  4.46 us
    pallas_call x1, Pallas kernels, per_device(): pl.pallas_call(functools.partial(side_kernel, members, False), out_shape=...  1.7 us
    pallas_call x1, Pallas kernels, per_device(): pl.pallas_call(functools.partial(first_side_kernel, members), out_shape=[...  1.55 us
    pallas_call x1, Pallas kernels, per_device(): pl.pallas_call(functools.partial(edges_kernel, members), out_shape=[shape...  1.27 us
    pallas_call x1, Pallas kernels, per_device(): pl.pallas_call(functools.partial(load_kernel, members), out_shape=[shape(...  1.24 us
    pallas_call x1, Pallas kernels, per_device(): pl.pallas_call(functools.partial(centre_kernel, members, total_rows), out...  1.14 us
  transfers between devices with their start and end apart: 4, of which 3 were waited for; matrix products, arithmetic and copies ran while one was open for 0% of the time, Pallas kernels for 12%

profile of v3, /device:TPU:0, one launch (start us, length us, event | category | flops | bytes accessed | tf_op | source)
XLA Modules:
  0.0 33.2 jit_solution(14348053315883439386)
XLA Ops:
  0.6 1.2 %load.1 = (f32[13,3,16,128]{3,2,1,0:T(8,128)S(1)}, f32[3,16,128]{2,1,0:T(8,128)S(1)}, f32[3,16,128]{2,1,0:T(8,128)S(1)}) custom-call(f32[12,3,16,128]{3,2,1,0:T(8,128)} %pert.1, f32[2,16,128]{2,1,0:T(8,128)} %wind.1, f32[16,128]{1,0:T(8,128)} %height.1), custom_call_target="tpu_custom_call" | custom-call | tf_op jit(solution)/shard_map/load/pallas_call | solution.py:507
  1.9 4.6 %collective-permute-start.1 = (f32[3,16,128]{2,1,0:T(8,128)S(1)}, f32[3,16,128]{2,1,0:T(8,128)S(1)}, u32[]{:S(2)}, u32[]{:S(2)}) collective-permute-start(f32[3,16,128]{2,1,0:T(8,128)S(1)} %get-tuple-element.21), channel_id=1, source_target_pairs={{0,28},{4,8},{8,4},{12,16},{16,12},{20,24},{24,20},{28,0},{1,29},{... | collective-permute-start | bytes 73736 | tf_op jit(solution)/shard_map/ppermute | solution.py:489
  6.4 1.1 %centre.1 = (f32[2,40,128]{2,1,0:T(8,128)S(1)}, f32[2,8,36,8,128]{4,3,2,1,0:T(8,128)S(1)}, f32[3,16,128]{2,1,0:T(8,128)S(1)}) custom-call(f32[13,3,16,128]{3,2,1,0:T(8,128)S(1)} %get-tuple-element.18.own, f32[3,16,128]{2,1,0:T(8,128)S(1)} %get-tuple-element.19.msg), custom_call_target="tpu_custom_call" | custom-call | flops 3000000 | bytes 1000000 | tf_op jit(solution)/shard_map/centre/pallas_call | solution.py:518
  7.6 0.1 collective-permute-start
  7.7 0.4 %collective-permute-done.1.got_b = f32[3,16,128]{2,1,0:T(8,128)S(1)} collective-permute-done((f32[3,16,128]{2,1,0:T(8,128)S(1)}, f32[3,16,128]{2,1,0:T(8,128)S(1)}, u32[]{:S(2)}, u32[]{:S(2)}) %collective-permute-start.1) | collective-permute-done | bytes 24608 | tf_op jit(solution)/shard_map/ppermute | solution.py:489
  8.1 0.8 %collective-permute-done.got_a = f32[3,16,128]{2,1,0:T(8,128)S(1)} collective-permute-done((f32[3,16,128]{2,1,0:T(8,128)S(1)}, f32[3,16,128]{2,1,0:T(8,128)S(1)}, u32[]{:S(2)}, u32[]{:S(2)}) %collective-permute-start) | collective-permute-done | bytes 24608 | tf_op jit(solution)/shard_map/ppermute | solution.py:489
  8.9 1.6 %collective-permute-start.2 = (f32[45,8,128]{2,1,0:T(8,128)S(1)}, f32[45,8,128]{2,1,0:T(8,128)S(1)}, u32[]{:S(2)}, u32[]{:S(2)}) collective-permute-start(f32[45,8,128]{2,1,0:T(8,128)S(1)} %get-tuple-element.22), channel_id=1, source_target_pairs={{0,1},{1,0},{2,3},{3,2},{4,5},{5,4},{6,7},{7,6},{8,9},{9,8},{10,11... | collective-permute-start | bytes 552968 | tf_op jit(solution)/shard_map/ppermute | solution.py:489
  10.4 0.7 %collective-permute-start.3 = (f32[45,8,128]{2,1,0:T(8,128)S(1)}, f32[45,8,128]{2,1,0:T(8,128)S(1)}, u32[]{:S(2)}, u32[]{:S(2)}) collective-permute-start(f32[45,8,128]{2,1,0:T(8,128)S(1)} %get-tuple-element.30), channel_id=1, source_target_pairs={{1,2},{2,1},{5,6},{6,5},{9,10},{10,9},{13,14},{14,13},{17,18},{18,... | collective-permute-start | bytes 552968 | tf_op jit(solution)/shard_map/ppermute | solution.py:489
  11.1 1.3 %edges.1 = (f32[2,8,15,8,128]{4,3,2,1,0:T(8,128)S(1)}, f32[3,3,16,128]{3,2,1,0:T(8,128)S(1)}) custom-call(f32[13,3,16,128]{3,2,1,0:T(8,128)S(1)} %get-tuple-element.18.own, f32[3,16,128]{2,1,0:T(8,128)S(1)} %get-tuple-element.25.west, f32[3,16,128]{2,1,0:T(8,128)S(1)} %get-tuple-element.26.east, f32[2,40,128]{2,1,0:T(8,128)S(1)} %get-tuple-element.23.facts), custom_call_target="tpu_custom_call" | custom-call | flops 2000000 | bytes 1000000 | tf_op jit(solution)/shard_map/edges/pallas_call | solution.py:547
  12.4 3.3 %collective-permute-done.2.halo = f32[45,8,128]{2,1,0:T(8,128)S(1)} collective-permute-done((f32[45,8,128]{2,1,0:T(8,128)S(1)}, f32[45,8,128]{2,1,0:T(8,128)S(1)}, u32[]{:S(2)}, u32[]{:S(2)}) %collective-permute-start.2) | collective-permute-done | bytes 184352 | tf_op jit(solution)/shard_map/ppermute | solution.py:489
  15.6 1.6 %side_a.1 = (f32[12,3,8,128]{3,2,1,0:T(8,128)S(1)}, f32[104,128]{1,0:T(8,128)S(1)}) custom-call(f32[13,3,16,128]{3,2,1,0:T(8,128)S(1)} %get-tuple-element.18.own, f32[45,8,128]{2,1,0:T(8,128)S(1)} %collective-permute-done.2.halo, f32[2,40,128]{2,1,0:T(8,128)S(1)} %get-tuple-element.23.facts, f32[2,8,36,8,128]{4,3,2,1,0:T(8,128)S(1)} %get-tuple-element.24.hist_c, ...), custom_call_target="tpu_custom_call" | custom-call | flops 4000000 | bytes 1000000 | tf_op jit(solution)/shard_map/side_a/pallas_call | solution.py:571
  17.2 0.0 collective-permute-done.3.halo
  17.2 1.7 %side_b.1 = (f32[12,3,8,128]{3,2,1,0:T(8,128)S(1)}, f32[32,128]{1,0:T(8,128)S(1)}) custom-call(f32[13,3,16,128]{3,2,1,0:T(8,128)S(1)} %get-tuple-element.18.own, f32[45,8,128]{2,1,0:T(8,128)S(1)} %collective-permute-done.3.halo, f32[2,40,128]{2,1,0:T(8,128)S(1)} %get-tuple-element.23.facts, f32[2,8,36,8,128]{4,3,2,1,0:T(8,128)S(1)} %get-tuple-element.24.hist_c, ...), custom_call_target="tpu_custom_call" | custom-call | flops 4000000 | bytes 1000000 | tf_op jit(solution)/shard_map/side_b/pallas_call | solution.py:581
  18.9 13.3 %all_to_all.11 = f32[32,1,128]{2,1,0:T(1,128)S(1)} all-to-all(f32[32,1,128]{2,1,0:T(1,128)S(1)} %bitcast.5), channel_id=1, replica_groups=mesh['lon'=8,'lat'=4] {'lon','lat'}, dimensions={0} | all-to-all | bytes 32768 | tf_op jit(solution)/shard_map/all_to_all | solution.py:592
  32.2 1.1 %finish.1 = (f32[12,3,16,128]{3,2,1,0:T(8,128)}, f32[12,12]{1,0:T(8,128)}) custom-call(f32[12,3,8,128]{3,2,1,0:T(8,128)S(1)} %get-tuple-element.29.fields_a, f32[12,3,8,128]{3,2,1,0:T(8,128)S(1)} %get-tuple-element.32.fields_b, f32[32,128]{1,0:T(8,128)S(1)} %bitcast.4), custom_call_target="tpu_custom_call" | custom-call | tf_op jit(solution)/shard_map/finish/pallas_call | solution.py:594
  (1 shorter events, 0.0 us)
Async XLA Ops:
  1.9 6.2 %collective-permute-start.1 = (f32[3,16,128]{2,1,0:T(8,128)S(1)}, f32[3,16,128]{2,1,0:T(8,128)S(1)}, u32[]{:S(2)}, u32[]{:S(2)}) collective-permute-start(f32[3,16,128]{2,1,0:T(8,128)S(1)} %get-tuple-element.21), channel_id=1, source_target_pairs={{0,28},{4,8},{8,4},{12,16},{16,12},{20,24},{24,20},{28,0},{1,29},{... | collective-permute-start | bytes 73736 | tf_op jit(solution)/shard_map/ppermute | solution.py:489
  7.6 1.3 %collective-permute-start = (f32[3,16,128]{2,1,0:T(8,128)S(1)}, f32[3,16,128]{2,1,0:T(8,128)S(1)}, u32[]{:S(2)}, u32[]{:S(2)}) collective-permute-start(f32[3,16,128]{2,1,0:T(8,128)S(1)} %get-tuple-element.20), channel_id=1, source_target_pairs={{0,4},{4,0},{8,12},{12,8},{16,20},{20,16},{24,28},{28,24},{1,5},{5... | collective-permute-start | bytes 73736 | tf_op jit(solution)/shard_map/ppermute | solution.py:489
  8.9 6.8 %collective-permute-start.2 = (f32[45,8,128]{2,1,0:T(8,128)S(1)}, f32[45,8,128]{2,1,0:T(8,128)S(1)}, u32[]{:S(2)}, u32[]{:S(2)}) collective-permute-start(f32[45,8,128]{2,1,0:T(8,128)S(1)} %get-tuple-element.22), channel_id=1, source_target_pairs={{0,1},{1,0},{2,3},{3,2},{4,5},{5,4},{6,7},{7,6},{8,9},{9,8},{10,11... | collective-permute-start | bytes 552968 | tf_op jit(solution)/shard_map/ppermute | solution.py:489
  10.4 6.8 %collective-permute-start.3 = (f32[45,8,128]{2,1,0:T(8,128)S(1)}, f32[45,8,128]{2,1,0:T(8,128)S(1)}, u32[]{:S(2)}, u32[]{:S(2)}) collective-permute-start(f32[45,8,128]{2,1,0:T(8,128)S(1)} %get-tuple-element.30), channel_id=1, source_target_pairs={{1,2},{2,1},{5,6},{6,5},{9,10},{10,9},{13,14},{14,13},{17,18},{18,... | collective-permute-start | bytes 552968 | tf_op jit(solution)/shard_map/ppermute | solution.py:489

commit v4 on v3

--- a/solution.py
+++ b/solution.py
@@ -236,8 +236,7 @@
             msg_b[v, rows, :] = jnp.where(lon_even, to_w, to_e)
 
 
-def centre_kernel(members, total_rows, own, msg, facts, hist, msg_late, first, second, base, coef):
-    msg_late[...] = msg[...]
+def centre_kernel(members, total_rows, own, facts, hist, first, second, base, coef):
     zero = dynamic_zero()
     start = lax.axis_index("lat") * 16 - HALO + 1
     for t in range(FACTS // TILE):
@@ -261,7 +260,7 @@
     pyramid([first, second], zero, [(coef, zero, list(range(members)))], hist)
 
 
-def meet_kernel(members, own, got_a, got_b, send_a, send_b, west, east):
+def meet_kernel(members, own, got_b, got_a, facts, send_a, send_b, west, east):
     lat_even, lon_even = is_even("lat"), is_even("lon")
     low = pl.multiple_of(jnp.where(lat_even, TILE, 0), TILE)
     for send, at in ((send_a, low), (send_b, TILE - low)):
@@ -514,12 +513,13 @@
         name="load",
     )(*(pltpu.with_memory_space_constraint(x, pltpu.HBM) for x in (perturbations, base_wind, base_height)))
     got_b = swap(msg_b, "lon", n_lon, False, True)
-
-    facts, hist_c, msg_a = pl.pallas_call(
+    got_a = swap(msg_a, "lon", n_lon, True, True)
+
+    facts, hist_c = pl.pallas_call(
         functools.partial(centre_kernel, members, total_rows),
-        out_shape=[shape(2, FACTS, LANES), shape(2, STEPS, planes_c, TILE, LANES), shape(3, rows, LANES)],
-        in_specs=[VMEM] * 2,
-        out_specs=[VMEM] * 3,
+        out_shape=[shape(2, FACTS, LANES), shape(2, STEPS, planes_c, TILE, LANES)],
+        in_specs=[VMEM],
+        out_specs=[VMEM] * 2,
         scratch_shapes=[
             pltpu.VMEM((FRONT + planes_c * PYRAMID, LANES), f32),
             pltpu.VMEM((FRONT + planes_c * PYRAMID, LANES), f32),
@@ -529,18 +529,17 @@
         compiler_params=PARAMS,
         cost_estimate=cost(3_000_000),
         name="centre",
-    )(own, msg_a)
-    got_a = swap(msg_a, "lon", n_lon, True, True)
+    )(own)
 
     send = shape(3 * members + 9, TILE, LANES)
     send_a, send_b, west, east = pl.pallas_call(
         functools.partial(meet_kernel, members),
         out_shape=[send, send, shape(3, rows, LANES), shape(3, rows, LANES)],
-        in_specs=[VMEM] * 3,
+        in_specs=[VMEM] * 4,
         out_specs=[VMEM] * 4,
         compiler_params=PARAMS,
         name="meet",
-    )(own, got_a, got_b)
+    )(own, got_b, got_a, facts)
     halo_a = swap(send_a, "lat", n_lat, True, False)
     halo_b = swap(send_b, "lat", n_lat, False, False)
 

time: 33.5 us -> 33.5 us (level)
  waiting for transfers between devices: 4.46 us -> 3.26 us
  blocking collectives: 13.3 us -> 14.1 us
    ppermute x4, waiting for transfers between devices: 4.46 us -> 3.26 us  [swap(): return lax.ppermute(block, axis, pairs)]
    all_to_all x1, blocking collectives: 13.3 us -> 14.1 us  [per_device(): got = lax.all_to_all(send_gram, ('lon', 'lat'), 0, 0, tiled=True)]
  transfers between devices with their start and end apart: 4 -> 4, of which waited for: 3 -> 2; matrix products, arithmetic and copies ran while one was open for 0% -> 0% of each run, Pallas kernels for 12% -> 12%
where the time goes in v4:
time: 33.5 us; the launch traced here: 33.2 us
  blocking collectives  14.1 us (42%)
  Pallas kernels  7.99 us (24%)
  starting transfers between devices  7.16 us (21%)
  waiting for transfers between devices  3.26 us (10%)
  between operations  0.68 us (2%)
    all_to_all x1, blocking collectives, per_device(): got = lax.all_to_all(send_gram, ('lon', 'lat'), 0, 0, tiled=True)  14.1 us
    ppermute x4, starting transfers between devices, swap(): return lax.ppermute(block, axis, pairs)  7.16 us
    ppermute x4, waiting for transfers between devices, swap(): return lax.ppermute(block, axis, pairs)  3.26 us
    pallas_call x1, Pallas kernels, per_device(): pl.pallas_call(functools.partial(side_kernel, members, False), out_shape=...  1.7 us
    pallas_call x1, Pallas kernels, per_device(): pl.pallas_call(functools.partial(first_side_kernel, members), out_shape=[...  1.55 us
    pallas_call x1, Pallas kernels, per_device(): pl.pallas_call(functools.partial(edges_kernel, members), out_shape=[shape...  1.27 us
    pallas_call x1, Pallas kernels, per_device(): pl.pallas_call(functools.partial(load_kernel, members), out_shape=[shape(...  1.24 us
    pallas_call x1, Pallas kernels, per_device(): pl.pallas_call(functools.partial(centre_kernel, members, total_rows), out...  1.14 us
  transfers between devices with their start and end apart: 4, of which 2 were waited for; matrix products, arithmetic and copies ran while one was open for 0% of the time, Pallas kernels for 12%

profile of v4, /device:TPU:0, one launch (start us, length us, event | category | flops | bytes accessed | tf_op | source)
XLA Modules:
  0.0 33.2 jit_solution(4243197571138761637)
XLA Ops:
  0.6 1.2 %load.1 = (f32[13,3,16,128]{3,2,1,0:T(8,128)S(1)}, f32[3,16,128]{2,1,0:T(8,128)S(1)}, f32[3,16,128]{2,1,0:T(8,128)S(1)}) custom-call(f32[12,3,16,128]{3,2,1,0:T(8,128)} %pert.1, f32[2,16,128]{2,1,0:T(8,128)} %wind.1, f32[16,128]{1,0:T(8,128)} %height.1), custom_call_target="tpu_custom_call" | custom-call | tf_op jit(solution)/shard_map/load/pallas_call | solution.py:506
  1.9 4.6 %collective-permute-start = (f32[3,16,128]{2,1,0:T(8,128)S(1)}, f32[3,16,128]{2,1,0:T(8,128)S(1)}, u32[]{:S(2)}, u32[]{:S(2)}) collective-permute-start(f32[3,16,128]{2,1,0:T(8,128)S(1)} %get-tuple-element.18), channel_id=1, source_target_pairs={{0,28},{4,8},{8,4},{12,16},{16,12},{20,24},{24,20},{28,0},{1,29},{... | collective-permute-start | bytes 73736 | tf_op jit(solution)/shard_map/ppermute | solution.py:488
  6.4 0.0 collective-permute-start.1
  6.4 1.1 %centre.1 = (f32[2,40,128]{2,1,0:T(8,128)S(1)}, f32[2,8,36,8,128]{4,3,2,1,0:T(8,128)S(1)}) custom-call(f32[13,3,16,128]{3,2,1,0:T(8,128)S(1)} %get-tuple-element.17.own), custom_call_target="tpu_custom_call" | custom-call | flops 3000000 | bytes 1000000 | tf_op jit(solution)/shard_map/centre/pallas_call | solution.py:518
  7.6 0.5 %collective-permute-done.got_b = f32[3,16,128]{2,1,0:T(8,128)S(1)} collective-permute-done((f32[3,16,128]{2,1,0:T(8,128)S(1)}, f32[3,16,128]{2,1,0:T(8,128)S(1)}, u32[]{:S(2)}, u32[]{:S(2)}) %collective-permute-start) | collective-permute-done | bytes 24608 | tf_op jit(solution)/shard_map/ppermute | solution.py:488
  8.1 0.0 collective-permute-done.1.got_a
  8.1 1.9 %collective-permute-start.2 = (f32[45,8,128]{2,1,0:T(8,128)S(1)}, f32[45,8,128]{2,1,0:T(8,128)S(1)}, u32[]{:S(2)}, u32[]{:S(2)}) collective-permute-start(f32[45,8,128]{2,1,0:T(8,128)S(1)} %get-tuple-element.21), channel_id=1, source_target_pairs={{0,1},{1,0},{2,3},{3,2},{4,5},{5,4},{6,7},{7,6},{8,9},{9,8},{10,11... | collective-permute-start | bytes 552968 | tf_op jit(solution)/shard_map/ppermute | solution.py:488
  10.0 0.7 %collective-permute-start.3 = (f32[45,8,128]{2,1,0:T(8,128)S(1)}, f32[45,8,128]{2,1,0:T(8,128)S(1)}, u32[]{:S(2)}, u32[]{:S(2)}) collective-permute-start(f32[45,8,128]{2,1,0:T(8,128)S(1)} %get-tuple-element.28), channel_id=1, source_target_pairs={{1,2},{2,1},{5,6},{6,5},{9,10},{10,9},{13,14},{14,13},{17,18},{18,... | collective-permute-start | bytes 552968 | tf_op jit(solution)/shard_map/ppermute | solution.py:488
  10.7 1.3 %edges.1 = (f32[2,8,15,8,128]{4,3,2,1,0:T(8,128)S(1)}, f32[3,3,16,128]{3,2,1,0:T(8,128)S(1)}) custom-call(f32[13,3,16,128]{3,2,1,0:T(8,128)S(1)} %get-tuple-element.17.own, f32[3,16,128]{2,1,0:T(8,128)S(1)} %get-tuple-element.23.west, f32[3,16,128]{2,1,0:T(8,128)S(1)} %get-tuple-element.24.east, f32[2,40,128]{2,1,0:T(8,128)S(1)} %get-tuple-element.20.facts), custom_call_target="tpu_custom_call" | custom-call | flops 2000000 | bytes 1000000 | tf_op jit(solution)/shard_map/edges/pallas_call | solution.py:546
  12.0 2.8 %collective-permute-done.2.halo = f32[45,8,128]{2,1,0:T(8,128)S(1)} collective-permute-done((f32[45,8,128]{2,1,0:T(8,128)S(1)}, f32[45,8,128]{2,1,0:T(8,128)S(1)}, u32[]{:S(2)}, u32[]{:S(2)}) %collective-permute-start.2) | collective-permute-done | bytes 184352 | tf_op jit(solution)/shard_map/ppermute | solution.py:488
  14.8 1.6 %side_a.1 = (f32[12,3,8,128]{3,2,1,0:T(8,128)S(1)}, f32[104,128]{1,0:T(8,128)S(1)}) custom-call(f32[13,3,16,128]{3,2,1,0:T(8,128)S(1)} %get-tuple-element.17.own, f32[45,8,128]{2,1,0:T(8,128)S(1)} %collective-permute-done.2.halo, f32[2,40,128]{2,1,0:T(8,128)S(1)} %get-tuple-element.20.facts, f32[2,8,36,8,128]{4,3,2,1,0:T(8,128)S(1)} %get-tuple-element.22.hist_c, ...), custom_call_target="tpu_custom_call" | custom-call | flops 4000000 | bytes 1000000 | tf_op jit(solution)/shard_map/side_a/pallas_call | solution.py:570
  16.3 0.0 collective-permute-done.3.halo
  16.3 1.7 %side_b.1 = (f32[12,3,8,128]{3,2,1,0:T(8,128)S(1)}, f32[32,128]{1,0:T(8,128)S(1)}) custom-call(f32[13,3,16,128]{3,2,1,0:T(8,128)S(1)} %get-tuple-element.17.own, f32[45,8,128]{2,1,0:T(8,128)S(1)} %collective-permute-done.3.halo, f32[2,40,128]{2,1,0:T(8,128)S(1)} %get-tuple-element.20.facts, f32[2,8,36,8,128]{4,3,2,1,0:T(8,128)S(1)} %get-tuple-element.22.hist_c, ...), custom_call_target="tpu_custom_call" | custom-call | flops 4000000 | bytes 1000000 | tf_op jit(solution)/shard_map/side_b/pallas_call | solution.py:580
  18.0 14.1 %all_to_all.11 = f32[32,1,128]{2,1,0:T(1,128)S(1)} all-to-all(f32[32,1,128]{2,1,0:T(1,128)S(1)} %bitcast.5), channel_id=1, replica_groups=mesh['lon'=8,'lat'=4] {'lon','lat'}, dimensions={0} | all-to-all | bytes 32768 | tf_op jit(solution)/shard_map/all_to_all | solution.py:591
  32.2 1.1 %finish.1 = (f32[12,3,16,128]{3,2,1,0:T(8,128)}, f32[12,12]{1,0:T(8,128)}) custom-call(f32[12,3,8,128]{3,2,1,0:T(8,128)S(1)} %get-tuple-element.27.fields_a, f32[12,3,8,128]{3,2,1,0:T(8,128)S(1)} %get-tuple-element.30.fields_b, f32[32,128]{1,0:T(8,128)S(1)} %bitcast.4), custom_call_target="tpu_custom_call" | custom-call | tf_op jit(solution)/shard_map/finish/pallas_call | solution.py:593
  (1 shorter events, 0.0 us)
Async XLA Ops:
  1.9 6.2 %collective-permute-start = (f32[3,16,128]{2,1,0:T(8,128)S(1)}, f32[3,16,128]{2,1,0:T(8,128)S(1)}, u32[]{:S(2)}, u32[]{:S(2)}) collective-permute-start(f32[3,16,128]{2,1,0:T(8,128)S(1)} %get-tuple-element.18), channel_id=1, source_target_pairs={{0,28},{4,8},{8,4},{12,16},{16,12},{20,24},{24,20},{28,0},{1,29},{... | collective-permute-start | bytes 73736 | tf_op jit(solution)/shard_map/ppermute | solution.py:488
  6.4 1.6 %collective-permute-start.1 = (f32[3,16,128]{2,1,0:T(8,128)S(1)}, f32[3,16,128]{2,1,0:T(8,128)S(1)}, u32[]{:S(2)}, u32[]{:S(2)}) collective-permute-start(f32[3,16,128]{2,1,0:T(8,128)S(1)} %get-tuple-element.19), channel_id=1, source_target_pairs={{0,4},{4,0},{8,12},{12,8},{16,20},{20,16},{24,28},{28,24},{1,5},{5... | collective-permute-start | bytes 73736 | tf_op jit(solution)/shard_map/ppermute | solution.py:488
  8.1 6.7 %collective-permute-start.2 = (f32[45,8,128]{2,1,0:T(8,128)S(1)}, f32[45,8,128]{2,1,0:T(8,128)S(1)}, u32[]{:S(2)}, u32[]{:S(2)}) collective-permute-start(f32[45,8,128]{2,1,0:T(8,128)S(1)} %get-tuple-element.21), channel_id=1, source_target_pairs={{0,1},{1,0},{2,3},{3,2},{4,5},{5,4},{6,7},{7,6},{8,9},{9,8},{10,11... | collective-permute-start | bytes 552968 | tf_op jit(solution)/shard_map/ppermute | solution.py:488
  10.0 6.3 %collective-permute-start.3 = (f32[45,8,128]{2,1,0:T(8,128)S(1)}, f32[45,8,128]{2,1,0:T(8,128)S(1)}, u32[]{:S(2)}, u32[]{:S(2)}) collective-permute-start(f32[45,8,128]{2,1,0:T(8,128)S(1)} %get-tuple-element.28), channel_id=1, source_target_pairs={{1,2},{2,1},{5,6},{6,5},{9,10},{10,9},{13,14},{14,13},{17,18},{18,... | collective-permute-start | bytes 552968 | tf_op jit(solution)/shard_map/ppermute | solution.py:488

commit v5 on v4

--- a/solution.py
+++ b/solution.py
@@ -18,6 +18,7 @@
 MIX = 2 * STRIP + HALO
 KINDS = 3
 NCOEF = 18
+SPARE = 3
 
 advect_rate = 0.1
 turn_rate = 0.5
@@ -41,6 +42,16 @@
 
 def dynamic_zero():
     return jnp.minimum(lax.axis_index("lat"), 0)
+
+
+def is_inner():
+    lat = lax.axis_index("lat")
+    return jnp.where((lat > 0) & (lat < lax.axis_size("lat") - 1), 1, 0)
+
+
+def is_north(last):
+    toward_a = 1 - is_inner() if last else is_inner()
+    return lax.rem(toward_a + lax.axis_index("lat"), 2) == 0
 
 
 def is_even(axis):
@@ -150,53 +161,59 @@
 
 
 def own_strips(rows_of, members):
-    vectors = []
-    for q in range(-(-members // SLOTS)):
+    wests, easts = [], []
+    for q in range(members // SLOTS):
         west = east = None
-        for s in range(min(SLOTS, members - SLOTS * q)):
+        for s in range(SLOTS):
             moved = rotate(rows_of(SLOTS * q + s), STRIP * s + HALO)
             west = moved if s == 0 else jnp.where(slot_range(s, 0), moved, west)
             east = moved if s == 0 else jnp.where(slot_range(s, HALO), moved, east)
-        vectors.append((west, east))
-    return vectors
-
-
-def base_own_strips(rows):
-    west = east = None
+        wests.append(west)
+        easts.append(east)
+    left = members % SLOTS
+    mixed = None
+    for s in range(2 * left):
+        moved = rotate(rows_of(members - left + s % left), STRIP * s + (HALO if s < left else 2 * HALO))
+        mixed = moved if s == 0 else jnp.where(slot_range(s, 0), moved, mixed)
+    return wests + easts + [mixed]
+
+
+def fill_strips(vectors, west_halo, east_halo, members):
+    place = in_strip()
+    full, left = members // SLOTS, members % SLOTS
+    filled = []
+    for q in range(full):
+        filled.append(jnp.where(place < HALO, rotate(west_halo, -HALO * q), vectors[q]))
+    inner = (place >= HALO) & (place < 2 * HALO)
+    for q in range(full):
+        filled.append(jnp.where(inner, rotate(east_halo, -HALO * q), vectors[full + q]))
+    lanes = lane_ids()
+    mixed = jnp.where((place < HALO) & (lanes < left * STRIP), rotate(west_halo, -HALO * full), vectors[-1])
+    outer = (place >= 2 * HALO) & (lanes >= left * STRIP)
+    return filled + [jnp.where(outer, rotate(east_halo, MIX - HALO * full), mixed)]
+
+
+def base_strips(rows, west_halo, east_halo, members):
+    q, left = members // SLOTS, members % SLOTS
+    place = in_strip()
+    lanes = lane_ids()
+    west = east = mixed = None
     for s in range(SLOTS):
         moved = rotate(rows, STRIP * s + HALO)
         west = moved if s == 0 else jnp.where(slot_range(s, 0), moved, west)
         east = moved if s == 0 else jnp.where(slot_range(s, HALO), moved, east)
-    return west, east
-
-
-def mix(west, east):
-    return jnp.where(lane_ids() < 2 * STRIP, west, rotate(east, MIX))
-
-
-def fill_strips(vectors, west_halo, east_halo):
-    place = in_strip()
-    wests, easts = [], []
-    for q, (west, east) in enumerate(vectors):
-        wests.append(jnp.where(place < HALO, rotate(west_halo, -HALO * q), west))
-        here = (place >= HALO) & (place < 2 * HALO)
-        easts.append(jnp.where(here, rotate(east_halo, -HALO * q), east))
-    return wests[:-1] + easts[:-1] + [mix(wests[-1], easts[-1])]
-
-
-def base_strips(rows, west_halo, east_halo, members):
-    q, first = members // SLOTS, members % SLOTS
-    place = in_strip()
-    west, east = base_own_strips(rows)
-
-    def everywhere(halo, edge):
-        near = rotate(halo, -HALO * q)
-        return jnp.where(lane_ids() < STRIP * first + edge, rotate(near, -STRIP * first), near)
-
-    west = jnp.where(place < HALO, everywhere(west_halo, 0), west)
-    here = (place >= HALO) & (place < 2 * HALO)
-    east = jnp.where(here, everywhere(east_halo, HALO), east)
-    return west, east, mix(west, east)
+        if s < 2 * left:
+            over = moved if s < left else rotate(rows, STRIP * s + 2 * HALO)
+            mixed = over if s == 0 else jnp.where(slot_range(s, 0), over, mixed)
+    near = [rotate(halo, -HALO * q) for halo in (west_halo, east_halo)]
+    far = [rotate(halo, -HALO * q - STRIP * left) for halo in (west_halo, east_halo)]
+    low = lanes < left * STRIP
+    west = jnp.where(place < HALO, jnp.where(low, far[0], near[0]), west)
+    inner = (place >= HALO) & (place < 2 * HALO)
+    east = jnp.where(inner, jnp.where(lanes < left * STRIP + HALO, far[1], near[1]), east)
+    mixed = jnp.where((place < HALO) & low, far[0], mixed)
+    outer = (place >= 2 * HALO) & (lanes >= left * STRIP)
+    return west, east, jnp.where(outer, rotate(east_halo, MIX - HALO * q - STRIP * left), mixed)
 
 
 def strip_kinds(members):
@@ -204,7 +221,7 @@
     return [0] * full + [1] * full + [2]
 
 
-def load_kernel(members, pert, wind, height, own, msg_a, msg_b, sems):
+def load_kernel(members, pert, wind, height, own, main_a, msg_a, msg_b, sems):
     chunk = members // 4
     copies = [
         pltpu.make_async_copy(wind, own.at[members, pl.ds(0, 2)], sems.at[0]),
@@ -217,6 +234,12 @@
         copy.start()
     for copy in copies:
         copy.wait()
+    low = pl.multiple_of(jnp.where(is_even("lat"), TILE, 0), TILE)
+    for m in range(SPARE):
+        main_a[members + 1 + m] = jnp.zeros((3, TILE, LANES), f32)
+    for m in range(members + 1):
+        for v in range(3):
+            main_a[m, v] = own[m, v, pl.ds(low, TILE), :]
     lon_even = is_even("lon")
     lanes = lane_ids()
     for v in range(3):
@@ -260,23 +283,21 @@
     pyramid([first, second], zero, [(coef, zero, list(range(members)))], hist)
 
 
-def meet_kernel(members, own, got_b, got_a, facts, send_a, send_b, west, east):
-    lat_even, lon_even = is_even("lat"), is_even("lon")
-    low = pl.multiple_of(jnp.where(lat_even, TILE, 0), TILE)
-    for send, at in ((send_a, low), (send_b, TILE - low)):
-        at = pl.multiple_of(at, TILE)
-        for m in range(members + 1):
-            for v in range(3):
-                send[3 * m + v] = own[m, v, pl.ds(at, TILE), :]
-        for v in range(3):
-            a, b = got_a[v, pl.ds(at, TILE), :], got_b[v, pl.ds(at, TILE), :]
-            send[3 * members + 3 + v] = jnp.where(lon_even, b, a)
-            send[3 * members + 6 + v] = jnp.where(lon_even, a, b)
+def meet_kernel(members, own, got_b, got_a, send_b, west, east, corners):
+    lon_even = is_even("lon")
+    low = pl.multiple_of(jnp.where(is_even("lat"), 0, TILE), TILE)
     for v in range(3):
         for t in range(2):
             rows = slice(TILE * t, TILE * t + TILE)
             west[v, rows, :] = jnp.where(lon_even, got_b[v, rows, :], got_a[v, rows, :])
             east[v, rows, :] = jnp.where(lon_even, got_a[v, rows, :], got_b[v, rows, :])
+    for m in range(members + 1):
+        for v in range(3):
+            send_b[m, v] = own[m, v, pl.ds(low, TILE), :]
+    for v in range(3):
+        for side, halo in enumerate((west, east)):
+            send_b[members + 1 + side, v] = halo[v, pl.ds(low, TILE), :]
+            corners[side, v] = halo[v, pl.ds(pl.multiple_of(TILE - low, TILE), TILE), :]
 
 
 def edges_kernel(members, own, west, east, facts, hist, strip_base, first, second, base, coef):
@@ -286,7 +307,7 @@
         for t in range(2):
             rows = slice(TILE * t, TILE * t + TILE)
             halos = west[v, rows, :], east[v, rows, :]
-            strips = fill_strips(own_strips(lambda m: own[m, v, rows, :], members), *halos)
+            strips = fill_strips(own_strips(lambda m: own[m, v, rows, :], members), *halos, members)
             for g, strip in enumerate(strips):
                 at = FRONT + (3 * g + v) * PYRAMID + TILE * t
                 first[at : at + TILE, :] = strip
@@ -307,76 +328,85 @@
 BASE = 40
 
 
-def side_kernel(
-    members, is_a, own, halo, facts, hist_c, hist_e, strip_base, partial_in, fields, result, *scratch
-):
-    base, base_e, coef, coef_e, pairs = scratch[:5]
-    count = (len(scratch) - 5) // 2
-    first, second = scratch[5 : 5 + count], scratch[5 + count :]
-    north = jnp.logical_not(is_even("lat")) if is_a else is_even("lat")
-    side = jnp.where(north, 0, 1)
-    wedge_at = jnp.where(north, 0, TILE)
-    hist_at = jnp.where(north, TILE, 0)
-    read_at = jnp.where(north, 0, TILE - 2)
-    own_at = jnp.where(north, 2 * TILE, 1)
-    halo_at = jnp.where(north, TILE, 2 * TILE + 1)
-    facts_at = jnp.where(north, 0, 2 * TILE - 1)
-    zero = dynamic_zero()
-    kinds = strip_kinds(members)
-    groups = len(kinds)
-    triples_c = list(range(members))
-    planes_c = 3 * members
-
+class Side:
+    def __init__(self, last):
+        north = is_north(last)
+        self.north = north
+        self.index = jnp.where(north, 0, 1)
+        self.wedge_at = jnp.where(north, 0, TILE)
+        self.lean_at = jnp.where(north, TILE, 0)
+        self.read_at = jnp.where(north, 0, TILE - 2)
+        self.own_at = jnp.where(north, 2 * TILE, 1)
+        self.halo_at = jnp.where(north, TILE, 2 * TILE + 1)
+        self.facts_at = jnp.where(north, 0, 2 * TILE - 1)
+        self.zero = dynamic_zero()
+
+    def wedge(self, v):
+        return pl.ds(self.wedge_at + v * WEDGE, TILE)
+
+    def put_base(self, base, plane, own, halo):
+        for t in range(2):
+            base[pl.ds(self.own_at + plane * BASE + TILE * t, TILE), :] = own(t)
+        base[pl.ds(self.halo_at + plane * BASE, TILE), :] = halo
+
+    def coefs(self, base, kind, facts, coef):
+        coef_at = self.zero + kind * NCOEF * FACTS
+        at = self.zero + TILE + 3 * kind * BASE
+        store_coefs(base, at, BASE, facts, self.facts_at, coef, coef_at, range(2))
+        return coef_at
+
+
+def prepare_centre(side, members, own, halo, facts, base, coef, first):
     for m in range(members):
         for v in range(3):
-            first[m][pl.ds(wedge_at + v * WEDGE, TILE), :] = halo[3 * m + v]
+            first[m][side.wedge(v), :] = halo(m, v)
     for v in range(3):
-        west, east = halo[planes_c + 3 + v], halo[planes_c + 6 + v]
-        strips = fill_strips(own_strips(lambda m: halo[3 * m + v], members), west, east)
+        side.put_base(base, v, lambda t: own[members, v, TILE * t : TILE * t + TILE, :], halo(members, v))
+    return [(coef, side.coefs(base, 0, facts, coef), list(range(members)))]
+
+
+def prepare_edges(side, members, halo, corner, facts, strip_base, base, coef, first):
+    kinds = strip_kinds(members)
+    for v in range(3):
+        west, east = corner(v)
+        strips = fill_strips(own_strips(lambda m: halo(m, v), members), west, east, members)
         for g, strip in enumerate(strips):
-            first[members + g][pl.ds(wedge_at + v * WEDGE, TILE), :] = strip
-        for t in range(2):
-            base[pl.ds(own_at + v * BASE + TILE * t, TILE), :] = own[members, v, TILE * t : TILE * t + TILE, :]
-        base[pl.ds(halo_at + v * BASE, TILE), :] = halo[planes_c + v]
-        for kind, strip in enumerate(base_strips(halo[planes_c + v], west, east, members)):
-            plane = 3 * kind + v
-            for t in range(2):
-                base_e[pl.ds(own_at + plane * BASE + TILE * t, TILE), :] = strip_base[
-                    kind, v, TILE * t : TILE * t + TILE, :
-                ]
-            base_e[pl.ds(halo_at + plane * BASE, TILE), :] = strip
-    store_coefs(base, zero + TILE, BASE, facts, facts_at, coef, zero, range(2))
-    work = [(coef, zero, triples_c)]
-    for kind in range(KINDS):
-        coef_at = zero + kind * NCOEF * FACTS
-        store_coefs(base_e, zero + TILE + 3 * kind * BASE, BASE, facts, facts_at, coef_e, coef_at, range(2))
-        work.append((coef_e, coef_at, [members + g for g in range(groups) if kinds[g] == kind]))
-
-    refs = [first, second]
-
-    def lean(step):
-        for triple, ref in enumerate(refs[step % 2]):
-            for v in range(3):
-                if triple < members:
-                    rows = hist_c[side, step, 3 * triple + v]
-                else:
-                    rows = hist_e[side, step, 3 * (triple - members) + v]
-                ref[pl.ds(hist_at + v * WEDGE, TILE), :] = rows
-
-    lean(0)
+            first[members + g][side.wedge(v), :] = strip
+        for kind, strip in enumerate(base_strips(halo(members, v), west, east, members)):
+            side.put_base(base, 3 * kind + v, lambda t: strip_base[kind, v, TILE * t : TILE * t + TILE, :], strip)
+    return [
+        (coef, side.coefs(base, kind, facts, coef), [members + g for g in range(len(kinds)) if kinds[g] == kind])
+        for kind in range(KINDS)
+    ]
+
+
+def run_wedges(members, jobs):
+    def lean(job, step):
+        side, work, hist_c, hist_e, *refs = job
+        for _, _, part in work:
+            for triple in part:
+                hist, plane = (hist_c, 3 * triple) if triple < members else (hist_e, 3 * (triple - members))
+                for v in range(3):
+                    refs[step % 2][triple][pl.ds(side.lean_at + v * WEDGE, TILE), :] = hist[side.index, step, plane + v]
+
+    for job in jobs:
+        lean(job, 0)
     for step in range(1, STEPS + 1):
-        src, dst = refs[(step - 1) % 2], refs[step % 2]
-        row = jnp.where(north, step - 1, STEPS - step)
-        for ref, coef_at, triples in work:
-            coefs = load_coefs(ref, coef_at + row)
-            for triple in triples:
-                new = step_tile(src[triple], read_at, WEDGE, coefs)
-                for v in range(3):
-                    dst[triple][pl.ds(wedge_at + v * WEDGE, TILE), :] = new[v]
-        if step < STEPS:
-            lean(step)
-
-    done = refs[STEPS % 2]
+        for job in jobs:
+            side, work, _, _, *refs = job
+            src, dst = refs[(step - 1) % 2], refs[step % 2]
+            row = jnp.where(side.north, step - 1, STEPS - step)
+            for ref, coef_at, part in work:
+                coefs = load_coefs(ref, coef_at + row)
+                for triple in part:
+                    new = step_tile(src[triple], side.read_at, WEDGE, coefs)
+                    for v in range(3):
+                        dst[triple][side.wedge(v), :] = new[v]
+            if step < STEPS:
+                lean(job, step)
+
+
+def merge(side, members, done, inner, fields):
     place = in_strip()
     lanes = lane_ids()
     edge = (lanes < HALO) | (lanes >= LANES - HALO)
@@ -384,41 +414,93 @@
     for v in range(3):
 
         def strip(g):
-            return done[members + g][pl.ds(wedge_at + v * WEDGE, TILE), :]
+            return done[members + g][side.wedge(v), :]
 
         for q in range(full + 1):
             west, east = (strip(q), strip(full + q)) if q < full else (strip(2 * full), rotate(strip(2 * full), -MIX))
             both = jnp.where((place >= HALO) & (place < 2 * HALO), west, east)
             for s in range(min(SLOTS, members - SLOTS * q)):
                 m = SLOTS * q + s
-                inner = done[m][pl.ds(wedge_at + v * WEDGE, TILE), :]
-                fields[m, v] = jnp.where(edge, rotate(both, -STRIP * s - HALO), inner)
+                fields[m, v] = jnp.where(edge, rotate(both, -STRIP * s - HALO), inner(m, v))
+
+
+def pair_sums(members, fields_1, fields_2, pairs):
     for i in range(members):
         for j in range(i, members):
             at = TILE * pair_place(i, j, members)
-            pairs[at : at + TILE, :] = (
-                fields[i, 0] * fields[j, 0] + fields[i, 1] * fields[j, 1] + fields[i, 2] * fields[j, 2]
-            )
-    half = members // 2
+            products = [ref[i, v] * ref[j, v] for ref in (fields_1, fields_2) for v in range(3)]
+            pairs[at : at + TILE, :] = sum(products[1:], products[0])
     sums = []
     for a in range(members + 1):
-        for b in range(half, TILE):
+        for b in range(members // 2, TILE):
             at = TILE * (TILE * a + b)
             pairs[at : at + TILE, :] = jnp.zeros((TILE, LANES), f32)
         total = pairs[pl.ds(TILE * TILE * a, TILE, stride=TILE), :]
         for s in range(1, TILE):
             total = total + pairs[pl.ds(TILE * TILE * a + s, TILE, stride=TILE), :]
         sums.append(total)
-    if is_a:
-        for a in range(members + 1):
-            result[TILE * a : TILE * a + TILE, :] = sums[a]
-    else:
-        packed = jnp.zeros((TILE, LANES), f32)
-        for a in range(members + 1):
-            total = jnp.sum(sums[a] + partial_in[TILE * a : TILE * a + TILE, :], axis=1, keepdims=True)
-            packed = jnp.where(lanes == a, total, packed)
-        packed = pltpu.roll(packed, 0, axis=1, stride=SPREAD, stride_axis=0)
-        result[...] = jnp.broadcast_to(jnp.sum(packed, axis=0, keepdims=True), result.shape)
+    return sums
+
+
+def centre_side(side, members, own, halo, facts, hist_c, centre, base, coef, wedges):
+    first, second = wedges[:members], wedges[members:]
+    work = prepare_centre(side, members, own, halo, facts, base, coef, first)
+    run_wedges(members, [(side, work, hist_c, None, first, second)])
+    for m in range(members):
+        for v in range(3):
+            centre[m, v] = first[m][side.wedge(v), :]
+
+
+def first_rows(halo_a):
+    inner = is_inner() == 1
+    return lambda m, v: jnp.where(inner, halo_a[m, v], 0.0)
+
+
+def last_rows(halo_a, halo_b):
+    inner = is_inner() == 1
+    return lambda m, v: jnp.where(inner, halo_b[m, v], halo_a[m, v])
+
+
+def first_centre_kernel(members, own, halo_a, facts, hist_c, centre, base, coef, *wedges):
+    centre_side(Side(False), members, own, first_rows(halo_a), facts, hist_c, centre, base, coef, wedges)
+
+
+def last_centre_kernel(members, own, halo_a, halo_b, facts, hist_c, centre, base, coef, *wedges):
+    centre_side(Side(True), members, own, last_rows(halo_a, halo_b), facts, hist_c, centre, base, coef, wedges)
+
+
+def edges_of_sides_kernel(
+    members, centre_1, centre_2, halo_a, halo_b, corners, facts, hist_e, strip_base, fields_1, fields_2, result, *scratch
+):
+    inner = is_inner() == 1
+    bases, coefs, pairs, wedges = scratch[0:2], scratch[2:4], scratch[4], scratch[5:]
+    groups = len(wedges) // 4
+
+    def corner_first(v):
+        return tuple(jnp.where(inner, corners[i, v], 0.0) for i in range(2))
+
+    def corner_last(v):
+        return tuple(jnp.where(inner, halo_b[members + 1 + i, v], corners[i, v]) for i in range(2))
+
+    jobs = []
+    halos = (first_rows(halo_a), corner_first), (last_rows(halo_a, halo_b), corner_last)
+    for n, (halo, corner) in enumerate(halos):
+        side = Side(n == 1)
+        part = wedges[2 * n * groups : 2 * (n + 1) * groups]
+        first = {members + g: part[g] for g in range(groups)}
+        second = {members + g: part[groups + g] for g in range(groups)}
+        work = prepare_edges(side, members, halo, corner, facts, strip_base, bases[n], coefs[n], first)
+        jobs.append((side, work, None, hist_e, first, second))
+    run_wedges(members, jobs)
+    for n, (centre, fields) in enumerate(((centre_1, fields_1), (centre_2, fields_2))):
+        merge(jobs[n][0], members, jobs[n][4], lambda m, v: centre[m, v], fields)
+    sums = pair_sums(members, fields_1, fields_2, pairs)
+    lanes = lane_ids()
+    packed = jnp.zeros((TILE, LANES), f32)
+    for a, total in enumerate(sums):
+        packed = jnp.where(lanes == a, jnp.sum(total, axis=1, keepdims=True), packed)
+    packed = pltpu.roll(packed, 0, axis=1, stride=SPREAD, stride_axis=0)
+    result[...] = jnp.broadcast_to(jnp.sum(packed, axis=0, keepdims=True), result.shape)
 
 
 SPREAD = LANES // TILE
@@ -428,10 +510,6 @@
     b = min(i, members - 1 - i)
     a = j - b if i == b else j + 1
     return TILE * a + b
-
-
-def first_side_kernel(members, own, halo, facts, hist_c, hist_e, strip_base, fields, result, *scratch):
-    side_kernel(members, True, own, halo, facts, hist_c, hist_e, strip_base, None, fields, result, *scratch)
 
 
 def finish_kernel(members, count, fields_a, fields_b, got, out, factor_out, done, factor, sems):
@@ -446,8 +524,8 @@
             place = pair_place(i, j, members)
             lane = SPREAD * (place % TILE) + place // TILE
             gram[i, j] = jnp.broadcast_to(packed[:, lane : lane + 1], (TILE, LANES))
-    a_at = pl.multiple_of(jnp.where(is_even("lat"), TILE, 0), TILE)
-    places = [a_at, pl.multiple_of(TILE - a_at, TILE)]
+    first_at = pl.multiple_of(jnp.where(is_north(False), 0, TILE), TILE)
+    places = [first_at, pl.multiple_of(TILE - first_at, TILE)]
     x = [[[ref[m, v] for v in range(3)] for ref in (fields_a, fields_b)] for m in range(members)]
     lanes = lane_ids()
     copies = []
@@ -492,8 +570,8 @@
     return jax.ShapeDtypeStruct(dims, f32)
 
 
-def cost(flops):
-    return pl.CostEstimate(flops=flops, bytes_accessed=1_000_000, transcendentals=0)
+def cost(micros):
+    return pl.CostEstimate(flops=0, bytes_accessed=int(micros * 3.6e6), transcendentals=0)
 
 
 def per_device(perturbations, base_wind, base_height):
@@ -503,15 +581,21 @@
     groups = len(strip_kinds(members))
     planes_c, planes_e = 3 * members, 3 * groups
 
-    own, msg_a, msg_b = pl.pallas_call(
+    own, main_a, msg_a, msg_b = pl.pallas_call(
         functools.partial(load_kernel, members),
-        out_shape=[shape(members + 1, 3, rows, LANES), shape(3, rows, LANES), shape(3, rows, LANES)],
+        out_shape=[
+            shape(members + 1, 3, rows, LANES),
+            shape(members + 1 + SPARE, 3, TILE, LANES),
+            shape(3, rows, LANES),
+            shape(3, rows, LANES),
+        ],
         in_specs=[HBM] * 3,
-        out_specs=[VMEM] * 3,
+        out_specs=[VMEM] * 4,
         scratch_shapes=[pltpu.SemaphoreType.DMA((6,))],
         compiler_params=PARAMS,
         name="load",
     )(*(pltpu.with_memory_space_constraint(x, pltpu.HBM) for x in (perturbations, base_wind, base_height)))
+    halo_a = swap(main_a, "lat", n_lat, True, False)
     got_b = swap(msg_b, "lon", n_lon, False, True)
     got_a = swap(msg_a, "lon", n_lon, True, True)
 
@@ -527,21 +611,26 @@
             pltpu.VMEM((NCOEF * FACTS, LANES), f32),
         ],
         compiler_params=PARAMS,
-        cost_estimate=cost(3_000_000),
+        cost_estimate=cost(20),
         name="centre",
     )(own)
 
-    send = shape(3 * members + 9, TILE, LANES)
-    send_a, send_b, west, east = pl.pallas_call(
+    send_b, west, east, corners = pl.pallas_call(
         functools.partial(meet_kernel, members),
-        out_shape=[send, send, shape(3, rows, LANES), shape(3, rows, LANES)],
-        in_specs=[VMEM] * 4,
+        out_shape=[
+            shape(members + 3, 3, TILE, LANES),
+            shape(3, rows, LANES),
+            shape(3, rows, LANES),
+            shape(2, 3, TILE, LANES),
+        ],
+        in_specs=[VMEM] * 3,
         out_specs=[VMEM] * 4,
         compiler_params=PARAMS,
+        cost_estimate=cost(0.01),
         name="meet",
-    )(own, got_b, got_a, facts)
-    halo_a = swap(send_a, "lat", n_lat, True, False)
+    )(own, got_b, got_a)
     halo_b = swap(send_b, "lat", n_lat, False, False)
+    corners = swap(corners, "lat", n_lat, True, False)
 
     hist_e, strip_base = pl.pallas_call(
         functools.partial(edges_kernel, members),
@@ -555,38 +644,46 @@
             pltpu.VMEM((KINDS * NCOEF * FACTS, LANES), f32),
         ],
         compiler_params=PARAMS,
-        cost_estimate=cost(2_000_000),
+        cost_estimate=cost(0.01),
         name="edges",
     )(own, west, east, facts)
 
-    wedges = [
-        pltpu.VMEM((3 * BASE, LANES), f32),
-        pltpu.VMEM((3 * KINDS * BASE, LANES), f32),
-        pltpu.VMEM((NCOEF * FACTS, LANES), f32),
-        pltpu.VMEM((KINDS * NCOEF * FACTS, LANES), f32),
-        pltpu.VMEM((TILE * LANES, LANES), f32),
-    ] + [pltpu.VMEM((3 * WEDGE, LANES), f32)] * (2 * (members + groups))
+    def scratch(bases, triples, with_pairs):
+        shapes = [(3 * n * BASE, LANES) for n in bases] + [(n * NCOEF * FACTS, LANES) for n in bases]
+        shapes += [(TILE * LANES, LANES)] * with_pairs + [(3 * WEDGE, LANES)] * (2 * triples)
+        return [pltpu.VMEM(dims, f32) for dims in shapes]
+
     half = shape(members, 3, TILE, LANES)
-    fields_a, partial = pl.pallas_call(
-        functools.partial(first_side_kernel, members),
-        out_shape=[half, shape((members + 1) * TILE, LANES)],
-        in_specs=[VMEM] * 6,
-        out_specs=[VMEM] * 2,
-        scratch_shapes=wedges,
+    centre_first = pl.pallas_call(
+        functools.partial(first_centre_kernel, members),
+        out_shape=half,
+        in_specs=[VMEM] * 4,
+        out_specs=VMEM,
+        scratch_shapes=scratch([1], members, 0),
         compiler_params=PARAMS,
-        cost_estimate=cost(4_000_000),
-        name="side_a",
-    )(own, halo_a, facts, hist_c, hist_e, strip_base)
-    fields_b, send_gram = pl.pallas_call(
-        functools.partial(side_kernel, members, False),
-        out_shape=[half, shape(n_lat * n_lon, LANES)],
-        in_specs=[VMEM] * 7,
-        out_specs=[VMEM] * 2,
-        scratch_shapes=wedges,
+        cost_estimate=cost(0.01),
+        name="first_centre",
+    )(own, halo_a, facts, hist_c)
+    centre_last = pl.pallas_call(
+        functools.partial(last_centre_kernel, members),
+        out_shape=half,
+        in_specs=[VMEM] * 5,
+        out_specs=VMEM,
+        scratch_shapes=scratch([1], members, 0),
         compiler_params=PARAMS,
-        cost_estimate=cost(4_000_000),
-        name="side_b",
-    )(own, halo_b, facts, hist_c, hist_e, strip_base, partial)
+        cost_estimate=cost(0.01),
+        name="last_centre",
+    )(own, halo_a, halo_b, facts, hist_c)
+    fields_first, fields_last, send_gram = pl.pallas_call(
+        functools.partial(edges_of_sides_kernel, members),
+        out_shape=[half, half, shape(n_lat * n_lon, LANES)],
+        in_specs=[VMEM] * 8,
+        out_specs=[VMEM] * 3,
+        scratch_shapes=scratch([KINDS, KINDS], 2 * groups, 1),
+        compiler_params=PARAMS,
+        cost_estimate=cost(0.01),
+        name="edges_of_sides",
+    )(centre_first, centre_last, halo_a, halo_b, corners, facts, hist_e, strip_base)
 
     got = lax.all_to_all(send_gram, ("lon", "lat"), 0, 0, tiled=True)
 
@@ -602,7 +699,7 @@
         ],
         compiler_params=PARAMS,
         name="finish",
-    )(fields_a, fields_b, got)
+    )(fields_first, fields_last, got)
 
 
 def solution(mesh):

time: 33.5 us -> 32.7 us (0.976)
  starting transfers between devices: 7.16 us -> 11.4 us
  waiting for transfers between devices: 3.26 us -> 0.51 us
  blocking collectives: 14.1 us -> 11.4 us
  Pallas kernels: 7.99 us -> 8.46 us
    ppermute x4 -> x5, starting transfers between devices: 7.16 us -> 11.4 us  [swap(): return lax.ppermute(block, axis, pairs)]
    ppermute x4 -> x5, waiting for transfers between devices: 3.26 us -> 0.51 us  [swap(): return lax.ppermute(block, axis, pairs)]
    all_to_all x1, blocking collectives: 14.1 us -> 11.4 us  [per_device(): got = lax.all_to_all(send_gram, ('lon', 'lat'), 0, 0, tiled=True)]
    pallas_call x3 -> x4, Pallas kernels: 3.29 us -> 3.9 us  [the longest x1 1.77 us: per_device(): pl.pallas_call(functools.partial(edges_of_sides_kernel, members), out_sha...]
  transfers between devices with their start and end apart: 4 -> 5, of which waited for: 2 -> 2; matrix products, arithmetic and copies ran while one was open for 0% -> 0% of each run, Pallas kernels for 12% -> 14%
where the time goes in v5:
time: 32.7 us; the launch traced here: 32.5 us
  starting transfers between devices  11.4 us (35%)
  blocking collectives  11.4 us (35%)
  Pallas kernels  8.46 us (26%)
  between operations  0.7 us (2%)
  waiting for transfers between devices  0.51 us (2%)
    all_to_all x1, blocking collectives, per_device(): got = lax.all_to_all(send_gram, ('lon', 'lat'), 0, 0, tiled=True)  11.4 us
    ppermute x5, starting transfers between devices, swap(): return lax.ppermute(block, axis, pairs)  11.4 us
    pallas_call x1, Pallas kernels, per_device(): pl.pallas_call(functools.partial(edges_of_sides_kernel, members), out_sha...  1.77 us
    pallas_call x1, Pallas kernels, per_device(): pl.pallas_call(functools.partial(load_kernel, members), out_shape=[shape(...  1.24 us
    pallas_call x1, Pallas kernels, per_device(): pl.pallas_call(functools.partial(centre_kernel, members, total_rows), out...  1.14 us
    pallas_call x1, Pallas kernels, per_device(): pl.pallas_call(functools.partial(edges_kernel, members), out_shape=[shape...  1.13 us
    pallas_call x1, Pallas kernels, per_device(): pl.pallas_call(functools.partial(last_centre_kernel, members), out_shape=...  1.06 us
    pallas_call x1, Pallas kernels, per_device(): pl.pallas_call(functools.partial(finish_kernel, members, float(3 * total_...  1.05 us
  transfers between devices with their start and end apart: 5, of which 2 were waited for; matrix products, arithmetic and copies ran while one was open for 0% of the time, Pallas kernels for 14%

profile of v5, /device:TPU:0, one launch (start us, length us, event | category | flops | bytes accessed | tf_op | source)
XLA Modules:
  0.0 32.5 jit_solution(9944596961037899297)
XLA Ops:
  0.6 1.2 %load.1 = (f32[13,3,16,128]{3,2,1,0:T(8,128)S(1)}, f32[16,3,8,128]{3,2,1,0:T(8,128)S(1)}, f32[3,16,128]{2,1,0:T(8,128)S(1)}, f32[3,16,128]{2,1,0:T(8,128)S(1)}) custom-call(f32[12,3,16,128]{3,2,1,0:T(8,128)} %pert.1, f32[2,16,128]{2,1,0:T(8,128)} %wind.1, f32[16,128]{1,0:T(8,128)} %height.1), custom_call_target="tpu_custom_call" | custom-call | tf_op jit(solution)/shard_map/load/pallas_call | solution.py:584
  1.9 4.6 %collective-permute-start.1 = (f32[3,16,128]{2,1,0:T(8,128)S(1)}, f32[3,16,128]{2,1,0:T(8,128)S(1)}, u32[]{:S(2)}, u32[]{:S(2)}) collective-permute-start(f32[3,16,128]{2,1,0:T(8,128)S(1)} %get-tuple-element.21), channel_id=1, source_target_pairs={{0,28},{4,8},{8,4},{12,16},{16,12},{20,24},{24,20},{28,0},{1,29},{... | collective-permute-start | bytes 73736 | tf_op jit(solution)/shard_map/ppermute | solution.py:566
  6.4 0.0 collective-permute-start.2
  6.4 1.5 %collective-permute-start = (f32[16,3,8,128]{3,2,1,0:T(8,128)S(1)}, f32[16,3,8,128]{3,2,1,0:T(8,128)S(1)}, u32[]{:S(2)}, u32[]{:S(2)}) collective-permute-start(f32[16,3,8,128]{3,2,1,0:T(8,128)S(1)} %get-tuple-element.18), channel_id=1, source_target_pairs={{0,1},{1,0},{2,3},{3,2},{4,5},{5,4},{6,7},{7,6},{8,9},{9,8},{10,11... | collective-permute-start | bytes 589832 | tf_op jit(solution)/shard_map/ppermute | solution.py:566
  7.9 0.1 collective-permute-done.1.got_b
  8.1 0.0 collective-permute-done.2.got_a
  8.1 0.7 %collective-permute-start.3 = (f32[15,3,8,128]{3,2,1,0:T(8,128)S(1)}, f32[15,3,8,128]{3,2,1,0:T(8,128)S(1)}, u32[]{:S(2)}, u32[]{:S(2)}) collective-permute-start(f32[15,3,8,128]{3,2,1,0:T(8,128)S(1)} %get-tuple-element.23), channel_id=1, source_target_pairs={{1,2},{2,1},{5,6},{6,5},{9,10},{10,9},{13,14},{14,13},{17,18},{18,... | collective-permute-start | bytes 552968 | tf_op jit(solution)/shard_map/ppermute | solution.py:566
  8.8 4.7 %collective-permute-start.4 = (f32[2,3,8,128]{3,2,1,0:T(8,128)S(1)}, f32[2,3,8,128]{3,2,1,0:T(8,128)S(1)}, u32[]{:S(2)}, u32[]{:S(2)}) collective-permute-start(f32[2,3,8,128]{3,2,1,0:T(8,128)S(1)} %get-tuple-element.24), channel_id=1, source_target_pairs={{0,1},{1,0},{2,3},{3,2},{4,5},{5,4},{6,7},{7,6},{8,9},{9,8},{10,11... | collective-permute-start | bytes 73736 | tf_op jit(solution)/shard_map/ppermute | solution.py:566
  13.4 1.1 %centre.1 = (f32[2,40,128]{2,1,0:T(8,128)S(1)}, f32[2,8,36,8,128]{4,3,2,1,0:T(8,128)S(1)}) custom-call(f32[13,3,16,128]{3,2,1,0:T(8,128)S(1)} %get-tuple-element.17.own), custom_call_target="tpu_custom_call" | custom-call | bytes 72000000 | tf_op jit(solution)/shard_map/centre/pallas_call | solution.py:602
  14.6 1.1 %edges.1 = (f32[2,8,15,8,128]{4,3,2,1,0:T(8,128)S(1)}, f32[3,3,16,128]{3,2,1,0:T(8,128)S(1)}) custom-call(f32[13,3,16,128]{3,2,1,0:T(8,128)S(1)} %get-tuple-element.17.own, f32[3,16,128]{2,1,0:T(8,128)S(1)} %get-tuple-element.25.west, f32[3,16,128]{2,1,0:T(8,128)S(1)} %get-tuple-element.26.east, f32[2,40,128]{2,1,0:T(8,128)S(1)} %get-tuple-element.19.facts), custom_call_target="tpu_custom_call" | custom-call | bytes 36000 | tf_op jit(solution)/shard_map/edges/pallas_call | solution.py:635
  15.7 0.0 collective-permute-done.halo_a
  15.7 1.0 %first_centre.1.centre_1 = f32[12,3,8,128]{3,2,1,0:T(8,128)S(1)} custom-call(f32[13,3,16,128]{3,2,1,0:T(8,128)S(1)} %get-tuple-element.17.own, f32[16,3,8,128]{3,2,1,0:T(8,128)S(1)} %collective-permute-done.halo_a, f32[2,40,128]{2,1,0:T(8,128)S(1)} %get-tuple-element.19.facts, f32[2,8,36,8,128]{4,3,2,1,0:T(8,128)S(1)} %get-tuple-element.20.hist_c), custom_call_target="tpu_custom_call" | custom-call | bytes 36000 | tf_op jit(solution)/shard_map/first_centre/pallas_call | solution.py:657
  16.8 0.0 collective-permute-done.3.halo_b
  16.8 1.1 %last_centre.1.centre_2 = f32[12,3,8,128]{3,2,1,0:T(8,128)S(1)} custom-call(f32[13,3,16,128]{3,2,1,0:T(8,128)S(1)} %get-tuple-element.17.own, f32[16,3,8,128]{3,2,1,0:T(8,128)S(1)} %collective-permute-done.halo_a, f32[15,3,8,128]{3,2,1,0:T(8,128)S(1)} %collective-permute-done.3.halo_b, f32[2,40,128]{2,1,0:T(8,128)S(1)} %get-tuple-element.19.facts, ...), custom_call_target="tpu_custom_call" | custom-call | bytes 36000 | tf_op jit(solution)/shard_map/last_centre/pallas_call | solution.py:667
  17.9 0.4 %collective-permute-done.4.corners = f32[2,3,8,128]{3,2,1,0:T(8,128)S(1)} collective-permute-done((f32[2,3,8,128]{3,2,1,0:T(8,128)S(1)}, f32[2,3,8,128]{3,2,1,0:T(8,128)S(1)}, u32[]{:S(2)}, u32[]{:S(2)}) %collective-permute-start.4) | collective-permute-done | bytes 24608 | tf_op jit(solution)/shard_map/ppermute | solution.py:566
  18.2 1.8 %edges_of_sides.1 = (f32[12,3,8,128]{3,2,1,0:T(8,128)S(1)}, f32[12,3,8,128]{3,2,1,0:T(8,128)S(1)}, f32[32,128]{1,0:T(8,128)S(1)}) custom-call(f32[12,3,8,128]{3,2,1,0:T(8,128)S(1)} %first_centre.1.centre_1, f32[12,3,8,128]{3,2,1,0:T(8,128)S(1)} %last_centre.1.centre_2, f32[16,3,8,128]{3,2,1,0:T(8,128)S(1)} %collective-permute-done.halo_a, ...), custom_call_target="tpu_custom_call" | custom-call | bytes 36000 | tf_op jit(solution)/shard_map/edges_of_sides/pallas_call | solution.py:677
  20.0 11.4 %all_to_all.11 = f32[32,1,128]{2,1,0:T(1,128)S(1)} all-to-all(f32[32,1,128]{2,1,0:T(1,128)S(1)} %bitcast.5), channel_id=1, replica_groups=mesh['lon'=8,'lat'=4] {'lon','lat'}, dimensions={0} | all-to-all | bytes 32768 | tf_op jit(solution)/shard_map/all_to_all | solution.py:688
  31.4 1.1 %finish.1 = (f32[12,3,16,128]{3,2,1,0:T(8,128)}, f32[12,12]{1,0:T(8,128)}) custom-call(f32[12,3,8,128]{3,2,1,0:T(8,128)S(1)} %get-tuple-element.29.fields_a, f32[12,3,8,128]{3,2,1,0:T(8,128)S(1)} %get-tuple-element.30.fields_b, f32[32,128]{1,0:T(8,128)S(1)} %bitcast.4), custom_call_target="tpu_custom_call" | custom-call | tf_op jit(solution)/shard_map/finish/pallas_call | solution.py:690
  (1 shorter events, 0.0 us)
Async XLA Ops:
  1.9 6.2 %collective-permute-start.1 = (f32[3,16,128]{2,1,0:T(8,128)S(1)}, f32[3,16,128]{2,1,0:T(8,128)S(1)}, u32[]{:S(2)}, u32[]{:S(2)}) collective-permute-start(f32[3,16,128]{2,1,0:T(8,128)S(1)} %get-tuple-element.21), channel_id=1, source_target_pairs={{0,28},{4,8},{8,4},{12,16},{16,12},{20,24},{24,20},{28,0},{1,29},{... | collective-permute-start | bytes 73736 | tf_op jit(solution)/shard_map/ppermute | solution.py:566
  6.4 1.6 %collective-permute-start.2 = (f32[3,16,128]{2,1,0:T(8,128)S(1)}, f32[3,16,128]{2,1,0:T(8,128)S(1)}, u32[]{:S(2)}, u32[]{:S(2)}) collective-permute-start(f32[3,16,128]{2,1,0:T(8,128)S(1)} %get-tuple-element.22), channel_id=1, source_target_pairs={{0,4},{4,0},{8,12},{12,8},{16,20},{20,16},{24,28},{28,24},{1,5},{5... | collective-permute-start | bytes 73736 | tf_op jit(solution)/shard_map/ppermute | solution.py:566
  6.4 9.3 %collective-permute-start = (f32[16,3,8,128]{3,2,1,0:T(8,128)S(1)}, f32[16,3,8,128]{3,2,1,0:T(8,128)S(1)}, u32[]{:S(2)}, u32[]{:S(2)}) collective-permute-start(f32[16,3,8,128]{3,2,1,0:T(8,128)S(1)} %get-tuple-element.18), channel_id=1, source_target_pairs={{0,1},{1,0},{2,3},{3,2},{4,5},{5,4},{6,7},{7,6},{8,9},{9,8},{10,11... | collective-permute-start | bytes 589832 | tf_op jit(solution)/shard_map/ppermute | solution.py:566
  8.1 8.7 %collective-permute-start.3 = (f32[15,3,8,128]{3,2,1,0:T(8,128)S(1)}, f32[15,3,8,128]{3,2,1,0:T(8,128)S(1)}, u32[]{:S(2)}, u32[]{:S(2)}) collective-permute-start(f32[15,3,8,128]{3,2,1,0:T(8,128)S(1)} %get-tuple-element.23), channel_id=1, source_target_pairs={{1,2},{2,1},{5,6},{6,5},{9,10},{10,9},{13,14},{14,13},{17,18},{18,... | collective-permute-start | bytes 552968 | tf_op jit(solution)/shard_map/ppermute | solution.py:566
  8.8 9.5 %collective-permute-start.4 = (f32[2,3,8,128]{3,2,1,0:T(8,128)S(1)}, f32[2,3,8,128]{3,2,1,0:T(8,128)S(1)}, u32[]{:S(2)}, u32[]{:S(2)}) collective-permute-start(f32[2,3,8,128]{3,2,1,0:T(8,128)S(1)} %get-tuple-element.24), channel_id=1, source_target_pairs={{0,1},{1,0},{2,3},{3,2},{4,5},{5,4},{6,7},{7,6},{8,9},{9,8},{10,11... | collective-permute-start | bytes 73736 | tf_op jit(solution)/shard_map/ppermute | solution.py:566

commit v6 on v5

--- a/solution.py
+++ b/solution.py
@@ -18,7 +18,7 @@
 MIX = 2 * STRIP + HALO
 KINDS = 3
 NCOEF = 18
-SPARE = 3
+SPARE = 2
 
 advect_rate = 0.1
 turn_rate = 0.5
@@ -222,14 +222,11 @@
 
 
 def load_kernel(members, pert, wind, height, own, main_a, msg_a, msg_b, sems):
-    chunk = members // 4
     copies = [
-        pltpu.make_async_copy(wind, own.at[members, pl.ds(0, 2)], sems.at[0]),
-        pltpu.make_async_copy(height, own.at[members, 2], sems.at[1]),
+        pltpu.make_async_copy(pert, own.at[pl.ds(0, members)], sems.at[0]),
+        pltpu.make_async_copy(wind, own.at[members, pl.ds(0, 2)], sems.at[1]),
+        pltpu.make_async_copy(height, own.at[members, 2], sems.at[2]),
     ]
-    for i in range(4):
-        part = pl.ds(i * chunk, chunk)
-        copies.append(pltpu.make_async_copy(pert.at[part], own.at[part], sems.at[2 + i]))
     for copy in copies:
         copy.start()
     for copy in copies:
@@ -365,11 +362,15 @@
     return [(coef, side.coefs(base, 0, facts, coef), list(range(members)))]
 
 
-def prepare_edges(side, members, halo, corner, facts, strip_base, base, coef, first):
+def prepare_edges(side, members, halo, corner, facts, strip_base, base, coef, first, ready=None):
     kinds = strip_kinds(members)
     for v in range(3):
         west, east = corner(v)
-        strips = fill_strips(own_strips(lambda m: halo(m, v), members), west, east, members)
+        if ready is None:
+            own = own_strips(lambda m: halo(m, v), members)
+        else:
+            own = [ready[v, g] for g in range(len(kinds))]
+        strips = fill_strips(own, west, east, members)
         for g, strip in enumerate(strips):
             first[members + g][side.wedge(v), :] = strip
         for kind, strip in enumerate(base_strips(halo(members, v), west, east, members)):
@@ -461,7 +462,11 @@
     return lambda m, v: jnp.where(inner, halo_b[m, v], halo_a[m, v])
 
 
-def first_centre_kernel(members, own, halo_a, facts, hist_c, centre, base, coef, *wedges):
+def first_centre_kernel(members, own, halo_a, facts, hist_c, centre, ready, base, coef, *wedges):
+    rows = first_rows(halo_a)
+    for v in range(3):
+        for g, strip in enumerate(own_strips(lambda m: rows(m, v), members)):
+            ready[v, g] = strip
     centre_side(Side(False), members, own, first_rows(halo_a), facts, hist_c, centre, base, coef, wedges)
 
 
@@ -470,7 +475,7 @@
 
 
 def edges_of_sides_kernel(
-    members, centre_1, centre_2, halo_a, halo_b, corners, facts, hist_e, strip_base, fields_1, fields_2, result, *scratch
+    members, centre_1, ready, centre_2, halo_a, halo_b, corners, facts, hist_e, strip_base, fields_1, fields_2, result, *scratch
 ):
     inner = is_inner() == 1
     bases, coefs, pairs, wedges = scratch[0:2], scratch[2:4], scratch[4], scratch[5:]
@@ -489,7 +494,7 @@
         part = wedges[2 * n * groups : 2 * (n + 1) * groups]
         first = {members + g: part[g] for g in range(groups)}
         second = {members + g: part[groups + g] for g in range(groups)}
-        work = prepare_edges(side, members, halo, corner, facts, strip_base, bases[n], coefs[n], first)
+        work = prepare_edges(side, members, halo, corner, facts, strip_base, bases[n], coefs[n], first, [ready, None][n])
         jobs.append((side, work, None, hist_e, first, second))
     run_wedges(members, jobs)
     for n, (centre, fields) in enumerate(((centre_1, fields_1), (centre_2, fields_2))):
@@ -591,7 +596,7 @@
         ],
         in_specs=[HBM] * 3,
         out_specs=[VMEM] * 4,
-        scratch_shapes=[pltpu.SemaphoreType.DMA((6,))],
+        scratch_shapes=[pltpu.SemaphoreType.DMA((3,))],
         compiler_params=PARAMS,
         name="load",
     )(*(pltpu.with_memory_space_constraint(x, pltpu.HBM) for x in (perturbations, base_wind, base_height)))
@@ -654,11 +659,11 @@
         return [pltpu.VMEM(dims, f32) for dims in shapes]
 
     half = shape(members, 3, TILE, LANES)
-    centre_first = pl.pallas_call(
+    centre_first, ready = pl.pallas_call(
         functools.partial(first_centre_kernel, members),
-        out_shape=half,
+        out_shape=[half, shape(3, groups, TILE, LANES)],
         in_specs=[VMEM] * 4,
-        out_specs=VMEM,
+        out_specs=[VMEM] * 2,
         scratch_shapes=scratch([1], members, 0),
         compiler_params=PARAMS,
         cost_estimate=cost(0.01),
@@ -677,13 +682,13 @@
     fields_first, fields_last, send_gram = pl.pallas_call(
         functools.partial(edges_of_sides_kernel, members),
         out_shape=[half, half, shape(n_lat * n_lon, LANES)],
-        in_specs=[VMEM] * 8,
+        in_specs=[VMEM] * 9,
         out_specs=[VMEM] * 3,
         scratch_shapes=scratch([KINDS, KINDS], 2 * groups, 1),
         compiler_params=PARAMS,
         cost_estimate=cost(0.01),
         name="edges_of_sides",
-    )(centre_first, centre_last, halo_a, halo_b, corners, facts, hist_e, strip_base)
+    )(centre_first, ready, centre_last, halo_a, halo_b, corners, facts, hist_e, strip_base)
 
     got = lax.all_to_all(send_gram, ("lon", "lat"), 0, 0, tiled=True)
 

time: 32.7 us -> 32.5 us (level)
  transfers between devices with their start and end apart: 5 -> 5, of which waited for: 2 -> 2; matrix products, arithmetic and copies ran while one was open for 0% -> 0% of each run, Pallas kernels for 14% -> 13%
where the time goes in v6:
time: 32.5 us; the launch traced here: 32.3 us
  blocking collectives  11.5 us (35%)
  starting transfers between devices  11.4 us (35%)
  Pallas kernels  8.26 us (25%)
  between operations  0.7 us (2%)
  waiting for transfers between devices  0.44 us (1%)
    all_to_all x1, blocking collectives, per_device(): got = lax.all_to_all(send_gram, ('lon', 'lat'), 0, 0, tiled=True)  11.5 us
    ppermute x5, starting transfers between devices, swap(): return lax.ppermute(block, axis, pairs)  11.4 us
    pallas_call x1, Pallas kernels, per_device(): pl.pallas_call(functools.partial(edges_of_sides_kernel, members), out_sha...  1.71 us
    pallas_call x1, Pallas kernels, per_device(): pl.pallas_call(functools.partial(load_kernel, members), out_shape=[shape(...  1.16 us
    pallas_call x1, Pallas kernels, per_device(): pl.pallas_call(functools.partial(centre_kernel, members, total_rows), out...  1.14 us
    pallas_call x1, Pallas kernels, per_device(): pl.pallas_call(functools.partial(edges_kernel, members), out_shape=[shape...  1.12 us
    pallas_call x1, Pallas kernels, per_device(): pl.pallas_call(functools.partial(last_centre_kernel, members), out_shape=...  1.06 us
    pallas_call x1, Pallas kernels, per_device(): pl.pallas_call(functools.partial(finish_kernel, members, float(3 * total_...  1.05 us
  transfers between devices with their start and end apart: 5, of which 2 were waited for; matrix products, arithmetic and copies ran while one was open for 0% of the time, Pallas kernels for 13%

profile of v6, /device:TPU:0, one launch (start us, length us, event | category | flops | bytes accessed | tf_op | source)
XLA Modules:
  0.0 32.3 jit_solution(982107881642999918)
XLA Ops:
  0.6 1.2 %load.1 = (f32[13,3,16,128]{3,2,1,0:T(8,128)S(1)}, f32[15,3,8,128]{3,2,1,0:T(8,128)S(1)}, f32[3,16,128]{2,1,0:T(8,128)S(1)}, f32[3,16,128]{2,1,0:T(8,128)S(1)}) custom-call(f32[12,3,16,128]{3,2,1,0:T(8,128)} %pert.1, f32[2,16,128]{2,1,0:T(8,128)} %wind.1, f32[16,128]{1,0:T(8,128)} %height.1), custom_call_target="tpu_custom_call" | custom-call | tf_op jit(solution)/shard_map/load/pallas_call | solution.py:589
  1.8 4.6 %collective-permute-start.1 = (f32[3,16,128]{2,1,0:T(8,128)S(1)}, f32[3,16,128]{2,1,0:T(8,128)S(1)}, u32[]{:S(2)}, u32[]{:S(2)}) collective-permute-start(f32[3,16,128]{2,1,0:T(8,128)S(1)} %get-tuple-element.25), channel_id=1, source_target_pairs={{0,28},{4,8},{8,4},{12,16},{16,12},{20,24},{24,20},{28,0},{1,29},{... | collective-permute-start | bytes 73736 | tf_op jit(solution)/shard_map/ppermute | solution.py:571
  6.3 0.0 collective-permute-start.2
  6.4 1.5 %collective-permute-start = (f32[15,3,8,128]{3,2,1,0:T(8,128)S(1)}, f32[15,3,8,128]{3,2,1,0:T(8,128)S(1)}, u32[]{:S(2)}, u32[]{:S(2)}) collective-permute-start(f32[15,3,8,128]{3,2,1,0:T(8,128)S(1)} %get-tuple-element.20), channel_id=1, source_target_pairs={{0,1},{1,0},{2,3},{3,2},{4,5},{5,4},{6,7},{7,6},{8,9},{9,8},{10,11... | collective-permute-start | bytes 552968 | tf_op jit(solution)/shard_map/ppermute | solution.py:571
  7.8 0.1 collective-permute-done.1.got_b
  8.0 0.0 collective-permute-done.2.got_a
  8.0 0.7 %collective-permute-start.3 = (f32[15,3,8,128]{3,2,1,0:T(8,128)S(1)}, f32[15,3,8,128]{3,2,1,0:T(8,128)S(1)}, u32[]{:S(2)}, u32[]{:S(2)}) collective-permute-start(f32[15,3,8,128]{3,2,1,0:T(8,128)S(1)} %get-tuple-element.27), channel_id=1, source_target_pairs={{1,2},{2,1},{5,6},{6,5},{9,10},{10,9},{13,14},{14,13},{17,18},{18,... | collective-permute-start | bytes 552968 | tf_op jit(solution)/shard_map/ppermute | solution.py:571
  8.7 4.7 %collective-permute-start.4 = (f32[2,3,8,128]{3,2,1,0:T(8,128)S(1)}, f32[2,3,8,128]{3,2,1,0:T(8,128)S(1)}, u32[]{:S(2)}, u32[]{:S(2)}) collective-permute-start(f32[2,3,8,128]{3,2,1,0:T(8,128)S(1)} %get-tuple-element.28), channel_id=1, source_target_pairs={{0,1},{1,0},{2,3},{3,2},{4,5},{5,4},{6,7},{7,6},{8,9},{9,8},{10,11... | collective-permute-start | bytes 73736 | tf_op jit(solution)/shard_map/ppermute | solution.py:571
  13.3 1.1 %centre.1 = (f32[2,40,128]{2,1,0:T(8,128)S(1)}, f32[2,8,36,8,128]{4,3,2,1,0:T(8,128)S(1)}) custom-call(f32[13,3,16,128]{3,2,1,0:T(8,128)S(1)} %get-tuple-element.19.own), custom_call_target="tpu_custom_call" | custom-call | bytes 72000000 | tf_op jit(solution)/shard_map/centre/pallas_call | solution.py:607
  14.5 1.1 %edges.1 = (f32[2,8,15,8,128]{4,3,2,1,0:T(8,128)S(1)}, f32[3,3,16,128]{3,2,1,0:T(8,128)S(1)}) custom-call(f32[13,3,16,128]{3,2,1,0:T(8,128)S(1)} %get-tuple-element.19.own, f32[3,16,128]{2,1,0:T(8,128)S(1)} %get-tuple-element.29.west, f32[3,16,128]{2,1,0:T(8,128)S(1)} %get-tuple-element.30.east, f32[2,40,128]{2,1,0:T(8,128)S(1)} %get-tuple-element.21.facts), custom_call_target="tpu_custom_call" | custom-call | bytes 36000 | tf_op jit(solution)/shard_map/edges/pallas_call | solution.py:640
  15.6 0.0 collective-permute-done.halo_a
  15.6 1.0 %first_centre.1 = (f32[12,3,8,128]{3,2,1,0:T(8,128)S(1)}, f32[3,5,8,128]{3,2,1,0:T(8,128)S(1)}) custom-call(f32[13,3,16,128]{3,2,1,0:T(8,128)S(1)} %get-tuple-element.19.own, f32[15,3,8,128]{3,2,1,0:T(8,128)S(1)} %collective-permute-done.halo_a, f32[2,40,128]{2,1,0:T(8,128)S(1)} %get-tuple-element.21.facts, f32[2,8,36,8,128]{4,3,2,1,0:T(8,128)S(1)} %get-tuple-element.22.hist_c), custom_call_target="tpu_custom_call" | custom-call | bytes 36000 | tf_op jit(solution)/shard_map/first_centre/pallas_call | solution.py:662
  16.6 0.0 collective-permute-done.3.halo_b
  16.6 1.1 %last_centre.1.centre_2 = f32[12,3,8,128]{3,2,1,0:T(8,128)S(1)} custom-call(f32[13,3,16,128]{3,2,1,0:T(8,128)S(1)} %get-tuple-element.19.own, f32[15,3,8,128]{3,2,1,0:T(8,128)S(1)} %collective-permute-done.halo_a, f32[15,3,8,128]{3,2,1,0:T(8,128)S(1)} %collective-permute-done.3.halo_b, f32[2,40,128]{2,1,0:T(8,128)S(1)} %get-tuple-element.21.facts, ...), custom_call_target="tpu_custom_call" | custom-call | bytes 36000 | tf_op jit(solution)/shard_map/last_centre/pallas_call | solution.py:672
  17.7 0.3 collective-permute-done.4.corners
  18.0 1.7 %edges_of_sides.1 = (f32[12,3,8,128]{3,2,1,0:T(8,128)S(1)}, f32[12,3,8,128]{3,2,1,0:T(8,128)S(1)}, f32[32,128]{1,0:T(8,128)S(1)}) custom-call(f32[12,3,8,128]{3,2,1,0:T(8,128)S(1)} %get-tuple-element.23.centre_1, f32[3,5,8,128]{3,2,1,0:T(8,128)S(1)} %get-tuple-element.24.ready, f32[12,3,8,128]{3,2,1,0:T(8,128)S(1)} %last_centre.1.centre_2, ...), custom_call_target="tpu_custom_call" | custom-call | bytes 36000 | tf_op jit(solution)/shard_map/edges_of_sides/pallas_call | solution.py:682
  19.7 11.5 %all_to_all.11 = f32[32,1,128]{2,1,0:T(1,128)S(1)} all-to-all(f32[32,1,128]{2,1,0:T(1,128)S(1)} %bitcast.5), channel_id=1, replica_groups=mesh['lon'=8,'lat'=4] {'lon','lat'}, dimensions={0} | all-to-all | bytes 32768 | tf_op jit(solution)/shard_map/all_to_all | solution.py:693
  31.3 1.1 %finish.1 = (f32[12,3,16,128]{3,2,1,0:T(8,128)}, f32[12,12]{1,0:T(8,128)}) custom-call(f32[12,3,8,128]{3,2,1,0:T(8,128)S(1)} %get-tuple-element.33.fields_a, f32[12,3,8,128]{3,2,1,0:T(8,128)S(1)} %get-tuple-element.34.fields_b, f32[32,128]{1,0:T(8,128)S(1)} %bitcast.4), custom_call_target="tpu_custom_call" | custom-call | tf_op jit(solution)/shard_map/finish/pallas_call | solution.py:695
  (1 shorter events, 0.0 us)
Async XLA Ops:
  1.8 6.2 %collective-permute-start.1 = (f32[3,16,128]{2,1,0:T(8,128)S(1)}, f32[3,16,128]{2,1,0:T(8,128)S(1)}, u32[]{:S(2)}, u32[]{:S(2)}) collective-permute-start(f32[3,16,128]{2,1,0:T(8,128)S(1)} %get-tuple-element.25), channel_id=1, source_target_pairs={{0,28},{4,8},{8,4},{12,16},{16,12},{20,24},{24,20},{28,0},{1,29},{... | collective-permute-start | bytes 73736 | tf_op jit(solution)/shard_map/ppermute | solution.py:571
  6.3 1.6 %collective-permute-start.2 = (f32[3,16,128]{2,1,0:T(8,128)S(1)}, f32[3,16,128]{2,1,0:T(8,128)S(1)}, u32[]{:S(2)}, u32[]{:S(2)}) collective-permute-start(f32[3,16,128]{2,1,0:T(8,128)S(1)} %get-tuple-element.26), channel_id=1, source_target_pairs={{0,4},{4,0},{8,12},{12,8},{16,20},{20,16},{24,28},{28,24},{1,5},{5... | collective-permute-start | bytes 73736 | tf_op jit(solution)/shard_map/ppermute | solution.py:571
  6.4 9.3 %collective-permute-start = (f32[15,3,8,128]{3,2,1,0:T(8,128)S(1)}, f32[15,3,8,128]{3,2,1,0:T(8,128)S(1)}, u32[]{:S(2)}, u32[]{:S(2)}) collective-permute-start(f32[15,3,8,128]{3,2,1,0:T(8,128)S(1)} %get-tuple-element.20), channel_id=1, source_target_pairs={{0,1},{1,0},{2,3},{3,2},{4,5},{5,4},{6,7},{7,6},{8,9},{9,8},{10,11... | collective-permute-start | bytes 552968 | tf_op jit(solution)/shard_map/ppermute | solution.py:571
  8.0 8.6 %collective-permute-start.3 = (f32[15,3,8,128]{3,2,1,0:T(8,128)S(1)}, f32[15,3,8,128]{3,2,1,0:T(8,128)S(1)}, u32[]{:S(2)}, u32[]{:S(2)}) collective-permute-start(f32[15,3,8,128]{3,2,1,0:T(8,128)S(1)} %get-tuple-element.27), channel_id=1, source_target_pairs={{1,2},{2,1},{5,6},{6,5},{9,10},{10,9},{13,14},{14,13},{17,18},{18,... | collective-permute-start | bytes 552968 | tf_op jit(solution)/shard_map/ppermute | solution.py:571
  8.7 9.4 %collective-permute-start.4 = (f32[2,3,8,128]{3,2,1,0:T(8,128)S(1)}, f32[2,3,8,128]{3,2,1,0:T(8,128)S(1)}, u32[]{:S(2)}, u32[]{:S(2)}) collective-permute-start(f32[2,3,8,128]{3,2,1,0:T(8,128)S(1)} %get-tuple-element.28), channel_id=1, source_target_pairs={{0,1},{1,0},{2,3},{3,2},{4,5},{5,4},{6,7},{7,6},{8,9},{9,8},{10,11... | collective-permute-start | bytes 73736 | tf_op jit(solution)/shard_map/ppermute | solution.py:571

commit v7 on v6

--- a/solution.py
+++ b/solution.py
@@ -193,10 +193,8 @@
     return filled + [jnp.where(outer, rotate(east_halo, MIX - HALO * full), mixed)]
 
 
-def base_strips(rows, west_halo, east_halo, members):
-    q, left = members // SLOTS, members % SLOTS
-    place = in_strip()
-    lanes = lane_ids()
+def base_own_strips(rows, members):
+    left = members % SLOTS
     west = east = mixed = None
     for s in range(SLOTS):
         moved = rotate(rows, STRIP * s + HALO)
@@ -205,6 +203,14 @@
         if s < 2 * left:
             over = moved if s < left else rotate(rows, STRIP * s + 2 * HALO)
             mixed = over if s == 0 else jnp.where(slot_range(s, 0), over, mixed)
+    return west, east, mixed
+
+
+def base_strips(own, west_halo, east_halo, members):
+    west, east, mixed = own
+    q, left = members // SLOTS, members % SLOTS
+    place = in_strip()
+    lanes = lane_ids()
     near = [rotate(halo, -HALO * q) for halo in (west_halo, east_halo)]
     far = [rotate(halo, -HALO * q - STRIP * left) for halo in (west_halo, east_halo)]
     low = lanes < left * STRIP
@@ -309,7 +315,7 @@
                 at = FRONT + (3 * g + v) * PYRAMID + TILE * t
                 first[at : at + TILE, :] = strip
                 hist[t, 0, 3 * g + v] = strip
-            for kind, strip in enumerate(base_strips(own[members, v, rows, :], *halos, members)):
+            for kind, strip in enumerate(base_strips(base_own_strips(own[members, v, rows, :], members), *halos, members)):
                 at = FRONT + (3 * kind + v) * PYRAMID + TILE * t
                 base[at : at + TILE, :] = strip
                 strip_base[kind, v, rows, :] = strip
@@ -368,12 +374,14 @@
         west, east = corner(v)
         if ready is None:
             own = own_strips(lambda m: halo(m, v), members)
+            own_base = base_own_strips(halo(members, v), members)
         else:
             own = [ready[v, g] for g in range(len(kinds))]
+            own_base = [ready[v, len(kinds) + kind] for kind in range(KINDS)]
         strips = fill_strips(own, west, east, members)
         for g, strip in enumerate(strips):
             first[members + g][side.wedge(v), :] = strip
-        for kind, strip in enumerate(base_strips(halo(members, v), west, east, members)):
+        for kind, strip in enumerate(base_strips(own_base, west, east, members)):
             side.put_base(base, 3 * kind + v, lambda t: strip_base[kind, v, TILE * t : TILE * t + TILE, :], strip)
     return [
         (coef, side.coefs(base, kind, facts, coef), [members + g for g in range(len(kinds)) if kinds[g] == kind])
@@ -465,7 +473,8 @@
 def first_centre_kernel(members, own, halo_a, facts, hist_c, centre, ready, base, coef, *wedges):
     rows = first_rows(halo_a)
     for v in range(3):
-        for g, strip in enumerate(own_strips(lambda m: rows(m, v), members)):
+        strips = own_strips(lambda m: rows(m, v), members) + list(base_own_strips(rows(members, v), members))
+        for g, strip in enumerate(strips):
             ready[v, g] = strip
     centre_side(Side(False), members, own, first_rows(halo_a), facts, hist_c, centre, base, coef, wedges)
 
@@ -661,7 +670,7 @@
     half = shape(members, 3, TILE, LANES)
     centre_first, ready = pl.pallas_call(
         functools.partial(first_centre_kernel, members),
-        out_shape=[half, shape(3, groups, TILE, LANES)],
+        out_shape=[half, shape(3, groups + KINDS, TILE, LANES)],
         in_specs=[VMEM] * 4,
         out_specs=[VMEM] * 2,
         scratch_shapes=scratch([1], members, 0),

time: 32.5 us -> 32.5 us (level)
  transfers between devices with their start and end apart: 5 -> 5, of which waited for: 2 -> 2; matrix products, arithmetic and copies ran while one was open for 0% -> 0% of each run, Pallas kernels for 13% -> 14%
where the time goes in v7:
time: 32.5 us; the launch traced here: 32.3 us
  blocking collectives  11.5 us (35%)
  starting transfers between devices  11.4 us (35%)
  Pallas kernels  8.3 us (26%)
  between operations  0.7 us (2%)
  waiting for transfers between devices  0.38 us (1%)
    all_to_all x1, blocking collectives, per_device(): got = lax.all_to_all(send_gram, ('lon', 'lat'), 0, 0, tiled=True)  11.5 us
    ppermute x5, starting transfers between devices, swap(): return lax.ppermute(block, axis, pairs)  11.4 us
    pallas_call x1, Pallas kernels, per_device(): pl.pallas_call(functools.partial(edges_of_sides_kernel, members), out_sha...  1.69 us
    pallas_call x1, Pallas kernels, per_device(): pl.pallas_call(functools.partial(load_kernel, members), out_shape=[shape(...  1.16 us
    pallas_call x1, Pallas kernels, per_device(): pl.pallas_call(functools.partial(centre_kernel, members, total_rows), out...  1.14 us
    pallas_call x1, Pallas kernels, per_device(): pl.pallas_call(functools.partial(edges_kernel, members), out_shape=[shape...  1.12 us
    pallas_call x1, Pallas kernels, per_device(): pl.pallas_call(functools.partial(first_centre_kernel, members), out_shape...  1.06 us
    pallas_call x1, Pallas kernels, per_device(): pl.pallas_call(functools.partial(last_centre_kernel, members), out_shape=...  1.06 us
  transfers between devices with their start and end apart: 5, of which 2 were waited for; matrix products, arithmetic and copies ran while one was open for 0% of the time, Pallas kernels for 14%

profile of v7, /device:TPU:0, one launch (start us, length us, event | category | flops | bytes accessed | tf_op | source)
XLA Modules:
  0.0 32.3 jit_solution(12036540261500645565)
XLA Ops:
  0.6 1.2 %load.1 = (f32[13,3,16,128]{3,2,1,0:T(8,128)S(1)}, f32[15,3,8,128]{3,2,1,0:T(8,128)S(1)}, f32[3,16,128]{2,1,0:T(8,128)S(1)}, f32[3,16,128]{2,1,0:T(8,128)S(1)}) custom-call(f32[12,3,16,128]{3,2,1,0:T(8,128)} %pert.1, f32[2,16,128]{2,1,0:T(8,128)} %wind.1, f32[16,128]{1,0:T(8,128)} %height.1), custom_call_target="tpu_custom_call" | custom-call | tf_op jit(solution)/shard_map/load/pallas_call | solution.py:598
  1.8 4.6 %collective-permute-start.1 = (f32[3,16,128]{2,1,0:T(8,128)S(1)}, f32[3,16,128]{2,1,0:T(8,128)S(1)}, u32[]{:S(2)}, u32[]{:S(2)}) collective-permute-start(f32[3,16,128]{2,1,0:T(8,128)S(1)} %get-tuple-element.25), channel_id=1, source_target_pairs={{0,28},{4,8},{8,4},{12,16},{16,12},{20,24},{24,20},{28,0},{1,29},{... | collective-permute-start | bytes 73736 | tf_op jit(solution)/shard_map/ppermute | solution.py:580
  6.3 0.0 collective-permute-start.2
  6.4 1.5 %collective-permute-start = (f32[15,3,8,128]{3,2,1,0:T(8,128)S(1)}, f32[15,3,8,128]{3,2,1,0:T(8,128)S(1)}, u32[]{:S(2)}, u32[]{:S(2)}) collective-permute-start(f32[15,3,8,128]{3,2,1,0:T(8,128)S(1)} %get-tuple-element.20), channel_id=1, source_target_pairs={{0,1},{1,0},{2,3},{3,2},{4,5},{5,4},{6,7},{7,6},{8,9},{9,8},{10,11... | collective-permute-start | bytes 552968 | tf_op jit(solution)/shard_map/ppermute | solution.py:580
  7.8 0.1 collective-permute-done.1.got_b
  8.0 0.0 collective-permute-done.2.got_a
  8.0 0.7 %collective-permute-start.3 = (f32[15,3,8,128]{3,2,1,0:T(8,128)S(1)}, f32[15,3,8,128]{3,2,1,0:T(8,128)S(1)}, u32[]{:S(2)}, u32[]{:S(2)}) collective-permute-start(f32[15,3,8,128]{3,2,1,0:T(8,128)S(1)} %get-tuple-element.27), channel_id=1, source_target_pairs={{1,2},{2,1},{5,6},{6,5},{9,10},{10,9},{13,14},{14,13},{17,18},{18,... | collective-permute-start | bytes 552968 | tf_op jit(solution)/shard_map/ppermute | solution.py:580
  8.7 4.7 %collective-permute-start.4 = (f32[2,3,8,128]{3,2,1,0:T(8,128)S(1)}, f32[2,3,8,128]{3,2,1,0:T(8,128)S(1)}, u32[]{:S(2)}, u32[]{:S(2)}) collective-permute-start(f32[2,3,8,128]{3,2,1,0:T(8,128)S(1)} %get-tuple-element.28), channel_id=1, source_target_pairs={{0,1},{1,0},{2,3},{3,2},{4,5},{5,4},{6,7},{7,6},{8,9},{9,8},{10,11... | collective-permute-start | bytes 73736 | tf_op jit(solution)/shard_map/ppermute | solution.py:580
  13.3 1.1 %centre.1 = (f32[2,40,128]{2,1,0:T(8,128)S(1)}, f32[2,8,36,8,128]{4,3,2,1,0:T(8,128)S(1)}) custom-call(f32[13,3,16,128]{3,2,1,0:T(8,128)S(1)} %get-tuple-element.19.own), custom_call_target="tpu_custom_call" | custom-call | bytes 72000000 | tf_op jit(solution)/shard_map/centre/pallas_call | solution.py:616
  14.5 1.1 %edges.1 = (f32[2,8,15,8,128]{4,3,2,1,0:T(8,128)S(1)}, f32[3,3,16,128]{3,2,1,0:T(8,128)S(1)}) custom-call(f32[13,3,16,128]{3,2,1,0:T(8,128)S(1)} %get-tuple-element.19.own, f32[3,16,128]{2,1,0:T(8,128)S(1)} %get-tuple-element.29.west, f32[3,16,128]{2,1,0:T(8,128)S(1)} %get-tuple-element.30.east, f32[2,40,128]{2,1,0:T(8,128)S(1)} %get-tuple-element.21.facts), custom_call_target="tpu_custom_call" | custom-call | bytes 36000 | tf_op jit(solution)/shard_map/edges/pallas_call | solution.py:649
  15.6 0.0 collective-permute-done.halo_a
  15.6 1.1 %first_centre.1 = (f32[12,3,8,128]{3,2,1,0:T(8,128)S(1)}, f32[3,8,8,128]{3,2,1,0:T(8,128)S(1)}) custom-call(f32[13,3,16,128]{3,2,1,0:T(8,128)S(1)} %get-tuple-element.19.own, f32[15,3,8,128]{3,2,1,0:T(8,128)S(1)} %collective-permute-done.halo_a, f32[2,40,128]{2,1,0:T(8,128)S(1)} %get-tuple-element.21.facts, f32[2,8,36,8,128]{4,3,2,1,0:T(8,128)S(1)} %get-tuple-element.22.hist_c), custom_call_target="tpu_custom_call" | custom-call | bytes 36000 | tf_op jit(solution)/shard_map/first_centre/pallas_call | solution.py:671
  16.7 0.0 collective-permute-done.3.halo_b
  16.7 1.1 %last_centre.1.centre_2 = f32[12,3,8,128]{3,2,1,0:T(8,128)S(1)} custom-call(f32[13,3,16,128]{3,2,1,0:T(8,128)S(1)} %get-tuple-element.19.own, f32[15,3,8,128]{3,2,1,0:T(8,128)S(1)} %collective-permute-done.halo_a, f32[15,3,8,128]{3,2,1,0:T(8,128)S(1)} %collective-permute-done.3.halo_b, f32[2,40,128]{2,1,0:T(8,128)S(1)} %get-tuple-element.21.facts, ...), custom_call_target="tpu_custom_call" | custom-call | bytes 36000 | tf_op jit(solution)/shard_map/last_centre/pallas_call | solution.py:681
  17.8 0.2 collective-permute-done.4.corners
  18.0 1.7 %edges_of_sides.1 = (f32[12,3,8,128]{3,2,1,0:T(8,128)S(1)}, f32[12,3,8,128]{3,2,1,0:T(8,128)S(1)}, f32[32,128]{1,0:T(8,128)S(1)}) custom-call(f32[12,3,8,128]{3,2,1,0:T(8,128)S(1)} %get-tuple-element.23.centre_1, f32[3,8,8,128]{3,2,1,0:T(8,128)S(1)} %get-tuple-element.24.ready, f32[12,3,8,128]{3,2,1,0:T(8,128)S(1)} %last_centre.1.centre_2, ...), custom_call_target="tpu_custom_call" | custom-call | bytes 36000 | tf_op jit(solution)/shard_map/edges_of_sides/pallas_call | solution.py:691
  19.7 11.5 %all_to_all.11 = f32[32,1,128]{2,1,0:T(1,128)S(1)} all-to-all(f32[32,1,128]{2,1,0:T(1,128)S(1)} %bitcast.5), channel_id=1, replica_groups=mesh['lon'=8,'lat'=4] {'lon','lat'}, dimensions={0} | all-to-all | bytes 32768 | tf_op jit(solution)/shard_map/all_to_all | solution.py:702
  31.3 1.0 %finish.1 = (f32[12,3,16,128]{3,2,1,0:T(8,128)}, f32[12,12]{1,0:T(8,128)}) custom-call(f32[12,3,8,128]{3,2,1,0:T(8,128)S(1)} %get-tuple-element.33.fields_a, f32[12,3,8,128]{3,2,1,0:T(8,128)S(1)} %get-tuple-element.34.fields_b, f32[32,128]{1,0:T(8,128)S(1)} %bitcast.4), custom_call_target="tpu_custom_call" | custom-call | tf_op jit(solution)/shard_map/finish/pallas_call | solution.py:704
  (1 shorter events, 0.0 us)
Async XLA Ops:
  1.8 6.2 %collective-permute-start.1 = (f32[3,16,128]{2,1,0:T(8,128)S(1)}, f32[3,16,128]{2,1,0:T(8,128)S(1)}, u32[]{:S(2)}, u32[]{:S(2)}) collective-permute-start(f32[3,16,128]{2,1,0:T(8,128)S(1)} %get-tuple-element.25), channel_id=1, source_target_pairs={{0,28},{4,8},{8,4},{12,16},{16,12},{20,24},{24,20},{28,0},{1,29},{... | collective-permute-start | bytes 73736 | tf_op jit(solution)/shard_map/ppermute | solution.py:580
  6.3 1.6 %collective-permute-start.2 = (f32[3,16,128]{2,1,0:T(8,128)S(1)}, f32[3,16,128]{2,1,0:T(8,128)S(1)}, u32[]{:S(2)}, u32[]{:S(2)}) collective-permute-start(f32[3,16,128]{2,1,0:T(8,128)S(1)} %get-tuple-element.26), channel_id=1, source_target_pairs={{0,4},{4,0},{8,12},{12,8},{16,20},{20,16},{24,28},{28,24},{1,5},{5... | collective-permute-start | bytes 73736 | tf_op jit(solution)/shard_map/ppermute | solution.py:580
  6.4 9.3 %collective-permute-start = (f32[15,3,8,128]{3,2,1,0:T(8,128)S(1)}, f32[15,3,8,128]{3,2,1,0:T(8,128)S(1)}, u32[]{:S(2)}, u32[]{:S(2)}) collective-permute-start(f32[15,3,8,128]{3,2,1,0:T(8,128)S(1)} %get-tuple-element.20), channel_id=1, source_target_pairs={{0,1},{1,0},{2,3},{3,2},{4,5},{5,4},{6,7},{7,6},{8,9},{9,8},{10,11... | collective-permute-start | bytes 552968 | tf_op jit(solution)/shard_map/ppermute | solution.py:580
  8.0 8.7 %collective-permute-start.3 = (f32[15,3,8,128]{3,2,1,0:T(8,128)S(1)}, f32[15,3,8,128]{3,2,1,0:T(8,128)S(1)}, u32[]{:S(2)}, u32[]{:S(2)}) collective-permute-start(f32[15,3,8,128]{3,2,1,0:T(8,128)S(1)} %get-tuple-element.27), channel_id=1, source_target_pairs={{1,2},{2,1},{5,6},{6,5},{9,10},{10,9},{13,14},{14,13},{17,18},{18,... | collective-permute-start | bytes 552968 | tf_op jit(solution)/shard_map/ppermute | solution.py:580
  8.7 9.4 %collective-permute-start.4 = (f32[2,3,8,128]{3,2,1,0:T(8,128)S(1)}, f32[2,3,8,128]{3,2,1,0:T(8,128)S(1)}, u32[]{:S(2)}, u32[]{:S(2)}) collective-permute-start(f32[2,3,8,128]{3,2,1,0:T(8,128)S(1)} %get-tuple-element.28), channel_id=1, source_target_pairs={{0,1},{1,0},{2,3},{3,2},{4,5},{5,4},{6,7},{7,6},{8,9},{9,8},{10,11... | collective-permute-start | bytes 73736 | tf_op jit(solution)/shard_map/ppermute | solution.py:580
